TPU v7x, 32 devices: a whole 2x2x4 slice. The times are simulated.
32 devices in a mesh: groups: 2 (over y), sector: 16 (over z, x, core).
Axes of the slice: x: 2, y: 2, z: 4, core: 2. Of those that a mesh axis runs over, the one named last changes fastest.
Arguments:
- wavefunction: bfloat16 [32768, 128], P(('groups', 'sector')), parts along dimension 0, may hold values from -90 to 90
- env_left: bfloat16 [256, 40, 128, 128], P(('groups', 'sector')), parts along dimension 0, may hold values from -3 to 3
- right_environment_terms: bfloat16 [80, 128, 128], P('groups'), parts along dimension 0, may hold values from -1 to 1
- source_tile_lookup: int32 [256, 10], P('groups'), parts along dimension 0, may hold values from 0 to 127, as said below
Outputs:
- image_three: float32 [32768, 128], P(('groups', 'sector')), parts along dimension 0
- projected: float32 [6, 3], P('groups'), parts along dimension 0
There are 2 independent parts, one for each index of `groups`. A program takes and returns all parts, laid end to end along the dimension named above; each array names one. Nothing has to cross between parts.
Inputs may be any that keep to these rules, and one draw needn't show every extreme that they name: `source_tile_lookup`: entry 0 of output tile i is i itself. Of the other 8 x (9) entries of one device's output tiles, none names a tile of that device, at most 10 name tiles held by any one other device, and exactly 10 for some device.
All inputs are finite; a program needn't handle non-finite values.
Results may differ from a plain program's by a relative error of at most 0.0076.
Values may be sent and summed in bfloat16 or wider, within the bound.
No kernel may reach another device: no remote copies, remote signals or barrier semaphores. Data moves between devices by JAX's collectives and lax.ppermute only.
A program may use at most 128 MiB of HBM per device.

v0:
```python
import jax
import jax.numpy as jnp
from jax import lax
from jax.sharding import PartitionSpec as P

epsilon = 1e-06


def per_device(wavefunction, env_left, right_environment_terms, source_tile_lookup):
    peer_count = lax.axis_size("sector")
    own_index = lax.axis_index("sector")
    tile_dev = env_left.shape[0]
    terms = env_left.shape[1]
    tile_rows = env_left.shape[2]
    columns = wavefunction.shape[1]
    shifts = source_tile_lookup.shape[1]
    group = terms // shifts
    records = tile_dev * shifts
    slot_capacity = max(1, 2 * records // peer_count)
    inverse_total = 1.0 / float(peer_count * wavefunction.shape[0] * columns)
    own_records = lax.dynamic_slice_in_dim(
        source_tile_lookup, own_index * tile_dev, tile_dev, 0
    ).reshape(records)
    left_group = env_left.reshape(tile_dev, shifts, group, tile_rows, tile_rows)
    right_sector_group = right_environment_terms.reshape(shifts, group, columns, columns)
    src_device = own_records // tile_dev
    is_self = src_device == own_index
    device_ids = jnp.arange(peer_count, dtype=jnp.int32)
    one_hot = (
        (src_device[:, None] == device_ids[None, :]) & jnp.logical_not(is_self)[:, None]
    ).astype(jnp.int32)
    rank_in_peer = jnp.sum(one_hot * jnp.cumsum(one_hot, axis=0), axis=1) - 1
    position = jnp.where(is_self, 0, src_device * slot_capacity + rank_in_peer)
    every_record = source_tile_lookup.reshape(peer_count, records)
    other_reader = (device_ids != own_index)[:, None]
    from_self = ((every_record // tile_dev == own_index) & other_reader).astype(jnp.int32)
    slot_order = jnp.cumsum(from_self, axis=1) - 1
    slot_ids = jnp.arange(slot_capacity, dtype=jnp.int32)
    chosen = from_self[:, :, None] * (slot_order[:, :, None] == slot_ids[None, None, :]).astype(
        jnp.int32
    )
    send_index = jnp.sum(chosen * (every_record % tile_dev)[:, :, None], axis=1).reshape(
        peer_count * slot_capacity
    )
    local_index = own_records % tile_dev

    def fetch(tile_stack):
        outgoing = tile_stack[send_index]
        incoming = lax.all_to_all(outgoing, "sector", split_axis=0, concat_axis=0, tiled=True)
        return jnp.where(is_self[:, None, None], tile_stack[local_index], incoming[position])

    def apply_operator(vector):
        tile_stack = vector.astype(jnp.bfloat16).reshape(tile_dev, tile_rows, columns)
        picked = fetch(tile_stack).reshape(tile_dev, shifts, tile_rows, columns)
        left_contracted_state = jnp.einsum(
            "iktab,ikbc->iktac", left_group, picked, preferred_element_type=jnp.float32
        ).astype(jnp.bfloat16)
        product = jnp.einsum(
            "lvjyq,vjqn->lyn",
            left_contracted_state,
            right_sector_group,
            preferred_element_type=jnp.float32,
        )
        return product.reshape(tile_dev * tile_rows, columns)

    def global_means(entry_values):
        return lax.psum(jnp.stack(entry_values), "sector") * inverse_total

    def orthogonal_step(basis_list, product):
        coefs = global_means([jnp.sum(vector_item * product) for vector_item in basis_list])
        remainder = product
        for index_item, vector_item in enumerate(basis_list):
            remainder = remainder - coefs[index_item] * vector_item
        norm_value = jnp.sqrt(global_means([jnp.sum(remainder * remainder)])[0] + epsilon)
        return (coefs, norm_value, remainder / norm_value)

    start = wavefunction.astype(jnp.float32)
    basis_one = start * lax.rsqrt(global_means([jnp.sum(start * start)])[0] + epsilon)
    first_krylov_image = apply_operator(basis_one)
    first_coefs, coef_ba, basis_two = orthogonal_step([basis_one], first_krylov_image)
    image_two = apply_operator(basis_two)
    second_coefs, coef_cb, basis_three = orthogonal_step([basis_one, basis_two], image_two)
    image_three = apply_operator(basis_three)
    third_coefs = global_means(
        [
            jnp.sum(basis_one * image_three),
            jnp.sum(basis_two * image_three),
            jnp.sum(basis_three * image_three),
        ]
    )
    zero_entry = jnp.zeros((), jnp.float32)
    projected = jnp.stack(
        [
            jnp.stack([first_coefs[0], second_coefs[0], third_coefs[0]]),
            jnp.stack([coef_ba, second_coefs[1], third_coefs[1]]),
            jnp.stack([zero_entry, coef_cb, third_coefs[2]]),
        ]
    )
    return (image_three, projected)


def solution(mesh):
    return jax.shard_map(
        per_device,
        mesh=mesh,
        in_specs=(
            P(("groups", "sector"), None),
            P(("groups", "sector"), None, None, None),
            P("groups", None, None),
            P("groups", None),
        ),
        out_specs=(P(("groups", "sector"), None), P("groups", None)),
        check_vma=False,
    )
```

profile of v0, /device:TPU:0, one launch (start us, length us, event | category | flops | bytes accessed | tf_op | source)
XLA Modules:
  0.0 698.5 jit_solution(8814537844812019135)
XLA Ops:
  0.6 1.8 fusion.24
  2.4 35.5 %psum.42 = f32[1]{0:T(128)} all-reduce(f32[1]{0:T(128)} %bitcast), channel_id=1, replica_groups=mesh['groups'=2,'sector'=16] {'sector'}, use_global_device_ids=true, to_apply=%region_1.2 | all-reduce | flops 1 | bytes 8 | tf_op jit(solution)/shard_map/psum | solution.py:67
  38.7 0.8 copy.44
  39.6 0.2 reduce_window_sum.22
  39.9 0.2 multiply_reduce_fusion.5
  40.3 1.0 fusion.17
  41.3 7.7 %gather_fusion.1 = bf16[160,128,128]{2,1,0:T(8,128)(2,1)} fusion(bf16[8,128,128]{2,1,0:T(8,128)(2,1)S(1)} %bitcast.88, s32[1024]{0:T(1024)S(1)} %pad_clamp_fusion.1), kind=kCustom, calls=%fused_computation.1 | custom fusion | bytes 10486400 | tf_op jit(solution)/shard_map/gather | solution.py:48
  49.0 4.6 all-to-all-start
  53.9 0.1 reduce_window_sum.23
  54.0 0.2 select_reduce_fusion
  54.2 2.5 gather_fusion
  56.8 92.7 %all-to-all-done = bf16[160,128,128]{2,1,0:T(8,128)(2,1)} async-done(((bf16[160,128,128]{2,1,0:T(8,128)(2,1)}), bf16[160,128,128]{2,1,0:T(8,128)(2,1)}, u32[]{:S(2)}, u32[]{:S(2)}) %all-to-all-start) | async-done | bytes 5242912 | tf_op jit(solution)/shard_map/all_to_all | solution.py:49
  149.5 5.0 gather_fusion.2
  154.4 9.6 %convert_bitcast_fusion.2 = bf16[8,128,4,128,10]{3,1,2,4,0:T(8,128)(2,1)} fusion(bf16[8,10,4,128,128]{4,3,2,1,0:T(8,128)(2,1)} %bitcast.94, bf16[8,10,128,128]{3,2,1,0:T(8,128)(2,1)} %bitcast.97, bf16[8,10,128,128]{3,2,1,0:T(8,128)(2,1)} %bitcast.101, pred[8,10]{1,0:T(8,128)(4,1)S(1)} %get-tuple-element.9), kind=kOutput, calls=%fused_computation.11 | convolution fusion | flops 1348730880 | bytes 26214480 | tf_op jit(solution)/shard_map/iktab,ikbc->iktac/dot_general | solution.py:55
  164.1 12.7 %copy.47 = bf16[8,128,4,128,10]{3,1,0,4,2:T(8,128)(2,1)} copy(bf16[8,128,4,128,10]{3,1,2,4,0:T(8,128)(2,1)} %convert_bitcast_fusion.2) | data formatting | bytes 20971520 | tf_op jit(solution)/shard_map/convert_element_type | solution.py:57
  176.8 6.2 fusion.18
  183.0 52.4 %psum.43 = f32[1]{0:T(128)} all-reduce(f32[1]{0:T(128)} %bitcast.18), channel_id=1, replica_groups=mesh['groups'=2,'sector'=16] {'sector'}, use_global_device_ids=true, to_apply=%region_7.8 | all-reduce | flops 1 | bytes 8 | tf_op jit(solution)/shard_map/psum | solution.py:67
  236.1 0.7 multiply_reduce_fusion.4
  236.8 30.3 %psum.44 = f32[1]{0:T(128)} all-reduce(f32[1]{0:T(128)} %bitcast.20), channel_id=1, replica_groups=mesh['groups'=2,'sector'=16] {'sector'}, use_global_device_ids=true, to_apply=%region_9.10 | all-reduce | flops 1 | bytes 8 | tf_op jit(solution)/shard_map/psum | solution.py:67
  267.8 0.1 fusion.37
  267.9 7.7 %gather_fusion.4 = bf16[160,128,128]{2,1,0:T(8,128)(2,1)} fusion(bf16[8,128,128]{2,1,0:T(8,128)(2,1)S(1)} %bitcast.90, s32[1024]{0:T(1024)S(1)} %pad_clamp_fusion.1), kind=kCustom, calls=%fused_computation.4 | custom fusion | bytes 10486400 | tf_op jit(solution)/shard_map/gather | solution.py:48
  275.6 4.6 all-to-all-start.1
  280.2 2.5 gather_fusion.3
  282.8 93.3 %all-to-all-done.1 = bf16[160,128,128]{2,1,0:T(8,128)(2,1)} async-done(((bf16[160,128,128]{2,1,0:T(8,128)(2,1)}), bf16[160,128,128]{2,1,0:T(8,128)(2,1)}, u32[]{:S(2)}, u32[]{:S(2)}) %all-to-all-start.1) | async-done | bytes 5242912 | tf_op jit(solution)/shard_map/all_to_all | solution.py:49
  376.1 5.0 gather_fusion.5
  381.1 9.6 %convert_bitcast_fusion.1 = bf16[8,128,4,128,10]{3,1,2,4,0:T(8,128)(2,1)} fusion(bf16[8,10,4,128,128]{4,3,2,1,0:T(8,128)(2,1)} %bitcast.95, bf16[8,10,128,128]{3,2,1,0:T(8,128)(2,1)} %bitcast.99, bf16[8,10,128,128]{3,2,1,0:T(8,128)(2,1)} %bitcast.102, pred[8,10]{1,0:T(8,128)(4,1)S(1)} %get-tuple-element.9), kind=kOutput, calls=%fused_computation.10 | convolution fusion | flops 1348730880 | bytes 26214480 | tf_op jit(solution)/shard_map/iktab,ikbc->iktac/dot_general | solution.py:55
  390.7 12.7 %copy.49 = bf16[8,128,4,128,10]{3,1,0,4,2:T(8,128)(2,1)} copy(bf16[8,128,4,128,10]{3,1,2,4,0:T(8,128)(2,1)} %convert_bitcast_fusion.1) | data formatting | bytes 20971520 | tf_op jit(solution)/shard_map/convert_element_type | solution.py:57
  403.4 6.2 fusion.20
  409.6 1.4 pad_maximum_fusion.1
  411.0 51.8 %psum.45 = f32[2]{0:T(128)S(1)} all-reduce(f32[2]{0:T(128)S(1)} %pad_maximum_fusion.1), channel_id=1, replica_groups=mesh['groups'=2,'sector'=16] {'sector'}, use_global_device_ids=true, to_apply=%region_12.13 | all-reduce | flops 2 | bytes 16 | tf_op jit(solution)/shard_map/psum | solution.py:67
  462.8 0.6 fusion.40
  463.4 2.0 multiply_reduce_fusion.2
  465.4 30.3 %psum.46 = f32[1]{0:T(128)} all-reduce(f32[1]{0:T(128)} %bitcast.36), channel_id=1, replica_groups=mesh['groups'=2,'sector'=16] {'sector'}, use_global_device_ids=true, to_apply=%region_14.15 | all-reduce | flops 1 | bytes 8 | tf_op jit(solution)/shard_map/psum | solution.py:67
  496.5 7.7 %gather_fusion.7 = bf16[160,128,128]{2,1,0:T(8,128)(2,1)} fusion(bf16[8,128,128]{2,1,0:T(8,128)(2,1)S(1)} %bitcast.92, s32[1024]{0:T(1024)S(1)} %pad_clamp_fusion.1), kind=kCustom, calls=%fused_computation.7 | custom fusion | bytes 10486400 | tf_op jit(solution)/shard_map/gather | solution.py:48
  504.2 4.6 all-to-all-start.2
  508.8 2.5 gather_fusion.6
  511.3 93.3 %all-to-all-done.2 = bf16[160,128,128]{2,1,0:T(8,128)(2,1)} async-done(((bf16[160,128,128]{2,1,0:T(8,128)(2,1)}), bf16[160,128,128]{2,1,0:T(8,128)(2,1)}, u32[]{:S(2)}, u32[]{:S(2)}) %all-to-all-start.2) | async-done | bytes 5242912 | tf_op jit(solution)/shard_map/all_to_all | solution.py:49
  604.7 5.1 gather_fusion.8
  609.7 9.7 %convert_bitcast_fusion = bf16[8,128,4,128,10]{3,1,2,4,0:T(8,128)(2,1)} fusion(bf16[8,10,4,128,128]{4,3,2,1,0:T(8,128)(2,1)} %bitcast.96, bf16[8,10,128,128]{3,2,1,0:T(8,128)(2,1)} %bitcast.98, bf16[8,10,128,128]{3,2,1,0:T(8,128)(2,1)} %bitcast.100, pred[8,10]{1,0:T(8,128)(4,1)S(1)} %get-tuple-element.9), kind=kOutput, calls=%fused_computation.9 | convolution fusion | flops 1348730880 | bytes 26214480 | tf_op jit(solution)/shard_map/iktab,ikbc->iktac/dot_general | solution.py:55
  619.4 12.8 %copy.51 = bf16[8,128,4,128,10]{3,1,0,4,2:T(8,128)(2,1)} copy(bf16[8,128,4,128,10]{3,1,2,4,0:T(8,128)(2,1)} %convert_bitcast_fusion) | data formatting | bytes 20971520 | tf_op jit(solution)/shard_map/convert_element_type | solution.py:57
  632.2 8.2 %fusion.23 = (f32[]{:T(128)}, f32[]{:T(128)}, f32[]{:T(128)}, f32[1024,128]{1,0:T(8,128)}) fusion(bf16[1024,128]{1,0:T(8,128)(2,1)S(1)} %copy-done.1, f32[]{:T(128)} %bitcast.1, f32[]{:T(128)} %bitcast.21, f32[1024,128]{1,0:T(8,128)S(1)} %get-tuple-element.21, f32[]{:T(128)} %bitcast.19, f32[1024,128]{1,0:T(8,128)S(1)} %get-tuple-element.8, f32[]{:T(128)} %bitcast.37, ...), kind=kOutput, calls=%fused_computation.40 | convolution fusion | flops 1343750144 | bytes 13631516 | tf_op jit(solution)/shard_map/lvjyq,vjqn->lyn/dot_general | solution.py:58
  640.4 1.8 pad_maximum_fusion.2
  642.2 51.8 %psum.47 = f32[3]{0:T(128)S(1)} all-reduce(f32[3]{0:T(128)S(1)} %pad_maximum_fusion.2), channel_id=1, replica_groups=mesh['groups'=2,'sector'=16] {'sector'}, use_global_device_ids=true, to_apply=%region_18.19 | all-reduce | flops 3 | bytes 24 | tf_op jit(solution)/shard_map/psum | solution.py:67
  694.0 0.6 fusion.39
  694.6 1.3 maximum_bitcast_fusion
  695.9 1.3 maximum_bitcast_fusion.1
  697.2 0.7 maximum_bitcast_fusion.2
  697.9 0.6 pad_maximum_fusion
  (23 shorter events, 0.8 us)
Async XLA Ops:
  0.6 176.2 %copy-start = (bf16[40,128,128]{2,1,0:T(8,128)(2,1)S(1)}, bf16[40,128,128]{2,1,0:T(8,128)(2,1)}, u32[]{:S(2)}) copy-start(bf16[40,128,128]{2,1,0:T(8,128)(2,1)} %param.6) | copy-start | bytes 3932164
  49.0 100.5 %all-to-all-start = ((bf16[160,128,128]{2,1,0:T(8,128)(2,1)}), bf16[160,128,128]{2,1,0:T(8,128)(2,1)}, u32[]{:S(2)}, u32[]{:S(2)}) async-start(bf16[160,128,128]{2,1,0:T(8,128)(2,1)} %gather_fusion.1), calls=%async_computation | async-start | bytes 10485760 | tf_op jit(solution)/shard_map/all_to_all | solution.py:49
  164.1 12.7 %copy-start.1 = (bf16[1024,128]{1,0:T(8,128)(2,1)S(1)}, bf16[1024,128]{1,0:T(8,128)(2,1)}, u32[]{:S(2)}) copy-start(bf16[1024,128]{1,0:T(8,128)(2,1)} %param.4) | copy-start | bytes 786436
  275.6 100.5 %all-to-all-start.1 = ((bf16[160,128,128]{2,1,0:T(8,128)(2,1)}), bf16[160,128,128]{2,1,0:T(8,128)(2,1)}, u32[]{:S(2)}, u32[]{:S(2)}) async-start(bf16[160,128,128]{2,1,0:T(8,128)(2,1)} %gather_fusion.4), calls=%async_computation.1 | async-start | bytes 10485760 | tf_op jit(solution)/shard_map/all_to_all | solution.py:49
  504.2 100.5 %all-to-all-start.2 = ((bf16[160,128,128]{2,1,0:T(8,128)(2,1)}), bf16[160,128,128]{2,1,0:T(8,128)(2,1)}, u32[]{:S(2)}, u32[]{:S(2)}) async-start(bf16[160,128,128]{2,1,0:T(8,128)(2,1)} %gather_fusion.7), calls=%async_computation.2 | async-start | bytes 10485760 | tf_op jit(solution)/shard_map/all_to_all | solution.py:49
where the time goes:
time: 699 us; the launch traced here: 698 us
  waiting for transfers between devices  279 us (40%)
  blocking collectives  252 us (36%)
  local copies, waits for them, and re-layouts  86.3 us (12%)
  matrix products  49.6 us (7%)
  other arithmetic  13.8 us (2%)
  starting transfers between devices  13.8 us (2%)
    all_to_all x3, waiting for transfers between devices, fetch(): lax.all_to_all(outgoing, 'sector', split_axis=0, concat_axis=0, tiled=True)  279 us
    psum x6, blocking collectives, global_means(): return lax.psum(jnp.stack(entry_values), 'sector') * inverse_total  252 us
    convert_element_type x3, local copies, waits for them, and re-layouts, apply_operator(): left_contracted_state = jnp.einsum('iktab,ikbc->iktac', left_group, picke...  38.2 us
    dot_general x3, matrix products, apply_operator(): jnp.einsum('iktab,ikbc->iktac', left_group, picked, preferred_element_typ...  28.9 us
    gather x3, local copies, waits for them, and re-layouts, fetch(): outgoing = tile_stack[send_index]  23 us
    dot_general x3, matrix products, apply_operator(): jnp.einsum('lvjyq,vjqn->lyn', left_contracted_state, right_sector_group,...  20.7 us
    gather x3, local copies, waits for them, and re-layouts, fetch(): incoming[position]  15 us
  transfers between devices with their start and end apart: 3, of which 3 were waited for; matrix products, arithmetic and copies ran while one was open for 1% of the time, Pallas kernels for 0%

commit v1 on v0

v1 whole, which is shorter than its diff:
```python
import functools

import jax
import jax.numpy as jnp
from jax import lax
from jax.experimental import pallas as pl
from jax.experimental.pallas import tpu as pltpu
from jax.sharding import PartitionSpec as P

epsilon = 1e-06
f32 = jnp.float32
bf16 = jnp.bfloat16
STAT_ROWS = 16


def row(value):
    return jnp.broadcast_to(value, (1, 128))


def lane_sums(product):
    return jnp.sum(product, axis=0, keepdims=True)


def split_rows(sums):
    rows = []
    for value in sums:
        high = value.astype(bf16)
        rest = value - high.astype(f32)
        middle = rest.astype(bf16)
        low = (rest - middle.astype(f32)).astype(bf16)
        rows += [high, middle, low]
    rows += [jnp.zeros((1, 128), bf16)] * (STAT_ROWS - len(rows))
    return jnp.concatenate([r.astype(f32) for r in rows], axis=0).astype(bf16)


def start_kernel(w_ref, piece_ref):
    rows = w_ref.shape[0]
    w = w_ref[...]
    piece_ref[0:rows, :] = w
    wide = w.astype(f32)
    piece_ref[rows:, :] = split_rows([lane_sums(wide * wide)])


def load_kernel(env_ref, right_ref, env_out, right_out, sems):
    parts = 8
    step = env_ref.shape[0] // parts
    copies = [
        pltpu.make_async_copy(
            env_ref.at[pl.ds(j * step, step)], env_out.at[pl.ds(j * step, step)], sems.at[j]
        )
        for j in range(parts)
    ]
    copies.append(pltpu.make_async_copy(right_ref, right_out, sems.at[parts]))
    for copy in copies:
        copy.start()
    for copy in copies:
        copy.wait()


def apply_kernel(stage, sizes, tile_ref, stat_ref, buf_ref, env_ref, right_ref, w_ref, *rest):
    tile_dev, shifts, group, tile_rows, total = sizes
    prior = rest[: stage - 1]
    rest = rest[stage - 1 :]
    if stage > 1:
        coef_in, rest = rest[0], rest[1:]
    image_ref, coef_ref, send_ref, left_ref = rest
    width = group * tile_rows

    def one_tile(i, carry):
        for k in range(shifts):
            offset = pl.multiple_of(tile_ref[i * shifts + k], 16)
            picked = buf_ref[pl.ds(offset, tile_rows), :]
            start = pl.multiple_of((i * shifts + k) * width, width)
            product = jnp.dot(
                env_ref[pl.ds(start, width), :], picked, preferred_element_type=f32
            ).astype(bf16)
            for t in range(group):
                left_ref[
                    pl.ds(pl.multiple_of(i * tile_rows, tile_rows), tile_rows),
                    (k * group + t) * 128 : (k * group + t + 1) * 128,
                ] = product[t * tile_rows : (t + 1) * tile_rows]
        return carry

    lax.fori_loop(0, tile_dev, one_tile, 0)
    applied = jnp.dot(left_ref[...], right_ref[...], preferred_element_type=f32)

    gathered = jnp.zeros((STAT_ROWS, 128), f32)
    for d in range(stat_ref.shape[0]):
        offset = pl.multiple_of(stat_ref[d], 16)
        gathered = gathered + buf_ref[pl.ds(offset, STAT_ROWS), :].astype(f32)

    def mean_of(j):
        lanes = gathered[3 * j : 3 * j + 1] + gathered[3 * j + 1 : 3 * j + 2]
        lanes = lanes + gathered[3 * j + 2 : 3 * j + 3]
        return row(jnp.sum(lanes, axis=1, keepdims=True) * (1.0 / total))

    w = w_ref[...].astype(f32)
    if stage == 1:
        square = mean_of(0)
        scale = lax.rsqrt(square + epsilon)
        coefs = [scale, scale * scale * square]
        image = scale * applied
        sums = [lane_sums((w * scale) * image), lane_sums(image * image)]
    elif stage == 2:
        scale, g11 = coef_in[0:1, :], coef_in[1:2, :]
        aa, norm = mean_of(0), mean_of(1)
        rest_square = jnp.maximum(norm - 2.0 * aa * aa + aa * aa * g11, 0.0)
        ba = jnp.sqrt(rest_square + epsilon)
        g12 = (aa - aa * g11) / ba
        g22 = rest_square / (ba * ba)
        coefs = [scale, g11, aa, ba, g12, g22]
        first = prior[0][...]
        basis_one = w * scale
        basis_two = (first - aa * basis_one) / ba
        image = (applied - aa * first) / ba
        sums = [
            lane_sums(basis_one * image),
            lane_sums(basis_two * image),
            lane_sums(image * image),
        ]
    else:
        scale, g11, aa, ba, g12, g22 = [coef_in[j : j + 1, :] for j in range(6)]
        ab, bb, norm = mean_of(0), mean_of(1), mean_of(2)
        rest_square = norm - 2.0 * (ab * ab + bb * bb) + ab * ab * g11 + bb * bb * g22
        rest_square = jnp.maximum(rest_square + 2.0 * ab * bb * g12, 0.0)
        cb = jnp.sqrt(rest_square + epsilon)
        coefs = [aa, ab, ba, bb, cb]
        first, second = prior[0][...], prior[1][...]
        basis_one = w * scale
        basis_two = (first - aa * basis_one) / ba
        basis_three = (second - ab * basis_one - bb * basis_two) / cb
        image = (applied - ab * first - bb * second) / cb
        sums = [lane_sums(b * image) for b in (basis_one, basis_two, basis_three)]

    image_ref[...] = image
    coef_ref[...] = jnp.concatenate(coefs + [jnp.zeros((1, 128), f32)] * (8 - len(coefs)), axis=0)
    if stage < 3:
        rows = image.shape[0]
        send_ref[0:rows, :] = image.astype(bf16)
        send_ref[rows:, :] = split_rows(sums)
    else:
        send_ref[...] = jnp.concatenate(sums + [jnp.zeros((1, 128), f32)] * 5, axis=0)


def finish_kernel(total, stat_ref, coef_ref, out_ref):
    last = [row(jnp.sum(stat_ref[j : j + 1, :], axis=1, keepdims=True) * (1.0 / total)) for j in range(3)]
    aa, ab, ba, bb, cb = [coef_ref[j : j + 1, :] for j in range(5)]
    lane = lax.broadcasted_iota(jnp.int32, (1, 128), 1)

    def line(a, b, c):
        return jnp.where(lane == 0, a, jnp.where(lane == 1, b, c))

    zero = jnp.zeros((1, 128), f32)
    table = jnp.concatenate(
        [line(aa, ab, last[0]), line(ba, bb, last[1]), line(zero, cb, last[2])], axis=0
    )
    out_ref[...] = table[:, 0:3]


def ring_pairs(peers):
    chips = peers // 2
    order = list(range(0, chips, 2)) + list(range(chips - 1, 0, -2))
    forward = [
        (order[j] * 2 + c, order[(j + 1) % chips] * 2 + c) for j in range(chips) for c in range(2)
    ]
    return forward, [(b, a) for a, b in forward]


def ring_place(chip, chips):
    return jnp.where(chip % 2 == 0, chip // 2, chips - 1 - chip // 2)


def per_device(wavefunction, env_left, right_environment_terms, source_tile_lookup):
    peers = lax.axis_size("sector")
    own = lax.axis_index("sector")
    tile_dev, terms, tile_rows = env_left.shape[0], env_left.shape[1], env_left.shape[2]
    rows, columns = wavefunction.shape
    shifts = source_tile_lookup.shape[1]
    records = tile_dev * shifts
    total = peers * rows * columns
    sizes = (tile_dev, shifts, terms // shifts, tile_rows, total)
    piece_rows = rows + STAT_ROWS
    lookup = source_tile_lookup
    own_records = lax.dynamic_slice_in_dim(lookup, own * tile_dev, tile_dev, 0).reshape(records)
    source = own_records // tile_dev
    local = own_records % tile_dev
    devices = jnp.arange(peers, dtype=jnp.int32)
    use_ring = peers * tile_dev <= 2 * records

    if use_ring:
        chips = peers // 2
        forward, backward = ring_pairs(peers)
        sibling = [(i, i ^ 1) for i in range(peers)]
        here = ring_place(own // 2, chips)

        def slot_of(device):
            steps = (ring_place(device // 2, chips) - here) % chips
            return steps * 2 + (device % 2 + own % 2) % 2

        tile_offset = slot_of(source) * piece_rows + local * tile_rows
        stat_offset = slot_of(devices) * piece_rows + rows

        def exchange(piece):
            pieces = {0: piece}
            ahead = behind = piece
            for step in range(1, chips // 2 + 1):
                ahead = lax.ppermute(ahead, "sector", forward)
                pieces[chips - step] = ahead
                if 2 * step < chips:
                    behind = lax.ppermute(behind, "sector", backward)
                    pieces[step] = behind
            parts = []
            for j in range(chips):
                parts += [pieces[j], lax.ppermute(pieces[j], "sector", sibling)]
            return jnp.concatenate(parts, axis=0)

    else:
        capacity = max(1, 2 * records // peers)
        is_self = source == own
        hot = ((source[:, None] == devices[None, :]) & ~is_self[:, None]).astype(jnp.int32)
        rank = jnp.sum(hot * jnp.cumsum(hot, axis=0), axis=1) - 1
        every = lookup.reshape(peers, records)
        wanted = ((every // tile_dev == own) & (devices != own)[:, None]).astype(jnp.int32)
        order = jnp.cumsum(wanted, axis=1) - 1
        slots = jnp.arange(capacity, dtype=jnp.int32)
        chosen = wanted[:, :, None] * (order[:, :, None] == slots).astype(jnp.int32)
        send_index = jnp.sum(chosen * (every % tile_dev)[:, :, None], axis=1).reshape(-1)
        place = jnp.where(is_self, local, tile_dev + source * capacity + rank)
        tile_offset = place * tile_rows
        stat_base = (tile_dev + peers * capacity) * tile_rows
        stat_offset = stat_base + devices * STAT_ROWS

        def exchange(piece):
            tiles = piece[:rows].reshape(tile_dev, tile_rows, columns)
            incoming = lax.all_to_all(tiles[send_index], "sector", 0, 0, tiled=True)
            stats = lax.all_gather(piece[rows:], "sector", axis=0, tiled=True)
            return jnp.concatenate([piece[:rows], incoming.reshape(-1, columns), stats], axis=0)

    vmem = pl.BlockSpec(memory_space=pltpu.VMEM)
    smem = pl.BlockSpec(memory_space=pltpu.SMEM)
    hbm = pl.BlockSpec(memory_space=pl.ANY)

    piece = pl.pallas_call(
        start_kernel,
        out_shape=jax.ShapeDtypeStruct((piece_rows, columns), bf16),
        in_specs=[vmem],
        out_specs=vmem,
        compiler_params=pltpu.CompilerParams(vmem_limit_bytes=4 * 2**20),
    )(wavefunction)
    env_flat = env_left.reshape(tile_dev * terms * tile_rows, tile_rows)
    right_flat = right_environment_terms.reshape(terms * columns, columns)
    env_near, right_near = pl.pallas_call(
        load_kernel,
        out_shape=(pltpu.VMEM(env_flat.shape, bf16), pltpu.VMEM(right_flat.shape, bf16)),
        in_specs=[hbm, hbm],
        out_specs=(vmem, vmem),
        scratch_shapes=[pltpu.SemaphoreType.DMA((9,))],
        compiler_params=pltpu.CompilerParams(vmem_limit_bytes=2 * 2**20),
    )(env_flat, right_flat)

    def apply_operator(stage, buffer, prior, coefs):
        image = jax.ShapeDtypeStruct((rows, columns), f32)
        small = jax.ShapeDtypeStruct((8, 128), f32)
        send = small if stage == 3 else jax.ShapeDtypeStruct((piece_rows, columns), bf16)
        operands = [buffer, env_near, right_near, wavefunction, *prior, *coefs]
        return pl.pallas_call(
            functools.partial(apply_kernel, stage, sizes),
            out_shape=(image, small, send),
            in_specs=[smem, smem] + [vmem] * len(operands),
            out_specs=(vmem, vmem, vmem),
            scratch_shapes=[pltpu.VMEM((rows, terms * columns), bf16)],
            compiler_params=pltpu.CompilerParams(vmem_limit_bytes=20 * 2**20),
            cost_estimate=pl.CostEstimate(
                flops=4 * rows * terms * tile_rows * columns, bytes_accessed=2**24, transcendentals=0
            ),
        )(tile_offset, stat_offset, *operands)

    image_one, coefs_one, piece = apply_operator(1, exchange(piece), [], [])
    image_two, coefs_two, piece = apply_operator(2, exchange(piece), [image_one], [coefs_one])
    image_three, coefs_three, stats = apply_operator(
        3, exchange(piece), [image_one, image_two], [coefs_two]
    )
    distance = 1
    while distance < peers:
        pairs = [(i, i ^ distance) for i in range(peers)]
        stats = stats + lax.ppermute(stats, "sector", pairs)
        distance *= 2
    projected = pl.pallas_call(
        functools.partial(finish_kernel, total),
        out_shape=jax.ShapeDtypeStruct((3, 3), f32),
        in_specs=[vmem, vmem],
        out_specs=vmem,
        compiler_params=pltpu.CompilerParams(vmem_limit_bytes=2 * 2**20),
    )(stats, coefs_three)
    return (image_three, projected)


def solution(mesh):
    return jax.shard_map(
        per_device,
        mesh=mesh,
        in_specs=(
            P(("groups", "sector"), None),
            P(("groups", "sector"), None, None, None),
            P("groups", None, None),
            P("groups", None),
        ),
        out_specs=(P(("groups", "sector"), None), P("groups", None)),
        check_vma=False,
    )
```

time: 699 us -> 151 us (0.22)
  blocking collectives: 252 us -> 0 us
  waiting for transfers between devices: 279 us -> 92.1 us
  local copies, waits for them, and re-layouts: 86.3 us -> 8.2 us
  matrix products: 49.6 us -> 0 us
  Pallas kernels: 0 us -> 24.8 us
  other arithmetic: 13.8 us -> 0.08 us
  starting transfers between devices: 13.8 us -> 24.9 us
    all_to_all x3 -> x0, waiting for transfers between devices: 279 us -> none  [fetch(): lax.all_to_all(outgoing, 'sector', split_axis=0, concat_axis=0, tiled=True)]
    psum x6 -> x0, blocking collectives: 252 us -> none  [global_means(): return lax.psum(jnp.stack(entry_values), 'sector') * inverse_total]
    ppermute x0 -> x49, waiting for transfers between devices: none -> 92.1 us  [the longest x12 44.1 us: exchange(): ahead = lax.ppermute(ahead, 'sector', forward)]
    dot_general x6 -> x0, matrix products: 49.6 us -> none  [the longest x3 28.9 us: apply_operator(): jnp.einsum('iktab,ikbc->iktac', left_group, picked, preferred_element_typ...]
    gather x9 -> x0, local copies, waits for them, and re-layouts: 45.7 us -> none  [the longest x3 23 us: fetch(): outgoing = tile_stack[send_index]]
    convert_element_type x3 -> x0, local copies, waits for them, and re-layouts: 38.2 us -> none  [apply_operator(): left_contracted_state = jnp.einsum('iktab,ikbc->iktac', left_group, picke...]
    ppermute x0 -> x49, starting transfers between devices: none -> 24.9 us  [the longest x9 15.5 us: exchange(): behind = lax.ppermute(behind, 'sector', backward)]
    pallas_call x0 -> x6, Pallas kernels: none -> 24.8 us  [the longest x3 23.1 us: apply_operator(): pl.pallas_call(functools.partial(apply_kernel, stage, sizes), out_shape=(...]
  transfers between devices with their start and end apart: 3 -> 49, of which waited for: 3 -> 19; matrix products, arithmetic and copies ran while one was open for 1% -> 1% of each run, Pallas kernels for 0% -> 1%
where the time goes in v1:
time: 151 us
  waiting for transfers between devices  92.1 us (61%)
  starting transfers between devices  24.9 us (16%)
  Pallas kernels  24.8 us (16%)
  local copies, waits for them, and re-layouts  8.2 us (5%)
    ppermute x12, waiting for transfers between devices, exchange(): ahead = lax.ppermute(ahead, 'sector', forward)  44.1 us
    ppermute x9, waiting for transfers between devices, exchange(): behind = lax.ppermute(behind, 'sector', backward)  33.2 us
    pallas_call x3, Pallas kernels, apply_operator(): pl.pallas_call(functools.partial(apply_kernel, stage, sizes), out_shape=(...  23.1 us
    ppermute x9, starting transfers between devices, exchange(): behind = lax.ppermute(behind, 'sector', backward)  15.5 us
    ppermute x4, waiting for transfers between devices, per_device(): stats = stats + lax.ppermute(stats, 'sector', pairs)  10.4 us
    unnamed x55, local copies, waits for them, and re-layouts  7.85 us
    ppermute x12, starting transfers between devices, exchange(): ahead = lax.ppermute(ahead, 'sector', forward)  4.85 us
    ppermute x24, waiting for transfers between devices, exchange(): parts += [pieces[j], lax.ppermute(pieces[j], 'sector', sibling)]  4.41 us
  transfers between devices with their start and end apart: 49, of which 19 were waited for; matrix products, arithmetic and copies ran while one was open for 1% of the time, Pallas kernels for 1%

profile of v1, /device:TPU:0, one launch (start us, length us, event | category | flops | bytes accessed | tf_op | source)
XLA Modules:
  0.0 151.2 jit_solution(8060443120211299042)
XLA Ops:
  0.7 0.9 copy-done.2
  1.8 0.5 collective-permute-start
  2.3 2.6 %collective-permute-start.1 = (bf16[1040,128]{1,0:T(8,128)(2,1)S(1)}, bf16[1040,128]{1,0:T(8,128)(2,1)S(1)}, u32[]{:S(2)}, u32[]{:S(2)}) collective-permute-start(bf16[1040,128]{1,0:T(8,128)(2,1)S(1)} %shard_map.59), channel_id=1, source_target_pairs={{4,0},{5,1},{8,4},{9,5},{12,8},{13,9},{14,12},{15,13},{10,14},{11,... | collective-permute-start | bytes 798728 | tf_op jit(solution)/shard_map/ppermute | solution.py:210
  5.3 4.0 %copy-done.1 = bf16[8,40,128,128]{3,2,1,0:T(8,128)(2,1)S(1)} copy-done((bf16[8,40,128,128]{3,2,1,0:T(8,128)(2,1)S(1)}, bf16[8,40,128,128]{3,2,1,0:T(8,128)(2,1)}, u32[]{:S(2)}) %copy-start.1) | copy-done | bytes 10485784
  9.3 1.3 copy-done.4
  10.6 0.9 shard_map.60
  11.9 1.7 %collective-permute-start.3 = (bf16[1040,128]{1,0:T(8,128)(2,1)S(1)}, bf16[1040,128]{1,0:T(8,128)(2,1)S(1)}, u32[]{:S(2)}, u32[]{:S(2)}) collective-permute-start(bf16[1040,128]{1,0:T(8,128)(2,1)S(1)} %collective-permute-done.1), channel_id=1, source_target_pairs={{4,0},{5,1},{8,4},{9,5},{12,8},{13,9},{14,12},{15,13},{10,14},{11,... | collective-permute-start | bytes 798728 | tf_op jit(solution)/shard_map/ppermute | solution.py:210
  14.1 6.7 %collective-permute-done.3 = bf16[1040,128]{1,0:T(8,128)(2,1)S(1)} collective-permute-done((bf16[1040,128]{1,0:T(8,128)(2,1)S(1)}, bf16[1040,128]{1,0:T(8,128)(2,1)S(1)}, u32[]{:S(2)}, u32[]{:S(2)}) %collective-permute-start.3) | collective-permute-done | bytes 266272 | tf_op jit(solution)/shard_map/ppermute | solution.py:210
  20.7 1.7 %collective-permute-start.5 = (bf16[1040,128]{1,0:T(8,128)(2,1)S(1)}, bf16[1040,128]{1,0:T(8,128)(2,1)S(1)}, u32[]{:S(2)}, u32[]{:S(2)}) collective-permute-start(bf16[1040,128]{1,0:T(8,128)(2,1)S(1)} %collective-permute-done.3), channel_id=1, source_target_pairs={{4,0},{5,1},{8,4},{9,5},{12,8},{13,9},{14,12},{15,13},{10,14},{11,... | collective-permute-start | bytes 798728 | tf_op jit(solution)/shard_map/ppermute | solution.py:210
  22.9 8.1 %collective-permute-done.9 = bf16[1040,128]{1,0:T(8,128)(2,1)S(1)} collective-permute-done((bf16[1040,128]{1,0:T(8,128)(2,1)S(1)}, bf16[1040,128]{1,0:T(8,128)(2,1)S(1)}, u32[]{:S(2)}, u32[]{:S(2)}) %collective-permute-start.9) | collective-permute-done | bytes 266272 | tf_op jit(solution)/shard_map/ppermute | solution.py:207
  31.3 0.5 collective-permute-start.6
  31.9 6.7 %collective-permute-done.10 = bf16[1040,128]{1,0:T(8,128)(2,1)S(1)} collective-permute-done((bf16[1040,128]{1,0:T(8,128)(2,1)S(1)}, bf16[1040,128]{1,0:T(8,128)(2,1)S(1)}, u32[]{:S(2)}, u32[]{:S(2)}) %collective-permute-start.10) | collective-permute-done | bytes 266272 | tf_op jit(solution)/shard_map/ppermute | solution.py:207
  38.7 1.4 collective-permute-done.11
  40.5 7.4 %shard_map.61 = (f32[1024,128]{1,0:T(8,128)S(1)}, f32[8,128]{1,0:T(8,128)S(1)}, bf16[1040,128]{1,0:T(8,128)(2,1)S(1)}) custom-call(s32[80]{0:T(128)S(1)} %fusion.6.tile_ref, s32[16]{0:T(128)S(1)} %fusion.13.stat_ref, bf16[16640,128]{1,0:T(8,128)(2,1)S(1)} %constant_dynamic-update-slice_fusion.buf_ref, bf16[40960,128]{1,0:T(8,128)(2,1)S(1)} %get-tuple-element.13.env_ref, ...), custom_call_target="tpu_custom_call" | custom-call | flops 2684354560 | bytes 16777216 | tf_op jit(solution)/shard_map/pallas_call | solution.py:266
  47.9 1.6 %collective-permute-start.16 = (bf16[1040,128]{1,0:T(8,128)(2,1)S(1)}, bf16[1040,128]{1,0:T(8,128)(2,1)S(1)}, u32[]{:S(2)}, u32[]{:S(2)}) collective-permute-start(bf16[1040,128]{1,0:T(8,128)(2,1)S(1)} %get-tuple-element.15), channel_id=1, source_target_pairs={{4,0},{5,1},{8,4},{9,5},{12,8},{13,9},{14,12},{15,13},{10,14},{11,... | collective-permute-start | bytes 798728 | tf_op jit(solution)/shard_map/ppermute | solution.py:210
  49.6 0.4 collective-permute-start.22
  50.0 6.4 %collective-permute-done.16 = bf16[1040,128]{1,0:T(8,128)(2,1)S(1)} collective-permute-done((bf16[1040,128]{1,0:T(8,128)(2,1)S(1)}, bf16[1040,128]{1,0:T(8,128)(2,1)S(1)}, u32[]{:S(2)}, u32[]{:S(2)}) %collective-permute-start.16) | collective-permute-done | bytes 266272 | tf_op jit(solution)/shard_map/ppermute | solution.py:210
  56.4 1.6 %collective-permute-start.18 = (bf16[1040,128]{1,0:T(8,128)(2,1)S(1)}, bf16[1040,128]{1,0:T(8,128)(2,1)S(1)}, u32[]{:S(2)}, u32[]{:S(2)}) collective-permute-start(bf16[1040,128]{1,0:T(8,128)(2,1)S(1)} %collective-permute-done.16), channel_id=1, source_target_pairs={{4,0},{5,1},{8,4},{9,5},{12,8},{13,9},{14,12},{15,13},{10,14},{11,... | collective-permute-start | bytes 798728 | tf_op jit(solution)/shard_map/ppermute | solution.py:210
  58.0 0.5 collective-permute-start.23
  58.5 6.7 %collective-permute-done.18 = bf16[1040,128]{1,0:T(8,128)(2,1)S(1)} collective-permute-done((bf16[1040,128]{1,0:T(8,128)(2,1)S(1)}, bf16[1040,128]{1,0:T(8,128)(2,1)S(1)}, u32[]{:S(2)}, u32[]{:S(2)}) %collective-permute-start.18) | collective-permute-done | bytes 266272 | tf_op jit(solution)/shard_map/ppermute | solution.py:210
  65.2 1.6 %collective-permute-start.20 = (bf16[1040,128]{1,0:T(8,128)(2,1)S(1)}, bf16[1040,128]{1,0:T(8,128)(2,1)S(1)}, u32[]{:S(2)}, u32[]{:S(2)}) collective-permute-start(bf16[1040,128]{1,0:T(8,128)(2,1)S(1)} %collective-permute-done.18), channel_id=1, source_target_pairs={{4,0},{5,1},{8,4},{9,5},{12,8},{13,9},{14,12},{15,13},{10,14},{11,... | collective-permute-start | bytes 798728 | tf_op jit(solution)/shard_map/ppermute | solution.py:210
  66.8 0.5 collective-permute-start.24
  67.3 8.0 %collective-permute-done.24 = bf16[1040,128]{1,0:T(8,128)(2,1)S(1)} collective-permute-done((bf16[1040,128]{1,0:T(8,128)(2,1)S(1)}, bf16[1040,128]{1,0:T(8,128)(2,1)S(1)}, u32[]{:S(2)}, u32[]{:S(2)}) %collective-permute-start.24) | collective-permute-done | bytes 266272 | tf_op jit(solution)/shard_map/ppermute | solution.py:207
  75.3 0.5 collective-permute-start.25
  75.8 0.5 collective-permute-start.21
  76.4 6.6 %collective-permute-done.25 = bf16[1040,128]{1,0:T(8,128)(2,1)S(1)} collective-permute-done((bf16[1040,128]{1,0:T(8,128)(2,1)S(1)}, bf16[1040,128]{1,0:T(8,128)(2,1)S(1)}, u32[]{:S(2)}, u32[]{:S(2)}) %collective-permute-start.25) | collective-permute-done | bytes 266272 | tf_op jit(solution)/shard_map/ppermute | solution.py:207
  83.1 1.4 collective-permute-done.26
  84.9 7.4 %shard_map.62 = (f32[1024,128]{1,0:T(8,128)S(1)}, f32[8,128]{1,0:T(8,128)S(1)}, bf16[1040,128]{1,0:T(8,128)(2,1)S(1)}) custom-call(s32[80]{0:T(128)S(1)} %fusion.6.tile_ref, s32[16]{0:T(128)S(1)} %fusion.13.stat_ref, bf16[16640,128]{1,0:T(8,128)(2,1)S(1)} %constant_dynamic-update-slice_fusion.16.buf_ref, bf16[40960,128]{1,0:T(8,128)(2,1)S(1)} %get-tuple-element.13.env_ref, ...), custom_call_target="tpu_custom_call" | custom-call | flops 2684354560 | bytes 16777216 | tf_op jit(solution)/shard_map/pallas_call | solution.py:266
  92.3 1.7 %collective-permute-start.31 = (bf16[1040,128]{1,0:T(8,128)(2,1)S(1)}, bf16[1040,128]{1,0:T(8,128)(2,1)S(1)}, u32[]{:S(2)}, u32[]{:S(2)}) collective-permute-start(bf16[1040,128]{1,0:T(8,128)(2,1)S(1)} %get-tuple-element.18), channel_id=1, source_target_pairs={{4,0},{5,1},{8,4},{9,5},{12,8},{13,9},{14,12},{15,13},{10,14},{11,... | collective-permute-start | bytes 798728 | tf_op jit(solution)/shard_map/ppermute | solution.py:210
  94.4 6.4 %collective-permute-done.31 = bf16[1040,128]{1,0:T(8,128)(2,1)S(1)} collective-permute-done((bf16[1040,128]{1,0:T(8,128)(2,1)S(1)}, bf16[1040,128]{1,0:T(8,128)(2,1)S(1)}, u32[]{:S(2)}, u32[]{:S(2)}) %collective-permute-start.31) | collective-permute-done | bytes 266272 | tf_op jit(solution)/shard_map/ppermute | solution.py:210
  100.8 1.6 %collective-permute-start.33 = (bf16[1040,128]{1,0:T(8,128)(2,1)S(1)}, bf16[1040,128]{1,0:T(8,128)(2,1)S(1)}, u32[]{:S(2)}, u32[]{:S(2)}) collective-permute-start(bf16[1040,128]{1,0:T(8,128)(2,1)S(1)} %collective-permute-done.31), channel_id=1, source_target_pairs={{4,0},{5,1},{8,4},{9,5},{12,8},{13,9},{14,12},{15,13},{10,14},{11,... | collective-permute-start | bytes 798728 | tf_op jit(solution)/shard_map/ppermute | solution.py:210
  102.4 0.4 collective-permute-start.38
  102.9 6.7 %collective-permute-done.33 = bf16[1040,128]{1,0:T(8,128)(2,1)S(1)} collective-permute-done((bf16[1040,128]{1,0:T(8,128)(2,1)S(1)}, bf16[1040,128]{1,0:T(8,128)(2,1)S(1)}, u32[]{:S(2)}, u32[]{:S(2)}) %collective-permute-start.33) | collective-permute-done | bytes 266272 | tf_op jit(solution)/shard_map/ppermute | solution.py:210
  109.6 1.6 %collective-permute-start.35 = (bf16[1040,128]{1,0:T(8,128)(2,1)S(1)}, bf16[1040,128]{1,0:T(8,128)(2,1)S(1)}, u32[]{:S(2)}, u32[]{:S(2)}) collective-permute-start(bf16[1040,128]{1,0:T(8,128)(2,1)S(1)} %collective-permute-done.33), channel_id=1, source_target_pairs={{4,0},{5,1},{8,4},{9,5},{12,8},{13,9},{14,12},{15,13},{10,14},{11,... | collective-permute-start | bytes 798728 | tf_op jit(solution)/shard_map/ppermute | solution.py:210
  111.2 0.4 collective-permute-start.39
  111.8 8.0 %collective-permute-done.39 = bf16[1040,128]{1,0:T(8,128)(2,1)S(1)} collective-permute-done((bf16[1040,128]{1,0:T(8,128)(2,1)S(1)}, bf16[1040,128]{1,0:T(8,128)(2,1)S(1)}, u32[]{:S(2)}, u32[]{:S(2)}) %collective-permute-start.39) | collective-permute-done | bytes 266272 | tf_op jit(solution)/shard_map/ppermute | solution.py:207
  119.7 0.4 collective-permute-start.40
  120.2 0.5 collective-permute-start.36
  120.8 6.7 %collective-permute-done.40 = bf16[1040,128]{1,0:T(8,128)(2,1)S(1)} collective-permute-done((bf16[1040,128]{1,0:T(8,128)(2,1)S(1)}, bf16[1040,128]{1,0:T(8,128)(2,1)S(1)}, u32[]{:S(2)}, u32[]{:S(2)}) %collective-permute-start.40) | collective-permute-done | bytes 266272 | tf_op jit(solution)/shard_map/ppermute | solution.py:207
  127.5 1.4 collective-permute-done.41
  129.3 8.3 %shard_map.63 = (f32[1024,128]{1,0:T(8,128)}, f32[8,128]{1,0:T(8,128)S(1)}, f32[8,128]{1,0:T(8,128)S(1)}) custom-call(s32[80]{0:T(128)S(1)} %fusion.6.tile_ref, s32[16]{0:T(128)S(1)} %fusion.13.stat_ref, bf16[16640,128]{1,0:T(8,128)(2,1)S(1)} %constant_dynamic-update-slice_fusion.32.buf_ref, bf16[40960,128]{1,0:T(8,128)(2,1)S(1)} %get-tuple-element.13.env_ref, ...), custom_call_target="tpu_custom_call" | custom-call | flops 2684354560 | bytes 16777216 | tf_op jit(solution)/shard_map/pallas_call | solution.py:266
  137.7 1.0 collective-permute-done.45
  138.8 1.6 %collective-permute-start.46 = (f32[8,128]{1,0:T(8,128)S(1)}, f32[8,128]{1,0:T(8,128)S(1)}, u32[]{:S(2)}, u32[]{:S(2)}) collective-permute-start(f32[8,128]{1,0:T(8,128)S(1)} %add.114), channel_id=1, source_target_pairs={{0,2},{1,3},{2,0},{3,1},{4,6},{5,7},{6,4},{7,5},{8,10},{9,11},{10,... | collective-permute-start | bytes 12296 | tf_op jit(solution)/shard_map/ppermute | solution.py:286
  140.4 2.0 %collective-permute-done.46 = f32[8,128]{1,0:T(8,128)S(1)} collective-permute-done((f32[8,128]{1,0:T(8,128)S(1)}, f32[8,128]{1,0:T(8,128)S(1)}, u32[]{:S(2)}, u32[]{:S(2)}) %collective-permute-start.46) | collective-permute-done | bytes 4128 | tf_op jit(solution)/shard_map/ppermute | solution.py:286
  142.4 0.5 collective-permute-start.47
  142.8 3.2 %collective-permute-done.47 = f32[8,128]{1,0:T(8,128)S(1)} collective-permute-done((f32[8,128]{1,0:T(8,128)S(1)}, f32[8,128]{1,0:T(8,128)S(1)}, u32[]{:S(2)}, u32[]{:S(2)}) %collective-permute-start.47) | collective-permute-done | bytes 4128 | tf_op jit(solution)/shard_map/ppermute | solution.py:286
  146.3 4.2 %collective-permute-done.48 = f32[8,128]{1,0:T(8,128)S(1)} collective-permute-done((f32[8,128]{1,0:T(8,128)S(1)}, f32[8,128]{1,0:T(8,128)S(1)}, u32[]{:S(2)}, u32[]{:S(2)}) %collective-permute-start.48) | collective-permute-done | bytes 4128 | tf_op jit(solution)/shard_map/ppermute | solution.py:286
  150.5 0.7 shard_map.64
  (123 shorter events, 4.9 us)
Async XLA Ops:
  1.8 12.2 %collective-permute-start = (bf16[1040,128]{1,0:T(8,128)(2,1)S(1)}, bf16[1040,128]{1,0:T(8,128)(2,1)S(1)}, u32[]{:S(2)}, u32[]{:S(2)}) collective-permute-start(bf16[1040,128]{1,0:T(8,128)(2,1)S(1)} %shard_map.59), channel_id=1, source_target_pairs={{0,1},{1,0},{2,3},{3,2},{4,5},{5,4},{6,7},{7,6},{8,9},{9,8},{10,11... | collective-permute-start | bytes 798728 | tf_op jit(solution)/shard_map/ppermute | solution.py:214
  2.3 9.6 %collective-permute-start.1 = (bf16[1040,128]{1,0:T(8,128)(2,1)S(1)}, bf16[1040,128]{1,0:T(8,128)(2,1)S(1)}, u32[]{:S(2)}, u32[]{:S(2)}) collective-permute-start(bf16[1040,128]{1,0:T(8,128)(2,1)S(1)} %shard_map.59), channel_id=1, source_target_pairs={{4,0},{5,1},{8,4},{9,5},{12,8},{13,9},{14,12},{15,13},{10,14},{11,... | collective-permute-start | bytes 798728 | tf_op jit(solution)/shard_map/ppermute | solution.py:210
  4.8 8.8 %collective-permute-start.7 = (bf16[1040,128]{1,0:T(8,128)(2,1)S(1)}, bf16[1040,128]{1,0:T(8,128)(2,1)S(1)}, u32[]{:S(2)}, u32[]{:S(2)}) collective-permute-start(bf16[1040,128]{1,0:T(8,128)(2,1)S(1)} %shard_map.59), channel_id=1, source_target_pairs={{0,4},{1,5},{4,8},{5,9},{8,12},{9,13},{12,14},{13,15},{14,10},{15,... | collective-permute-start | bytes 798728 | tf_op jit(solution)/shard_map/ppermute | solution.py:207
  11.9 10.8 %collective-permute-start.2 = (bf16[1040,128]{1,0:T(8,128)(2,1)S(1)}, bf16[1040,128]{1,0:T(8,128)(2,1)S(1)}, u32[]{:S(2)}, u32[]{:S(2)}) collective-permute-start(bf16[1040,128]{1,0:T(8,128)(2,1)S(1)} %collective-permute-done.1), channel_id=1, source_target_pairs={{0,1},{1,0},{2,3},{3,2},{4,5},{5,4},{6,7},{7,6},{8,9},{9,8},{10,11... | collective-permute-start | bytes 798728 | tf_op jit(solution)/shard_map/ppermute | solution.py:214
  11.9 8.8 %collective-permute-start.3 = (bf16[1040,128]{1,0:T(8,128)(2,1)S(1)}, bf16[1040,128]{1,0:T(8,128)(2,1)S(1)}, u32[]{:S(2)}, u32[]{:S(2)}) collective-permute-start(bf16[1040,128]{1,0:T(8,128)(2,1)S(1)} %collective-permute-done.1), channel_id=1, source_target_pairs={{4,0},{5,1},{8,4},{9,5},{12,8},{13,9},{14,12},{15,13},{10,14},{11,... | collective-permute-start | bytes 798728 | tf_op jit(solution)/shard_map/ppermute | solution.py:210
  13.6 8.8 %collective-permute-start.8 = (bf16[1040,128]{1,0:T(8,128)(2,1)S(1)}, bf16[1040,128]{1,0:T(8,128)(2,1)S(1)}, u32[]{:S(2)}, u32[]{:S(2)}) collective-permute-start(bf16[1040,128]{1,0:T(8,128)(2,1)S(1)} %collective-permute-done.7), channel_id=1, source_target_pairs={{0,4},{1,5},{4,8},{5,9},{8,12},{9,13},{12,14},{13,15},{14,10},{15,... | collective-permute-start | bytes 798728 | tf_op jit(solution)/shard_map/ppermute | solution.py:207
  14.0 26.5 %collective-permute-start.14 = (bf16[1040,128]{1,0:T(8,128)(2,1)S(1)}, bf16[1040,128]{1,0:T(8,128)(2,1)S(1)}, u32[]{:S(2)}, u32[]{:S(2)}) collective-permute-start(bf16[1040,128]{1,0:T(8,128)(2,1)S(1)} %collective-permute-done.7), channel_id=1, source_target_pairs={{0,1},{1,0},{2,3},{3,2},{4,5},{5,4},{6,7},{7,6},{8,9},{9,8},{10,11... | collective-permute-start | bytes 798728 | tf_op jit(solution)/shard_map/ppermute | solution.py:214
  20.7 10.6 %collective-permute-start.4 = (bf16[1040,128]{1,0:T(8,128)(2,1)S(1)}, bf16[1040,128]{1,0:T(8,128)(2,1)S(1)}, u32[]{:S(2)}, u32[]{:S(2)}) collective-permute-start(bf16[1040,128]{1,0:T(8,128)(2,1)S(1)} %collective-permute-done.3), channel_id=1, source_target_pairs={{0,1},{1,0},{2,3},{3,2},{4,5},{5,4},{6,7},{7,6},{8,9},{9,8},{10,11... | collective-permute-start | bytes 798728 | tf_op jit(solution)/shard_map/ppermute | solution.py:214
  20.7 10.6 %collective-permute-start.5 = (bf16[1040,128]{1,0:T(8,128)(2,1)S(1)}, bf16[1040,128]{1,0:T(8,128)(2,1)S(1)}, u32[]{:S(2)}, u32[]{:S(2)}) collective-permute-start(bf16[1040,128]{1,0:T(8,128)(2,1)S(1)} %collective-permute-done.3), channel_id=1, source_target_pairs={{4,0},{5,1},{8,4},{9,5},{12,8},{13,9},{14,12},{15,13},{10,14},{11,... | collective-permute-start | bytes 798728 | tf_op jit(solution)/shard_map/ppermute | solution.py:210
  22.4 8.5 %collective-permute-start.9 = (bf16[1040,128]{1,0:T(8,128)(2,1)S(1)}, bf16[1040,128]{1,0:T(8,128)(2,1)S(1)}, u32[]{:S(2)}, u32[]{:S(2)}) collective-permute-start(bf16[1040,128]{1,0:T(8,128)(2,1)S(1)} %collective-permute-done.8), channel_id=1, source_target_pairs={{0,4},{1,5},{4,8},{5,9},{8,12},{9,13},{12,14},{13,15},{14,10},{15,... | collective-permute-start | bytes 798728 | tf_op jit(solution)/shard_map/ppermute | solution.py:207
  22.8 17.6 %collective-permute-start.13 = (bf16[1040,128]{1,0:T(8,128)(2,1)S(1)}, bf16[1040,128]{1,0:T(8,128)(2,1)S(1)}, u32[]{:S(2)}, u32[]{:S(2)}) collective-permute-start(bf16[1040,128]{1,0:T(8,128)(2,1)S(1)} %collective-permute-done.8), channel_id=1, source_target_pairs={{0,1},{1,0},{2,3},{3,2},{4,5},{5,4},{6,7},{7,6},{8,9},{9,8},{10,11... | collective-permute-start | bytes 798728 | tf_op jit(solution)/shard_map/ppermute | solution.py:214
  30.9 7.7 %collective-permute-start.10 = (bf16[1040,128]{1,0:T(8,128)(2,1)S(1)}, bf16[1040,128]{1,0:T(8,128)(2,1)S(1)}, u32[]{:S(2)}, u32[]{:S(2)}) collective-permute-start(bf16[1040,128]{1,0:T(8,128)(2,1)S(1)} %collective-permute-done.9), channel_id=1, source_target_pairs={{0,4},{1,5},{4,8},{5,9},{8,12},{9,13},{12,14},{13,15},{14,10},{15,... | collective-permute-start | bytes 798728 | tf_op jit(solution)/shard_map/ppermute | solution.py:207
  31.3 9.0 %collective-permute-start.12 = (bf16[1040,128]{1,0:T(8,128)(2,1)S(1)}, bf16[1040,128]{1,0:T(8,128)(2,1)S(1)}, u32[]{:S(2)}, u32[]{:S(2)}) collective-permute-start(bf16[1040,128]{1,0:T(8,128)(2,1)S(1)} %collective-permute-done.9), channel_id=1, source_target_pairs={{0,1},{1,0},{2,3},{3,2},{4,5},{5,4},{6,7},{7,6},{8,9},{9,8},{10,11... | collective-permute-start | bytes 798728 | tf_op jit(solution)/shard_map/ppermute | solution.py:214
  31.3 7.3 %collective-permute-start.6 = (bf16[1040,128]{1,0:T(8,128)(2,1)S(1)}, bf16[1040,128]{1,0:T(8,128)(2,1)S(1)}, u32[]{:S(2)}, u32[]{:S(2)}) collective-permute-start(bf16[1040,128]{1,0:T(8,128)(2,1)S(1)} %collective-permute-done.5), channel_id=1, source_target_pairs={{0,1},{1,0},{2,3},{3,2},{4,5},{5,4},{6,7},{7,6},{8,9},{9,8},{10,11... | collective-permute-start | bytes 798728 | tf_op jit(solution)/shard_map/ppermute | solution.py:214
  38.6 1.5 %collective-permute-start.11 = (bf16[1040,128]{1,0:T(8,128)(2,1)S(1)}, bf16[1040,128]{1,0:T(8,128)(2,1)S(1)}, u32[]{:S(2)}, u32[]{:S(2)}) collective-permute-start(bf16[1040,128]{1,0:T(8,128)(2,1)S(1)} %collective-permute-done.10), channel_id=1, source_target_pairs={{0,1},{1,0},{2,3},{3,2},{4,5},{5,4},{6,7},{7,6},{8,9},{9,8},{10,11... | collective-permute-start | bytes 798728 | tf_op jit(solution)/shard_map/ppermute | solution.py:214
  47.9 8.5 %collective-permute-start.16 = (bf16[1040,128]{1,0:T(8,128)(2,1)S(1)}, bf16[1040,128]{1,0:T(8,128)(2,1)S(1)}, u32[]{:S(2)}, u32[]{:S(2)}) collective-permute-start(bf16[1040,128]{1,0:T(8,128)(2,1)S(1)} %get-tuple-element.15), channel_id=1, source_target_pairs={{4,0},{5,1},{8,4},{9,5},{12,8},{13,9},{14,12},{15,13},{10,14},{11,... | collective-permute-start | bytes 798728 | tf_op jit(solution)/shard_map/ppermute | solution.py:210
  49.6 8.4 %collective-permute-start.22 = (bf16[1040,128]{1,0:T(8,128)(2,1)S(1)}, bf16[1040,128]{1,0:T(8,128)(2,1)S(1)}, u32[]{:S(2)}, u32[]{:S(2)}) collective-permute-start(bf16[1040,128]{1,0:T(8,128)(2,1)S(1)} %get-tuple-element.15), channel_id=1, source_target_pairs={{0,4},{1,5},{4,8},{5,9},{8,12},{9,13},{12,14},{13,15},{14,10},{15,... | collective-permute-start | bytes 798728 | tf_op jit(solution)/shard_map/ppermute | solution.py:207
  50.0 8.4 %collective-permute-start.15 = (bf16[1040,128]{1,0:T(8,128)(2,1)S(1)}, bf16[1040,128]{1,0:T(8,128)(2,1)S(1)}, u32[]{:S(2)}, u32[]{:S(2)}) collective-permute-start(bf16[1040,128]{1,0:T(8,128)(2,1)S(1)} %get-tuple-element.15), channel_id=1, source_target_pairs={{0,1},{1,0},{2,3},{3,2},{4,5},{5,4},{6,7},{7,6},{8,9},{9,8},{10,11... | collective-permute-start | bytes 798728 | tf_op jit(solution)/shard_map/ppermute | solution.py:214
  56.4 10.8 %collective-permute-start.17 = (bf16[1040,128]{1,0:T(8,128)(2,1)S(1)}, bf16[1040,128]{1,0:T(8,128)(2,1)S(1)}, u32[]{:S(2)}, u32[]{:S(2)}) collective-permute-start(bf16[1040,128]{1,0:T(8,128)(2,1)S(1)} %collective-permute-done.16), channel_id=1, source_target_pairs={{0,1},{1,0},{2,3},{3,2},{4,5},{5,4},{6,7},{7,6},{8,9},{9,8},{10,11... | collective-permute-start | bytes 798728 | tf_op jit(solution)/shard_map/ppermute | solution.py:214
  56.4 8.8 %collective-permute-start.18 = (bf16[1040,128]{1,0:T(8,128)(2,1)S(1)}, bf16[1040,128]{1,0:T(8,128)(2,1)S(1)}, u32[]{:S(2)}, u32[]{:S(2)}) collective-permute-start(bf16[1040,128]{1,0:T(8,128)(2,1)S(1)} %collective-permute-done.16), channel_id=1, source_target_pairs={{4,0},{5,1},{8,4},{9,5},{12,8},{13,9},{14,12},{15,13},{10,14},{11,... | collective-permute-start | bytes 798728 | tf_op jit(solution)/shard_map/ppermute | solution.py:210
  58.0 8.8 %collective-permute-start.23 = (bf16[1040,128]{1,0:T(8,128)(2,1)S(1)}, bf16[1040,128]{1,0:T(8,128)(2,1)S(1)}, u32[]{:S(2)}, u32[]{:S(2)}) collective-permute-start(bf16[1040,128]{1,0:T(8,128)(2,1)S(1)} %collective-permute-done.22), channel_id=1, source_target_pairs={{0,4},{1,5},{4,8},{5,9},{8,12},{9,13},{12,14},{13,15},{14,10},{15,... | collective-permute-start | bytes 798728 | tf_op jit(solution)/shard_map/ppermute | solution.py:207
  58.4 26.4 %collective-permute-start.29 = (bf16[1040,128]{1,0:T(8,128)(2,1)S(1)}, bf16[1040,128]{1,0:T(8,128)(2,1)S(1)}, u32[]{:S(2)}, u32[]{:S(2)}) collective-permute-start(bf16[1040,128]{1,0:T(8,128)(2,1)S(1)} %collective-permute-done.22), channel_id=1, source_target_pairs={{0,1},{1,0},{2,3},{3,2},{4,5},{5,4},{6,7},{7,6},{8,9},{9,8},{10,11... | collective-permute-start | bytes 798728 | tf_op jit(solution)/shard_map/ppermute | solution.py:214
  65.2 10.6 %collective-permute-start.19 = (bf16[1040,128]{1,0:T(8,128)(2,1)S(1)}, bf16[1040,128]{1,0:T(8,128)(2,1)S(1)}, u32[]{:S(2)}, u32[]{:S(2)}) collective-permute-start(bf16[1040,128]{1,0:T(8,128)(2,1)S(1)} %collective-permute-done.18), channel_id=1, source_target_pairs={{0,1},{1,0},{2,3},{3,2},{4,5},{5,4},{6,7},{7,6},{8,9},{9,8},{10,11... | collective-permute-start | bytes 798728 | tf_op jit(solution)/shard_map/ppermute | solution.py:214
  65.2 10.6 %collective-permute-start.20 = (bf16[1040,128]{1,0:T(8,128)(2,1)S(1)}, bf16[1040,128]{1,0:T(8,128)(2,1)S(1)}, u32[]{:S(2)}, u32[]{:S(2)}) collective-permute-start(bf16[1040,128]{1,0:T(8,128)(2,1)S(1)} %collective-permute-done.18), channel_id=1, source_target_pairs={{4,0},{5,1},{8,4},{9,5},{12,8},{13,9},{14,12},{15,13},{10,14},{11,... | collective-permute-start | bytes 798728 | tf_op jit(solution)/shard_map/ppermute | solution.py:210
  66.8 8.5 %collective-permute-start.24 = (bf16[1040,128]{1,0:T(8,128)(2,1)S(1)}, bf16[1040,128]{1,0:T(8,128)(2,1)S(1)}, u32[]{:S(2)}, u32[]{:S(2)}) collective-permute-start(bf16[1040,128]{1,0:T(8,128)(2,1)S(1)} %collective-permute-done.23), channel_id=1, source_target_pairs={{0,4},{1,5},{4,8},{5,9},{8,12},{9,13},{12,14},{13,15},{14,10},{15,... | collective-permute-start | bytes 798728 | tf_op jit(solution)/shard_map/ppermute | solution.py:207
  67.3 17.5 %collective-permute-start.28 = (bf16[1040,128]{1,0:T(8,128)(2,1)S(1)}, bf16[1040,128]{1,0:T(8,128)(2,1)S(1)}, u32[]{:S(2)}, u32[]{:S(2)}) collective-permute-start(bf16[1040,128]{1,0:T(8,128)(2,1)S(1)} %collective-permute-done.23), channel_id=1, source_target_pairs={{0,1},{1,0},{2,3},{3,2},{4,5},{5,4},{6,7},{7,6},{8,9},{9,8},{10,11... | collective-permute-start | bytes 798728 | tf_op jit(solution)/shard_map/ppermute | solution.py:214
  75.3 7.7 %collective-permute-start.25 = (bf16[1040,128]{1,0:T(8,128)(2,1)S(1)}, bf16[1040,128]{1,0:T(8,128)(2,1)S(1)}, u32[]{:S(2)}, u32[]{:S(2)}) collective-permute-start(bf16[1040,128]{1,0:T(8,128)(2,1)S(1)} %collective-permute-done.24), channel_id=1, source_target_pairs={{0,4},{1,5},{4,8},{5,9},{8,12},{9,13},{12,14},{13,15},{14,10},{15,... | collective-permute-start | bytes 798728 | tf_op jit(solution)/shard_map/ppermute | solution.py:207
  75.8 8.9 %collective-permute-start.27 = (bf16[1040,128]{1,0:T(8,128)(2,1)S(1)}, bf16[1040,128]{1,0:T(8,128)(2,1)S(1)}, u32[]{:S(2)}, u32[]{:S(2)}) collective-permute-start(bf16[1040,128]{1,0:T(8,128)(2,1)S(1)} %collective-permute-done.24), channel_id=1, source_target_pairs={{0,1},{1,0},{2,3},{3,2},{4,5},{5,4},{6,7},{7,6},{8,9},{9,8},{10,11... | collective-permute-start | bytes 798728 | tf_op jit(solution)/shard_map/ppermute | solution.py:214
  75.8 7.2 %collective-permute-start.21 = (bf16[1040,128]{1,0:T(8,128)(2,1)S(1)}, bf16[1040,128]{1,0:T(8,128)(2,1)S(1)}, u32[]{:S(2)}, u32[]{:S(2)}) collective-permute-start(bf16[1040,128]{1,0:T(8,128)(2,1)S(1)} %collective-permute-done.20), channel_id=1, source_target_pairs={{0,1},{1,0},{2,3},{3,2},{4,5},{5,4},{6,7},{7,6},{8,9},{9,8},{10,11... | collective-permute-start | bytes 798728 | tf_op jit(solution)/shard_map/ppermute | solution.py:214
  83.0 1.5 %collective-permute-start.26 = (bf16[1040,128]{1,0:T(8,128)(2,1)S(1)}, bf16[1040,128]{1,0:T(8,128)(2,1)S(1)}, u32[]{:S(2)}, u32[]{:S(2)}) collective-permute-start(bf16[1040,128]{1,0:T(8,128)(2,1)S(1)} %collective-permute-done.25), channel_id=1, source_target_pairs={{0,1},{1,0},{2,3},{3,2},{4,5},{5,4},{6,7},{7,6},{8,9},{9,8},{10,11... | collective-permute-start | bytes 798728 | tf_op jit(solution)/shard_map/ppermute | solution.py:214
  92.3 8.5 %collective-permute-start.31 = (bf16[1040,128]{1,0:T(8,128)(2,1)S(1)}, bf16[1040,128]{1,0:T(8,128)(2,1)S(1)}, u32[]{:S(2)}, u32[]{:S(2)}) collective-permute-start(bf16[1040,128]{1,0:T(8,128)(2,1)S(1)} %get-tuple-element.18), channel_id=1, source_target_pairs={{4,0},{5,1},{8,4},{9,5},{12,8},{13,9},{14,12},{15,13},{10,14},{11,... | collective-permute-start | bytes 798728 | tf_op jit(solution)/shard_map/ppermute | solution.py:210
  94.0 8.4 %collective-permute-start.37 = (bf16[1040,128]{1,0:T(8,128)(2,1)S(1)}, bf16[1040,128]{1,0:T(8,128)(2,1)S(1)}, u32[]{:S(2)}, u32[]{:S(2)}) collective-permute-start(bf16[1040,128]{1,0:T(8,128)(2,1)S(1)} %get-tuple-element.18), channel_id=1, source_target_pairs={{0,4},{1,5},{4,8},{5,9},{8,12},{9,13},{12,14},{13,15},{14,10},{15,... | collective-permute-start | bytes 798728 | tf_op jit(solution)/shard_map/ppermute | solution.py:207
  94.4 8.5 %collective-permute-start.30 = (bf16[1040,128]{1,0:T(8,128)(2,1)S(1)}, bf16[1040,128]{1,0:T(8,128)(2,1)S(1)}, u32[]{:S(2)}, u32[]{:S(2)}) collective-permute-start(bf16[1040,128]{1,0:T(8,128)(2,1)S(1)} %get-tuple-element.18), channel_id=1, source_target_pairs={{0,1},{1,0},{2,3},{3,2},{4,5},{5,4},{6,7},{7,6},{8,9},{9,8},{10,11... | collective-permute-start | bytes 798728 | tf_op jit(solution)/shard_map/ppermute | solution.py:214
  100.8 10.8 %collective-permute-start.32 = (bf16[1040,128]{1,0:T(8,128)(2,1)S(1)}, bf16[1040,128]{1,0:T(8,128)(2,1)S(1)}, u32[]{:S(2)}, u32[]{:S(2)}) collective-permute-start(bf16[1040,128]{1,0:T(8,128)(2,1)S(1)} %collective-permute-done.31), channel_id=1, source_target_pairs={{0,1},{1,0},{2,3},{3,2},{4,5},{5,4},{6,7},{7,6},{8,9},{9,8},{10,11... | collective-permute-start | bytes 798728 | tf_op jit(solution)/shard_map/ppermute | solution.py:214
  100.8 8.8 %collective-permute-start.33 = (bf16[1040,128]{1,0:T(8,128)(2,1)S(1)}, bf16[1040,128]{1,0:T(8,128)(2,1)S(1)}, u32[]{:S(2)}, u32[]{:S(2)}) collective-permute-start(bf16[1040,128]{1,0:T(8,128)(2,1)S(1)} %collective-permute-done.31), channel_id=1, source_target_pairs={{4,0},{5,1},{8,4},{9,5},{12,8},{13,9},{14,12},{15,13},{10,14},{11,... | collective-permute-start | bytes 798728 | tf_op jit(solution)/shard_map/ppermute | solution.py:210
  102.4 8.8 %collective-permute-start.38 = (bf16[1040,128]{1,0:T(8,128)(2,1)S(1)}, bf16[1040,128]{1,0:T(8,128)(2,1)S(1)}, u32[]{:S(2)}, u32[]{:S(2)}) collective-permute-start(bf16[1040,128]{1,0:T(8,128)(2,1)S(1)} %collective-permute-done.37), channel_id=1, source_target_pairs={{0,4},{1,5},{4,8},{5,9},{8,12},{9,13},{12,14},{13,15},{14,10},{15,... | collective-permute-start | bytes 798728 | tf_op jit(solution)/shard_map/ppermute | solution.py:207
  102.9 26.4 %collective-permute-start.44 = (bf16[1040,128]{1,0:T(8,128)(2,1)S(1)}, bf16[1040,128]{1,0:T(8,128)(2,1)S(1)}, u32[]{:S(2)}, u32[]{:S(2)}) collective-permute-start(bf16[1040,128]{1,0:T(8,128)(2,1)S(1)} %collective-permute-done.37), channel_id=1, source_target_pairs={{0,1},{1,0},{2,3},{3,2},{4,5},{5,4},{6,7},{7,6},{8,9},{9,8},{10,11... | collective-permute-start | bytes 798728 | tf_op jit(solution)/shard_map/ppermute | solution.py:214
  109.6 10.6 %collective-permute-start.34 = (bf16[1040,128]{1,0:T(8,128)(2,1)S(1)}, bf16[1040,128]{1,0:T(8,128)(2,1)S(1)}, u32[]{:S(2)}, u32[]{:S(2)}) collective-permute-start(bf16[1040,128]{1,0:T(8,128)(2,1)S(1)} %collective-permute-done.33), channel_id=1, source_target_pairs={{0,1},{1,0},{2,3},{3,2},{4,5},{5,4},{6,7},{7,6},{8,9},{9,8},{10,11... | collective-permute-start | bytes 798728 | tf_op jit(solution)/shard_map/ppermute | solution.py:214
  109.6 10.6 %collective-permute-start.35 = (bf16[1040,128]{1,0:T(8,128)(2,1)S(1)}, bf16[1040,128]{1,0:T(8,128)(2,1)S(1)}, u32[]{:S(2)}, u32[]{:S(2)}) collective-permute-start(bf16[1040,128]{1,0:T(8,128)(2,1)S(1)} %collective-permute-done.33), channel_id=1, source_target_pairs={{4,0},{5,1},{8,4},{9,5},{12,8},{13,9},{14,12},{15,13},{10,14},{11,... | collective-permute-start | bytes 798728 | tf_op jit(solution)/shard_map/ppermute | solution.py:210
  111.2 8.5 %collective-permute-start.39 = (bf16[1040,128]{1,0:T(8,128)(2,1)S(1)}, bf16[1040,128]{1,0:T(8,128)(2,1)S(1)}, u32[]{:S(2)}, u32[]{:S(2)}) collective-permute-start(bf16[1040,128]{1,0:T(8,128)(2,1)S(1)} %collective-permute-done.38), channel_id=1, source_target_pairs={{0,4},{1,5},{4,8},{5,9},{8,12},{9,13},{12,14},{13,15},{14,10},{15,... | collective-permute-start | bytes 798728 | tf_op jit(solution)/shard_map/ppermute | solution.py:207
  111.7 17.5 %collective-permute-start.43 = (bf16[1040,128]{1,0:T(8,128)(2,1)S(1)}, bf16[1040,128]{1,0:T(8,128)(2,1)S(1)}, u32[]{:S(2)}, u32[]{:S(2)}) collective-permute-start(bf16[1040,128]{1,0:T(8,128)(2,1)S(1)} %collective-permute-done.38), channel_id=1, source_target_pairs={{0,1},{1,0},{2,3},{3,2},{4,5},{5,4},{6,7},{7,6},{8,9},{9,8},{10,11... | collective-permute-start | bytes 798728 | tf_op jit(solution)/shard_map/ppermute | solution.py:214
  119.7 7.7 %collective-permute-start.40 = (bf16[1040,128]{1,0:T(8,128)(2,1)S(1)}, bf16[1040,128]{1,0:T(8,128)(2,1)S(1)}, u32[]{:S(2)}, u32[]{:S(2)}) collective-permute-start(bf16[1040,128]{1,0:T(8,128)(2,1)S(1)} %collective-permute-done.39), channel_id=1, source_target_pairs={{0,4},{1,5},{4,8},{5,9},{8,12},{9,13},{12,14},{13,15},{14,10},{15,... | collective-permute-start | bytes 798728 | tf_op jit(solution)/shard_map/ppermute | solution.py:207
  120.2 8.9 %collective-permute-start.42 = (bf16[1040,128]{1,0:T(8,128)(2,1)S(1)}, bf16[1040,128]{1,0:T(8,128)(2,1)S(1)}, u32[]{:S(2)}, u32[]{:S(2)}) collective-permute-start(bf16[1040,128]{1,0:T(8,128)(2,1)S(1)} %collective-permute-done.39), channel_id=1, source_target_pairs={{0,1},{1,0},{2,3},{3,2},{4,5},{5,4},{6,7},{7,6},{8,9},{9,8},{10,11... | collective-permute-start | bytes 798728 | tf_op jit(solution)/shard_map/ppermute | solution.py:214
  120.2 7.3 %collective-permute-start.36 = (bf16[1040,128]{1,0:T(8,128)(2,1)S(1)}, bf16[1040,128]{1,0:T(8,128)(2,1)S(1)}, u32[]{:S(2)}, u32[]{:S(2)}) collective-permute-start(bf16[1040,128]{1,0:T(8,128)(2,1)S(1)} %collective-permute-done.35), channel_id=1, source_target_pairs={{0,1},{1,0},{2,3},{3,2},{4,5},{5,4},{6,7},{7,6},{8,9},{9,8},{10,11... | collective-permute-start | bytes 798728 | tf_op jit(solution)/shard_map/ppermute | solution.py:214
  127.5 1.5 %collective-permute-start.41 = (bf16[1040,128]{1,0:T(8,128)(2,1)S(1)}, bf16[1040,128]{1,0:T(8,128)(2,1)S(1)}, u32[]{:S(2)}, u32[]{:S(2)}) collective-permute-start(bf16[1040,128]{1,0:T(8,128)(2,1)S(1)} %collective-permute-done.40), channel_id=1, source_target_pairs={{0,1},{1,0},{2,3},{3,2},{4,5},{5,4},{6,7},{7,6},{8,9},{9,8},{10,11... | collective-permute-start | bytes 798728 | tf_op jit(solution)/shard_map/ppermute | solution.py:214
  138.8 3.6 %collective-permute-start.46 = (f32[8,128]{1,0:T(8,128)S(1)}, f32[8,128]{1,0:T(8,128)S(1)}, u32[]{:S(2)}, u32[]{:S(2)}) collective-permute-start(f32[8,128]{1,0:T(8,128)S(1)} %add.114), channel_id=1, source_target_pairs={{0,2},{1,3},{2,0},{3,1},{4,6},{5,7},{6,4},{7,5},{8,10},{9,11},{10,... | collective-permute-start | bytes 12296 | tf_op jit(solution)/shard_map/ppermute | solution.py:286
  142.4 3.6 %collective-permute-start.47 = (f32[8,128]{1,0:T(8,128)S(1)}, f32[8,128]{1,0:T(8,128)S(1)}, u32[]{:S(2)}, u32[]{:S(2)}) collective-permute-start(f32[8,128]{1,0:T(8,128)S(1)} %add.115), channel_id=1, source_target_pairs={{0,4},{1,5},{2,6},{3,7},{4,0},{5,1},{6,2},{7,3},{8,12},{9,13},{10,... | collective-permute-start | bytes 12296 | tf_op jit(solution)/shard_map/ppermute | solution.py:286
  146.0 4.5 %collective-permute-start.48 = (f32[8,128]{1,0:T(8,128)S(1)}, f32[8,128]{1,0:T(8,128)S(1)}, u32[]{:S(2)}, u32[]{:S(2)}) collective-permute-start(f32[8,128]{1,0:T(8,128)S(1)} %add.116), channel_id=1, source_target_pairs={{0,8},{1,9},{2,10},{3,11},{4,12},{5,13},{6,14},{7,15},{8,0},{9,1},... | collective-permute-start | bytes 12296 | tf_op jit(solution)/shard_map/ppermute | solution.py:286
  (6 other events, 40.8 us)

commit v2 on v1

--- a/solution.py
+++ b/solution.py
@@ -160,10 +160,11 @@
 def ring_pairs(peers):
     chips = peers // 2
     order = list(range(0, chips, 2)) + list(range(chips - 1, 0, -2))
-    forward = [
-        (order[j] * 2 + c, order[(j + 1) % chips] * 2 + c) for j in range(chips) for c in range(2)
-    ]
-    return forward, [(b, a) for a, b in forward]
+    pairs = []
+    for j in range(chips):
+        here, after = order[j] * 2, order[(j + 1) % chips] * 2
+        pairs += [(here, after), (after + 1, here + 1)]
+    return pairs
 
 
 def ring_place(chip, chips):
@@ -189,29 +190,37 @@
 
     if use_ring:
         chips = peers // 2
-        forward, backward = ring_pairs(peers)
+        onward = ring_pairs(peers)
         sibling = [(i, i ^ 1) for i in range(peers)]
+        core = own % 2
         here = ring_place(own // 2, chips)
 
         def slot_of(device):
-            steps = (ring_place(device // 2, chips) - here) % chips
-            return steps * 2 + (device % 2 + own % 2) % 2
+            ahead = (here - ring_place(device // 2, chips)) % chips
+            steps = jnp.where(core == 0, ahead, (chips - ahead) % chips)
+            other = (device + core) % 2
+            half = chips // 2
+            last = 2 + 4 * (half - 1)
+            direct = 2 + 4 * (steps - 1) + 2 * other
+            passed = 2 + 4 * (chips - steps - 1) + 3 - 2 * other
+            slot = jnp.where(steps < half, direct, passed)
+            slot = jnp.where(steps == half, last + other, slot)
+            return jnp.where(steps == 0, other, slot)
 
         tile_offset = slot_of(source) * piece_rows + local * tile_rows
         stat_offset = slot_of(devices) * piece_rows + rows
 
         def exchange(piece):
-            pieces = {0: piece}
-            ahead = behind = piece
+            first, second = lax.optimization_barrier(
+                (piece, lax.ppermute(piece, "sector", sibling))
+            )
+            parts = [first, second]
             for step in range(1, chips // 2 + 1):
-                ahead = lax.ppermute(ahead, "sector", forward)
-                pieces[chips - step] = ahead
+                first = lax.ppermute(first, "sector", onward)
+                parts += [first, lax.ppermute(first, "sector", sibling)]
                 if 2 * step < chips:
-                    behind = lax.ppermute(behind, "sector", backward)
-                    pieces[step] = behind
-            parts = []
-            for j in range(chips):
-                parts += [pieces[j], lax.ppermute(pieces[j], "sector", sibling)]
+                    second = lax.ppermute(second, "sector", onward)
+                    parts += [second, lax.ppermute(second, "sector", sibling)]
             return jnp.concatenate(parts, axis=0)
 
     else:
@@ -238,7 +247,7 @@
 
     vmem = pl.BlockSpec(memory_space=pltpu.VMEM)
     smem = pl.BlockSpec(memory_space=pltpu.SMEM)
-    hbm = pl.BlockSpec(memory_space=pl.ANY)
+    hbm = pl.BlockSpec(memory_space=pltpu.HBM)
 
     piece = pl.pallas_call(
         start_kernel,

time: 151 us -> 130 us (0.86)
  waiting for transfers between devices: 92.1 us -> 54.8 us
  starting transfers between devices: 24.9 us -> 40.6 us
    ppermute x45, waiting for transfers between devices: 81.7 us -> 47.1 us  [the longest x12 29.1 us: exchange(): first = lax.ppermute(first, 'sector', onward)]
    ppermute x45, starting transfers between devices: 22.4 us -> 35.3 us  [the longest x12 20.2 us: exchange(): first = lax.ppermute(first, 'sector', onward)]
    ppermute x4, waiting for transfers between devices: 10.4 us -> 7.68 us  [per_device(): stats = stats + lax.ppermute(stats, 'sector', pairs)]
    ppermute x4, starting transfers between devices: 2.5 us -> 5.21 us  [per_device(): stats = stats + lax.ppermute(stats, 'sector', pairs)]
  transfers between devices with their start and end apart: 49 -> 49, of which waited for: 19 -> 29; matrix products, arithmetic and copies ran while one was open for 1% -> 1% of each run, Pallas kernels for 1% -> 1%
where the time goes in v2:
time: 130 us
  waiting for transfers between devices  54.8 us (42%)
  starting transfers between devices  40.6 us (31%)
  Pallas kernels  24.8 us (19%)
  local copies, waits for them, and re-layouts  8.2 us (6%)
    ppermute x12, waiting for transfers between devices, exchange(): first = lax.ppermute(first, 'sector', onward)  29.1 us
    pallas_call x3, Pallas kernels, apply_operator(): pl.pallas_call(functools.partial(apply_kernel, stage, sizes), out_shape=(...  23.1 us
    ppermute x12, starting transfers between devices, exchange(): first = lax.ppermute(first, 'sector', onward)  20.2 us
    ppermute x9, starting transfers between devices, exchange(): second = lax.ppermute(second, 'sector', onward)  13.9 us
    ppermute x9, waiting for transfers between devices, exchange(): second = lax.ppermute(second, 'sector', onward)  10.3 us
    unnamed x55, local copies, waits for them, and re-layouts  7.86 us
    ppermute x4, waiting for transfers between devices, per_device(): stats = stats + lax.ppermute(stats, 'sector', pairs)  7.68 us
    ppermute x4, starting transfers between devices, per_device(): stats = stats + lax.ppermute(stats, 'sector', pairs)  5.21 us
  transfers between devices with their start and end apart: 49, of which 29 were waited for; matrix products, arithmetic and copies ran while one was open for 1% of the time, Pallas kernels for 1%

profile of v2, /device:TPU:0, one launch (start us, length us, event | category | flops | bytes accessed | tf_op | source)
XLA Modules:
  0.0 129.7 jit_solution(16684210658380949342)
XLA Ops:
  3.5 2.9 %collective-permute-start.1 = (bf16[1040,128]{1,0:T(8,128)(2,1)S(1)}, bf16[1040,128]{1,0:T(8,128)(2,1)S(1)}, u32[]{:S(2)}, u32[]{:S(2)}) collective-permute-start(bf16[1040,128]{1,0:T(8,128)(2,1)S(1)} %shard_map.59), channel_id=1, source_target_pairs={{0,4},{5,1},{4,8},{9,5},{8,12},{13,9},{12,14},{15,13},{14,10},{11,... | collective-permute-start | bytes 798728 | tf_op jit(solution)/shard_map/ppermute | solution.py:219
  6.4 1.6 %collective-permute-start.3 = (bf16[1040,128]{1,0:T(8,128)(2,1)S(1)}, bf16[1040,128]{1,0:T(8,128)(2,1)S(1)}, u32[]{:S(2)}, u32[]{:S(2)}) collective-permute-start(bf16[1040,128]{1,0:T(8,128)(2,1)S(1)} %collective-permute-done), channel_id=1, source_target_pairs={{0,4},{5,1},{4,8},{9,5},{8,12},{13,9},{12,14},{15,13},{14,10},{11,... | collective-permute-start | bytes 798728 | tf_op jit(solution)/shard_map/ppermute | solution.py:222
  8.0 4.0 %copy-done.1 = bf16[8,40,128,128]{3,2,1,0:T(8,128)(2,1)S(1)} copy-done((bf16[8,40,128,128]{3,2,1,0:T(8,128)(2,1)S(1)}, bf16[8,40,128,128]{3,2,1,0:T(8,128)(2,1)}, u32[]{:S(2)}) %copy-start.1) | copy-done | bytes 10485784
  12.0 1.3 %copy-done.4 = bf16[40,128,128]{2,1,0:T(8,128)(2,1)S(1)} copy-done((bf16[40,128,128]{2,1,0:T(8,128)(2,1)S(1)}, bf16[40,128,128]{2,1,0:T(8,128)(2,1)}, u32[]{:S(2)}) %copy-start.4) | copy-done | bytes 1310744
  14.3 1.6 %collective-permute-start.5 = (bf16[1040,128]{1,0:T(8,128)(2,1)S(1)}, bf16[1040,128]{1,0:T(8,128)(2,1)S(1)}, u32[]{:S(2)}, u32[]{:S(2)}) collective-permute-start(bf16[1040,128]{1,0:T(8,128)(2,1)S(1)} %collective-permute-done.1), channel_id=1, source_target_pairs={{0,4},{5,1},{4,8},{9,5},{8,12},{13,9},{12,14},{15,13},{14,10},{11,... | collective-permute-start | bytes 798728 | tf_op jit(solution)/shard_map/ppermute | solution.py:219
  16.0 1.5 %collective-permute-start.7 = (bf16[1040,128]{1,0:T(8,128)(2,1)S(1)}, bf16[1040,128]{1,0:T(8,128)(2,1)S(1)}, u32[]{:S(2)}, u32[]{:S(2)}) collective-permute-start(bf16[1040,128]{1,0:T(8,128)(2,1)S(1)} %collective-permute-done.3), channel_id=1, source_target_pairs={{0,4},{5,1},{4,8},{9,5},{8,12},{13,9},{12,14},{15,13},{14,10},{11,... | collective-permute-start | bytes 798728 | tf_op jit(solution)/shard_map/ppermute | solution.py:222
  17.6 3.2 %collective-permute-done.5 = bf16[1040,128]{1,0:T(8,128)(2,1)S(1)} collective-permute-done((bf16[1040,128]{1,0:T(8,128)(2,1)S(1)}, bf16[1040,128]{1,0:T(8,128)(2,1)S(1)}, u32[]{:S(2)}, u32[]{:S(2)}) %collective-permute-start.5) | collective-permute-done | bytes 266272 | tf_op jit(solution)/shard_map/ppermute | solution.py:219
  20.8 1.6 %collective-permute-start.9 = (bf16[1040,128]{1,0:T(8,128)(2,1)S(1)}, bf16[1040,128]{1,0:T(8,128)(2,1)S(1)}, u32[]{:S(2)}, u32[]{:S(2)}) collective-permute-start(bf16[1040,128]{1,0:T(8,128)(2,1)S(1)} %collective-permute-done.5), channel_id=1, source_target_pairs={{0,4},{5,1},{4,8},{9,5},{8,12},{13,9},{12,14},{15,13},{14,10},{11,... | collective-permute-start | bytes 798728 | tf_op jit(solution)/shard_map/ppermute | solution.py:219
  23.7 1.6 %collective-permute-start.11 = (bf16[1040,128]{1,0:T(8,128)(2,1)S(1)}, bf16[1040,128]{1,0:T(8,128)(2,1)S(1)}, u32[]{:S(2)}, u32[]{:S(2)}) collective-permute-start(bf16[1040,128]{1,0:T(8,128)(2,1)S(1)} %collective-permute-done.7), channel_id=1, source_target_pairs={{0,4},{5,1},{4,8},{9,5},{8,12},{13,9},{12,14},{15,13},{14,10},{11,... | collective-permute-start | bytes 798728 | tf_op jit(solution)/shard_map/ppermute | solution.py:222
  25.4 1.8 %collective-permute-done.9 = bf16[1040,128]{1,0:T(8,128)(2,1)S(1)} collective-permute-done((bf16[1040,128]{1,0:T(8,128)(2,1)S(1)}, bf16[1040,128]{1,0:T(8,128)(2,1)S(1)}, u32[]{:S(2)}, u32[]{:S(2)}) %collective-permute-start.9) | collective-permute-done | bytes 266272 | tf_op jit(solution)/shard_map/ppermute | solution.py:219
  27.2 1.6 %collective-permute-start.13 = (bf16[1040,128]{1,0:T(8,128)(2,1)S(1)}, bf16[1040,128]{1,0:T(8,128)(2,1)S(1)}, u32[]{:S(2)}, u32[]{:S(2)}) collective-permute-start(bf16[1040,128]{1,0:T(8,128)(2,1)S(1)} %collective-permute-done.9), channel_id=1, source_target_pairs={{0,4},{5,1},{4,8},{9,5},{8,12},{13,9},{12,14},{15,13},{14,10},{11,... | collective-permute-start | bytes 798728 | tf_op jit(solution)/shard_map/ppermute | solution.py:219
  30.3 3.4 %collective-permute-done.13 = bf16[1040,128]{1,0:T(8,128)(2,1)S(1)} collective-permute-done((bf16[1040,128]{1,0:T(8,128)(2,1)S(1)}, bf16[1040,128]{1,0:T(8,128)(2,1)S(1)}, u32[]{:S(2)}, u32[]{:S(2)}) %collective-permute-start.13) | collective-permute-done | bytes 266272 | tf_op jit(solution)/shard_map/ppermute | solution.py:219
  33.8 1.4 %collective-permute-done.14 = bf16[1040,128]{1,0:T(8,128)(2,1)S(1)} collective-permute-done((bf16[1040,128]{1,0:T(8,128)(2,1)S(1)}, bf16[1040,128]{1,0:T(8,128)(2,1)S(1)}, u32[]{:S(2)}, u32[]{:S(2)}) %collective-permute-start.14) | collective-permute-done | bytes 266272 | tf_op jit(solution)/shard_map/ppermute | solution.py:220
  35.2 7.4 %shard_map.61 = (f32[1024,128]{1,0:T(8,128)S(1)}, f32[8,128]{1,0:T(8,128)S(1)}, bf16[1040,128]{1,0:T(8,128)(2,1)S(1)}) custom-call(s32[80]{0:T(128)S(1)} %fusion.1.tile_ref, s32[16]{0:T(128)S(1)} %fusion.10.stat_ref, bf16[16640,128]{1,0:T(8,128)(2,1)S(1)} %constant_dynamic-update-slice_fusion.buf_ref, bf16[40960,128]{1,0:T(8,128)(2,1)S(1)} %get-tuple-element.21.env_ref, ...), custom_call_target="tpu_custom_call" | custom-call | flops 2684354560 | bytes 16777216 | tf_op jit(solution)/shard_map/pallas_call | solution.py:275
  42.9 1.4 %collective-permute-done.15 = bf16[1040,128]{1,0:T(8,128)(2,1)S(1)} collective-permute-done((bf16[1040,128]{1,0:T(8,128)(2,1)S(1)}, bf16[1040,128]{1,0:T(8,128)(2,1)S(1)}, u32[]{:S(2)}, u32[]{:S(2)}) %collective-permute-start.15) | collective-permute-done | bytes 266272 | tf_op jit(solution)/shard_map/ppermute | solution.py:215
  44.3 1.6 %collective-permute-start.16 = (bf16[1040,128]{1,0:T(8,128)(2,1)S(1)}, bf16[1040,128]{1,0:T(8,128)(2,1)S(1)}, u32[]{:S(2)}, u32[]{:S(2)}) collective-permute-start(bf16[1040,128]{1,0:T(8,128)(2,1)S(1)} %get-tuple-element.24), channel_id=1, source_target_pairs={{0,4},{5,1},{4,8},{9,5},{8,12},{13,9},{12,14},{15,13},{14,10},{11,... | collective-permute-start | bytes 798728 | tf_op jit(solution)/shard_map/ppermute | solution.py:219
  45.8 1.5 %collective-permute-start.18 = (bf16[1040,128]{1,0:T(8,128)(2,1)S(1)}, bf16[1040,128]{1,0:T(8,128)(2,1)S(1)}, u32[]{:S(2)}, u32[]{:S(2)}) collective-permute-start(bf16[1040,128]{1,0:T(8,128)(2,1)S(1)} %collective-permute-done.15), channel_id=1, source_target_pairs={{0,4},{5,1},{4,8},{9,5},{8,12},{13,9},{12,14},{15,13},{14,10},{11,... | collective-permute-start | bytes 798728 | tf_op jit(solution)/shard_map/ppermute | solution.py:222
  47.3 3.3 %collective-permute-done.16 = bf16[1040,128]{1,0:T(8,128)(2,1)S(1)} collective-permute-done((bf16[1040,128]{1,0:T(8,128)(2,1)S(1)}, bf16[1040,128]{1,0:T(8,128)(2,1)S(1)}, u32[]{:S(2)}, u32[]{:S(2)}) %collective-permute-start.16) | collective-permute-done | bytes 266272 | tf_op jit(solution)/shard_map/ppermute | solution.py:219
  50.7 1.6 %collective-permute-start.20 = (bf16[1040,128]{1,0:T(8,128)(2,1)S(1)}, bf16[1040,128]{1,0:T(8,128)(2,1)S(1)}, u32[]{:S(2)}, u32[]{:S(2)}) collective-permute-start(bf16[1040,128]{1,0:T(8,128)(2,1)S(1)} %collective-permute-done.16), channel_id=1, source_target_pairs={{0,4},{5,1},{4,8},{9,5},{8,12},{13,9},{12,14},{15,13},{14,10},{11,... | collective-permute-start | bytes 798728 | tf_op jit(solution)/shard_map/ppermute | solution.py:219
  53.5 1.6 %collective-permute-start.22 = (bf16[1040,128]{1,0:T(8,128)(2,1)S(1)}, bf16[1040,128]{1,0:T(8,128)(2,1)S(1)}, u32[]{:S(2)}, u32[]{:S(2)}) collective-permute-start(bf16[1040,128]{1,0:T(8,128)(2,1)S(1)} %collective-permute-done.18), channel_id=1, source_target_pairs={{0,4},{5,1},{4,8},{9,5},{8,12},{13,9},{12,14},{15,13},{14,10},{11,... | collective-permute-start | bytes 798728 | tf_op jit(solution)/shard_map/ppermute | solution.py:222
  55.3 1.8 %collective-permute-done.20 = bf16[1040,128]{1,0:T(8,128)(2,1)S(1)} collective-permute-done((bf16[1040,128]{1,0:T(8,128)(2,1)S(1)}, bf16[1040,128]{1,0:T(8,128)(2,1)S(1)}, u32[]{:S(2)}, u32[]{:S(2)}) %collective-permute-start.20) | collective-permute-done | bytes 266272 | tf_op jit(solution)/shard_map/ppermute | solution.py:219
  57.1 1.6 %collective-permute-start.24 = (bf16[1040,128]{1,0:T(8,128)(2,1)S(1)}, bf16[1040,128]{1,0:T(8,128)(2,1)S(1)}, u32[]{:S(2)}, u32[]{:S(2)}) collective-permute-start(bf16[1040,128]{1,0:T(8,128)(2,1)S(1)} %collective-permute-done.20), channel_id=1, source_target_pairs={{0,4},{5,1},{4,8},{9,5},{8,12},{13,9},{12,14},{15,13},{14,10},{11,... | collective-permute-start | bytes 798728 | tf_op jit(solution)/shard_map/ppermute | solution.py:219
  60.0 1.6 %collective-permute-start.26 = (bf16[1040,128]{1,0:T(8,128)(2,1)S(1)}, bf16[1040,128]{1,0:T(8,128)(2,1)S(1)}, u32[]{:S(2)}, u32[]{:S(2)}) collective-permute-start(bf16[1040,128]{1,0:T(8,128)(2,1)S(1)} %collective-permute-done.22), channel_id=1, source_target_pairs={{0,4},{5,1},{4,8},{9,5},{8,12},{13,9},{12,14},{15,13},{14,10},{11,... | collective-permute-start | bytes 798728 | tf_op jit(solution)/shard_map/ppermute | solution.py:222
  61.7 1.8 %collective-permute-done.24 = bf16[1040,128]{1,0:T(8,128)(2,1)S(1)} collective-permute-done((bf16[1040,128]{1,0:T(8,128)(2,1)S(1)}, bf16[1040,128]{1,0:T(8,128)(2,1)S(1)}, u32[]{:S(2)}, u32[]{:S(2)}) %collective-permute-start.24) | collective-permute-done | bytes 266272 | tf_op jit(solution)/shard_map/ppermute | solution.py:219
  63.5 1.6 %collective-permute-start.28 = (bf16[1040,128]{1,0:T(8,128)(2,1)S(1)}, bf16[1040,128]{1,0:T(8,128)(2,1)S(1)}, u32[]{:S(2)}, u32[]{:S(2)}) collective-permute-start(bf16[1040,128]{1,0:T(8,128)(2,1)S(1)} %collective-permute-done.24), channel_id=1, source_target_pairs={{0,4},{5,1},{4,8},{9,5},{8,12},{13,9},{12,14},{15,13},{14,10},{11,... | collective-permute-start | bytes 798728 | tf_op jit(solution)/shard_map/ppermute | solution.py:219
  66.6 3.4 %collective-permute-done.28 = bf16[1040,128]{1,0:T(8,128)(2,1)S(1)} collective-permute-done((bf16[1040,128]{1,0:T(8,128)(2,1)S(1)}, bf16[1040,128]{1,0:T(8,128)(2,1)S(1)}, u32[]{:S(2)}, u32[]{:S(2)}) %collective-permute-start.28) | collective-permute-done | bytes 266272 | tf_op jit(solution)/shard_map/ppermute | solution.py:219
  70.1 1.4 %collective-permute-done.29 = bf16[1040,128]{1,0:T(8,128)(2,1)S(1)} collective-permute-done((bf16[1040,128]{1,0:T(8,128)(2,1)S(1)}, bf16[1040,128]{1,0:T(8,128)(2,1)S(1)}, u32[]{:S(2)}, u32[]{:S(2)}) %collective-permute-start.29) | collective-permute-done | bytes 266272 | tf_op jit(solution)/shard_map/ppermute | solution.py:220
  71.5 7.4 %shard_map.62 = (f32[1024,128]{1,0:T(8,128)S(1)}, f32[8,128]{1,0:T(8,128)S(1)}, bf16[1040,128]{1,0:T(8,128)(2,1)S(1)}) custom-call(s32[80]{0:T(128)S(1)} %fusion.1.tile_ref, s32[16]{0:T(128)S(1)} %fusion.10.stat_ref, bf16[16640,128]{1,0:T(8,128)(2,1)S(1)} %constant_dynamic-update-slice_fusion.16.buf_ref, bf16[40960,128]{1,0:T(8,128)(2,1)S(1)} %get-tuple-element.21.env_ref, ...), custom_call_target="tpu_custom_call" | custom-call | flops 2684354560 | bytes 16777216 | tf_op jit(solution)/shard_map/pallas_call | solution.py:275
  79.1 1.4 %collective-permute-done.30 = bf16[1040,128]{1,0:T(8,128)(2,1)S(1)} collective-permute-done((bf16[1040,128]{1,0:T(8,128)(2,1)S(1)}, bf16[1040,128]{1,0:T(8,128)(2,1)S(1)}, u32[]{:S(2)}, u32[]{:S(2)}) %collective-permute-start.30) | collective-permute-done | bytes 266272 | tf_op jit(solution)/shard_map/ppermute | solution.py:215
  80.6 1.6 %collective-permute-start.31 = (bf16[1040,128]{1,0:T(8,128)(2,1)S(1)}, bf16[1040,128]{1,0:T(8,128)(2,1)S(1)}, u32[]{:S(2)}, u32[]{:S(2)}) collective-permute-start(bf16[1040,128]{1,0:T(8,128)(2,1)S(1)} %get-tuple-element.29), channel_id=1, source_target_pairs={{0,4},{5,1},{4,8},{9,5},{8,12},{13,9},{12,14},{15,13},{14,10},{11,... | collective-permute-start | bytes 798728 | tf_op jit(solution)/shard_map/ppermute | solution.py:219
  82.1 1.5 %collective-permute-start.33 = (bf16[1040,128]{1,0:T(8,128)(2,1)S(1)}, bf16[1040,128]{1,0:T(8,128)(2,1)S(1)}, u32[]{:S(2)}, u32[]{:S(2)}) collective-permute-start(bf16[1040,128]{1,0:T(8,128)(2,1)S(1)} %collective-permute-done.30), channel_id=1, source_target_pairs={{0,4},{5,1},{4,8},{9,5},{8,12},{13,9},{12,14},{15,13},{14,10},{11,... | collective-permute-start | bytes 798728 | tf_op jit(solution)/shard_map/ppermute | solution.py:222
  83.6 3.4 %collective-permute-done.31 = bf16[1040,128]{1,0:T(8,128)(2,1)S(1)} collective-permute-done((bf16[1040,128]{1,0:T(8,128)(2,1)S(1)}, bf16[1040,128]{1,0:T(8,128)(2,1)S(1)}, u32[]{:S(2)}, u32[]{:S(2)}) %collective-permute-start.31) | collective-permute-done | bytes 266272 | tf_op jit(solution)/shard_map/ppermute | solution.py:219
  87.0 1.6 %collective-permute-start.35 = (bf16[1040,128]{1,0:T(8,128)(2,1)S(1)}, bf16[1040,128]{1,0:T(8,128)(2,1)S(1)}, u32[]{:S(2)}, u32[]{:S(2)}) collective-permute-start(bf16[1040,128]{1,0:T(8,128)(2,1)S(1)} %collective-permute-done.31), channel_id=1, source_target_pairs={{0,4},{5,1},{4,8},{9,5},{8,12},{13,9},{12,14},{15,13},{14,10},{11,... | collective-permute-start | bytes 798728 | tf_op jit(solution)/shard_map/ppermute | solution.py:219
  89.8 1.6 %collective-permute-start.37 = (bf16[1040,128]{1,0:T(8,128)(2,1)S(1)}, bf16[1040,128]{1,0:T(8,128)(2,1)S(1)}, u32[]{:S(2)}, u32[]{:S(2)}) collective-permute-start(bf16[1040,128]{1,0:T(8,128)(2,1)S(1)} %collective-permute-done.33), channel_id=1, source_target_pairs={{0,4},{5,1},{4,8},{9,5},{8,12},{13,9},{12,14},{15,13},{14,10},{11,... | collective-permute-start | bytes 798728 | tf_op jit(solution)/shard_map/ppermute | solution.py:222
  91.6 1.8 %collective-permute-done.35 = bf16[1040,128]{1,0:T(8,128)(2,1)S(1)} collective-permute-done((bf16[1040,128]{1,0:T(8,128)(2,1)S(1)}, bf16[1040,128]{1,0:T(8,128)(2,1)S(1)}, u32[]{:S(2)}, u32[]{:S(2)}) %collective-permute-start.35) | collective-permute-done | bytes 266272 | tf_op jit(solution)/shard_map/ppermute | solution.py:219
  93.4 1.6 %collective-permute-start.39 = (bf16[1040,128]{1,0:T(8,128)(2,1)S(1)}, bf16[1040,128]{1,0:T(8,128)(2,1)S(1)}, u32[]{:S(2)}, u32[]{:S(2)}) collective-permute-start(bf16[1040,128]{1,0:T(8,128)(2,1)S(1)} %collective-permute-done.35), channel_id=1, source_target_pairs={{0,4},{5,1},{4,8},{9,5},{8,12},{13,9},{12,14},{15,13},{14,10},{11,... | collective-permute-start | bytes 798728 | tf_op jit(solution)/shard_map/ppermute | solution.py:219
  96.3 1.6 %collective-permute-start.41 = (bf16[1040,128]{1,0:T(8,128)(2,1)S(1)}, bf16[1040,128]{1,0:T(8,128)(2,1)S(1)}, u32[]{:S(2)}, u32[]{:S(2)}) collective-permute-start(bf16[1040,128]{1,0:T(8,128)(2,1)S(1)} %collective-permute-done.37), channel_id=1, source_target_pairs={{0,4},{5,1},{4,8},{9,5},{8,12},{13,9},{12,14},{15,13},{14,10},{11,... | collective-permute-start | bytes 798728 | tf_op jit(solution)/shard_map/ppermute | solution.py:222
  98.0 1.8 %collective-permute-done.39 = bf16[1040,128]{1,0:T(8,128)(2,1)S(1)} collective-permute-done((bf16[1040,128]{1,0:T(8,128)(2,1)S(1)}, bf16[1040,128]{1,0:T(8,128)(2,1)S(1)}, u32[]{:S(2)}, u32[]{:S(2)}) %collective-permute-start.39) | collective-permute-done | bytes 266272 | tf_op jit(solution)/shard_map/ppermute | solution.py:219
  99.8 1.6 %collective-permute-start.43 = (bf16[1040,128]{1,0:T(8,128)(2,1)S(1)}, bf16[1040,128]{1,0:T(8,128)(2,1)S(1)}, u32[]{:S(2)}, u32[]{:S(2)}) collective-permute-start(bf16[1040,128]{1,0:T(8,128)(2,1)S(1)} %collective-permute-done.39), channel_id=1, source_target_pairs={{0,4},{5,1},{4,8},{9,5},{8,12},{13,9},{12,14},{15,13},{14,10},{11,... | collective-permute-start | bytes 798728 | tf_op jit(solution)/shard_map/ppermute | solution.py:219
  101.4 1.3 collective-permute-done.41
  102.9 3.4 %collective-permute-done.43 = bf16[1040,128]{1,0:T(8,128)(2,1)S(1)} collective-permute-done((bf16[1040,128]{1,0:T(8,128)(2,1)S(1)}, bf16[1040,128]{1,0:T(8,128)(2,1)S(1)}, u32[]{:S(2)}, u32[]{:S(2)}) %collective-permute-start.43) | collective-permute-done | bytes 266272 | tf_op jit(solution)/shard_map/ppermute | solution.py:219
  106.4 1.4 %collective-permute-done.44 = bf16[1040,128]{1,0:T(8,128)(2,1)S(1)} collective-permute-done((bf16[1040,128]{1,0:T(8,128)(2,1)S(1)}, bf16[1040,128]{1,0:T(8,128)(2,1)S(1)}, u32[]{:S(2)}, u32[]{:S(2)}) %collective-permute-start.44) | collective-permute-done | bytes 266272 | tf_op jit(solution)/shard_map/ppermute | solution.py:220
  107.8 8.3 %shard_map.63 = (f32[1024,128]{1,0:T(8,128)}, f32[8,128]{1,0:T(8,128)S(1)}, f32[8,128]{1,0:T(8,128)S(1)}) custom-call(s32[80]{0:T(128)S(1)} %fusion.1.tile_ref, s32[16]{0:T(128)S(1)} %fusion.10.stat_ref, bf16[16640,128]{1,0:T(8,128)(2,1)S(1)} %constant_dynamic-update-slice_fusion.32.buf_ref, bf16[40960,128]{1,0:T(8,128)(2,1)S(1)} %get-tuple-element.21.env_ref, ...), custom_call_target="tpu_custom_call" | custom-call | flops 2684354560 | bytes 16777216 | tf_op jit(solution)/shard_map/pallas_call | solution.py:275
  118.3 2.6 %collective-permute-done.46 = f32[8,128]{1,0:T(8,128)S(1)} collective-permute-done((f32[8,128]{1,0:T(8,128)S(1)}, f32[8,128]{1,0:T(8,128)S(1)}, u32[]{:S(2)}, u32[]{:S(2)}) %collective-permute-start.46) | collective-permute-done | bytes 4128 | tf_op jit(solution)/shard_map/ppermute | solution.py:295
  120.9 1.6 %collective-permute-start.47 = (f32[8,128]{1,0:T(8,128)S(1)}, f32[8,128]{1,0:T(8,128)S(1)}, u32[]{:S(2)}, u32[]{:S(2)}) collective-permute-start(f32[8,128]{1,0:T(8,128)S(1)} %add.161), channel_id=1, source_target_pairs={{0,4},{1,5},{2,6},{3,7},{4,0},{5,1},{6,2},{7,3},{8,12},{9,13},{10,... | collective-permute-start | bytes 12296 | tf_op jit(solution)/shard_map/ppermute | solution.py:295
  122.4 2.0 %collective-permute-done.47 = f32[8,128]{1,0:T(8,128)S(1)} collective-permute-done((f32[8,128]{1,0:T(8,128)S(1)}, f32[8,128]{1,0:T(8,128)S(1)}, u32[]{:S(2)}, u32[]{:S(2)}) %collective-permute-start.47) | collective-permute-done | bytes 4128 | tf_op jit(solution)/shard_map/ppermute | solution.py:295
  124.5 2.5 %collective-permute-start.48 = (f32[8,128]{1,0:T(8,128)S(1)}, f32[8,128]{1,0:T(8,128)S(1)}, u32[]{:S(2)}, u32[]{:S(2)}) collective-permute-start(f32[8,128]{1,0:T(8,128)S(1)} %add.162), channel_id=1, source_target_pairs={{0,8},{1,9},{2,10},{3,11},{4,12},{5,13},{6,14},{7,15},{8,0},{9,1},... | collective-permute-start | bytes 12296 | tf_op jit(solution)/shard_map/ppermute | solution.py:295
  127.0 2.0 %collective-permute-done.48 = f32[8,128]{1,0:T(8,128)S(1)} collective-permute-done((f32[8,128]{1,0:T(8,128)S(1)}, f32[8,128]{1,0:T(8,128)S(1)}, u32[]{:S(2)}, u32[]{:S(2)}) %collective-permute-start.48) | collective-permute-done | bytes 4128 | tf_op jit(solution)/shard_map/ppermute | solution.py:295
  (123 shorter events, 18.0 us)
Async XLA Ops:
  1.8 1.7 %collective-permute-start = (bf16[1040,128]{1,0:T(8,128)(2,1)S(1)}, bf16[1040,128]{1,0:T(8,128)(2,1)S(1)}, u32[]{:S(2)}, u32[]{:S(2)}) collective-permute-start(bf16[1040,128]{1,0:T(8,128)(2,1)S(1)} %shard_map.59), channel_id=1, source_target_pairs={{0,1},{1,0},{2,3},{3,2},{4,5},{5,4},{6,7},{7,6},{8,9},{9,8},{10,11... | collective-permute-start | bytes 798728 | tf_op jit(solution)/shard_map/ppermute | solution.py:215
  3.5 10.8 %collective-permute-start.1 = (bf16[1040,128]{1,0:T(8,128)(2,1)S(1)}, bf16[1040,128]{1,0:T(8,128)(2,1)S(1)}, u32[]{:S(2)}, u32[]{:S(2)}) collective-permute-start(bf16[1040,128]{1,0:T(8,128)(2,1)S(1)} %shard_map.59), channel_id=1, source_target_pairs={{0,4},{5,1},{4,8},{9,5},{8,12},{13,9},{12,14},{15,13},{14,10},{11,... | collective-permute-start | bytes 798728 | tf_op jit(solution)/shard_map/ppermute | solution.py:219
  6.4 9.6 %collective-permute-start.3 = (bf16[1040,128]{1,0:T(8,128)(2,1)S(1)}, bf16[1040,128]{1,0:T(8,128)(2,1)S(1)}, u32[]{:S(2)}, u32[]{:S(2)}) collective-permute-start(bf16[1040,128]{1,0:T(8,128)(2,1)S(1)} %collective-permute-done), channel_id=1, source_target_pairs={{0,4},{5,1},{4,8},{9,5},{8,12},{13,9},{12,14},{15,13},{14,10},{11,... | collective-permute-start | bytes 798728 | tf_op jit(solution)/shard_map/ppermute | solution.py:222
  14.3 9.4 %collective-permute-start.2 = (bf16[1040,128]{1,0:T(8,128)(2,1)S(1)}, bf16[1040,128]{1,0:T(8,128)(2,1)S(1)}, u32[]{:S(2)}, u32[]{:S(2)}) collective-permute-start(bf16[1040,128]{1,0:T(8,128)(2,1)S(1)} %collective-permute-done.1), channel_id=1, source_target_pairs={{0,1},{1,0},{2,3},{3,2},{4,5},{5,4},{6,7},{7,6},{8,9},{9,8},{10,11... | collective-permute-start | bytes 798728 | tf_op jit(solution)/shard_map/ppermute | solution.py:220
  14.3 6.5 %collective-permute-start.5 = (bf16[1040,128]{1,0:T(8,128)(2,1)S(1)}, bf16[1040,128]{1,0:T(8,128)(2,1)S(1)}, u32[]{:S(2)}, u32[]{:S(2)}) collective-permute-start(bf16[1040,128]{1,0:T(8,128)(2,1)S(1)} %collective-permute-done.1), channel_id=1, source_target_pairs={{0,4},{5,1},{4,8},{9,5},{8,12},{13,9},{12,14},{15,13},{14,10},{11,... | collective-permute-start | bytes 798728 | tf_op jit(solution)/shard_map/ppermute | solution.py:219
  16.0 7.7 %collective-permute-start.7 = (bf16[1040,128]{1,0:T(8,128)(2,1)S(1)}, bf16[1040,128]{1,0:T(8,128)(2,1)S(1)}, u32[]{:S(2)}, u32[]{:S(2)}) collective-permute-start(bf16[1040,128]{1,0:T(8,128)(2,1)S(1)} %collective-permute-done.3), channel_id=1, source_target_pairs={{0,4},{5,1},{4,8},{9,5},{8,12},{13,9},{12,14},{15,13},{14,10},{11,... | collective-permute-start | bytes 798728 | tf_op jit(solution)/shard_map/ppermute | solution.py:222
  17.5 7.8 %collective-permute-start.4 = (bf16[1040,128]{1,0:T(8,128)(2,1)S(1)}, bf16[1040,128]{1,0:T(8,128)(2,1)S(1)}, u32[]{:S(2)}, u32[]{:S(2)}) collective-permute-start(bf16[1040,128]{1,0:T(8,128)(2,1)S(1)} %collective-permute-done.3), channel_id=1, source_target_pairs={{0,1},{1,0},{2,3},{3,2},{4,5},{5,4},{6,7},{7,6},{8,9},{9,8},{10,11... | collective-permute-start | bytes 798728 | tf_op jit(solution)/shard_map/ppermute | solution.py:223
  20.8 9.3 %collective-permute-start.6 = (bf16[1040,128]{1,0:T(8,128)(2,1)S(1)}, bf16[1040,128]{1,0:T(8,128)(2,1)S(1)}, u32[]{:S(2)}, u32[]{:S(2)}) collective-permute-start(bf16[1040,128]{1,0:T(8,128)(2,1)S(1)} %collective-permute-done.5), channel_id=1, source_target_pairs={{0,1},{1,0},{2,3},{3,2},{4,5},{5,4},{6,7},{7,6},{8,9},{9,8},{10,11... | collective-permute-start | bytes 798728 | tf_op jit(solution)/shard_map/ppermute | solution.py:220
  20.8 6.4 %collective-permute-start.9 = (bf16[1040,128]{1,0:T(8,128)(2,1)S(1)}, bf16[1040,128]{1,0:T(8,128)(2,1)S(1)}, u32[]{:S(2)}, u32[]{:S(2)}) collective-permute-start(bf16[1040,128]{1,0:T(8,128)(2,1)S(1)} %collective-permute-done.5), channel_id=1, source_target_pairs={{0,4},{5,1},{4,8},{9,5},{8,12},{13,9},{12,14},{15,13},{14,10},{11,... | collective-permute-start | bytes 798728 | tf_op jit(solution)/shard_map/ppermute | solution.py:219
  23.7 6.5 %collective-permute-start.8 = (bf16[1040,128]{1,0:T(8,128)(2,1)S(1)}, bf16[1040,128]{1,0:T(8,128)(2,1)S(1)}, u32[]{:S(2)}, u32[]{:S(2)}) collective-permute-start(bf16[1040,128]{1,0:T(8,128)(2,1)S(1)} %collective-permute-done.7), channel_id=1, source_target_pairs={{0,1},{1,0},{2,3},{3,2},{4,5},{5,4},{6,7},{7,6},{8,9},{9,8},{10,11... | collective-permute-start | bytes 798728 | tf_op jit(solution)/shard_map/ppermute | solution.py:223
  23.7 6.4 %collective-permute-start.11 = (bf16[1040,128]{1,0:T(8,128)(2,1)S(1)}, bf16[1040,128]{1,0:T(8,128)(2,1)S(1)}, u32[]{:S(2)}, u32[]{:S(2)}) collective-permute-start(bf16[1040,128]{1,0:T(8,128)(2,1)S(1)} %collective-permute-done.7), channel_id=1, source_target_pairs={{0,4},{5,1},{4,8},{9,5},{8,12},{13,9},{12,14},{15,13},{14,10},{11,... | collective-permute-start | bytes 798728 | tf_op jit(solution)/shard_map/ppermute | solution.py:222
  27.2 6.4 %collective-permute-start.10 = (bf16[1040,128]{1,0:T(8,128)(2,1)S(1)}, bf16[1040,128]{1,0:T(8,128)(2,1)S(1)}, u32[]{:S(2)}, u32[]{:S(2)}) collective-permute-start(bf16[1040,128]{1,0:T(8,128)(2,1)S(1)} %collective-permute-done.9), channel_id=1, source_target_pairs={{0,1},{1,0},{2,3},{3,2},{4,5},{5,4},{6,7},{7,6},{8,9},{9,8},{10,11... | collective-permute-start | bytes 798728 | tf_op jit(solution)/shard_map/ppermute | solution.py:220
  27.2 6.4 %collective-permute-start.13 = (bf16[1040,128]{1,0:T(8,128)(2,1)S(1)}, bf16[1040,128]{1,0:T(8,128)(2,1)S(1)}, u32[]{:S(2)}, u32[]{:S(2)}) collective-permute-start(bf16[1040,128]{1,0:T(8,128)(2,1)S(1)} %collective-permute-done.9), channel_id=1, source_target_pairs={{0,4},{5,1},{4,8},{9,5},{8,12},{13,9},{12,14},{15,13},{14,10},{11,... | collective-permute-start | bytes 798728 | tf_op jit(solution)/shard_map/ppermute | solution.py:219
  30.1 3.7 %collective-permute-start.12 = (bf16[1040,128]{1,0:T(8,128)(2,1)S(1)}, bf16[1040,128]{1,0:T(8,128)(2,1)S(1)}, u32[]{:S(2)}, u32[]{:S(2)}) collective-permute-start(bf16[1040,128]{1,0:T(8,128)(2,1)S(1)} %collective-permute-done.11), channel_id=1, source_target_pairs={{0,1},{1,0},{2,3},{3,2},{4,5},{5,4},{6,7},{7,6},{8,9},{9,8},{10,11... | collective-permute-start | bytes 798728 | tf_op jit(solution)/shard_map/ppermute | solution.py:223
  33.7 1.5 %collective-permute-start.14 = (bf16[1040,128]{1,0:T(8,128)(2,1)S(1)}, bf16[1040,128]{1,0:T(8,128)(2,1)S(1)}, u32[]{:S(2)}, u32[]{:S(2)}) collective-permute-start(bf16[1040,128]{1,0:T(8,128)(2,1)S(1)} %collective-permute-done.13), channel_id=1, source_target_pairs={{0,1},{1,0},{2,3},{3,2},{4,5},{5,4},{6,7},{7,6},{8,9},{9,8},{10,11... | collective-permute-start | bytes 798728 | tf_op jit(solution)/shard_map/ppermute | solution.py:220
  42.7 1.6 %collective-permute-start.15 = (bf16[1040,128]{1,0:T(8,128)(2,1)S(1)}, bf16[1040,128]{1,0:T(8,128)(2,1)S(1)}, u32[]{:S(2)}, u32[]{:S(2)}) collective-permute-start(bf16[1040,128]{1,0:T(8,128)(2,1)S(1)} %get-tuple-element.24), channel_id=1, source_target_pairs={{0,1},{1,0},{2,3},{3,2},{4,5},{5,4},{6,7},{7,6},{8,9},{9,8},{10,11... | collective-permute-start | bytes 798728 | tf_op jit(solution)/shard_map/ppermute | solution.py:215
  44.3 6.4 %collective-permute-start.16 = (bf16[1040,128]{1,0:T(8,128)(2,1)S(1)}, bf16[1040,128]{1,0:T(8,128)(2,1)S(1)}, u32[]{:S(2)}, u32[]{:S(2)}) collective-permute-start(bf16[1040,128]{1,0:T(8,128)(2,1)S(1)} %get-tuple-element.24), channel_id=1, source_target_pairs={{0,4},{5,1},{4,8},{9,5},{8,12},{13,9},{12,14},{15,13},{14,10},{11,... | collective-permute-start | bytes 798728 | tf_op jit(solution)/shard_map/ppermute | solution.py:219
  45.8 7.7 %collective-permute-start.18 = (bf16[1040,128]{1,0:T(8,128)(2,1)S(1)}, bf16[1040,128]{1,0:T(8,128)(2,1)S(1)}, u32[]{:S(2)}, u32[]{:S(2)}) collective-permute-start(bf16[1040,128]{1,0:T(8,128)(2,1)S(1)} %collective-permute-done.15), channel_id=1, source_target_pairs={{0,4},{5,1},{4,8},{9,5},{8,12},{13,9},{12,14},{15,13},{14,10},{11,... | collective-permute-start | bytes 798728 | tf_op jit(solution)/shard_map/ppermute | solution.py:222
  50.7 9.3 %collective-permute-start.17 = (bf16[1040,128]{1,0:T(8,128)(2,1)S(1)}, bf16[1040,128]{1,0:T(8,128)(2,1)S(1)}, u32[]{:S(2)}, u32[]{:S(2)}) collective-permute-start(bf16[1040,128]{1,0:T(8,128)(2,1)S(1)} %collective-permute-done.16), channel_id=1, source_target_pairs={{0,1},{1,0},{2,3},{3,2},{4,5},{5,4},{6,7},{7,6},{8,9},{9,8},{10,11... | collective-permute-start | bytes 798728 | tf_op jit(solution)/shard_map/ppermute | solution.py:220
  50.7 6.4 %collective-permute-start.20 = (bf16[1040,128]{1,0:T(8,128)(2,1)S(1)}, bf16[1040,128]{1,0:T(8,128)(2,1)S(1)}, u32[]{:S(2)}, u32[]{:S(2)}) collective-permute-start(bf16[1040,128]{1,0:T(8,128)(2,1)S(1)} %collective-permute-done.16), channel_id=1, source_target_pairs={{0,4},{5,1},{4,8},{9,5},{8,12},{13,9},{12,14},{15,13},{14,10},{11,... | collective-permute-start | bytes 798728 | tf_op jit(solution)/shard_map/ppermute | solution.py:219
  53.5 6.4 %collective-permute-start.22 = (bf16[1040,128]{1,0:T(8,128)(2,1)S(1)}, bf16[1040,128]{1,0:T(8,128)(2,1)S(1)}, u32[]{:S(2)}, u32[]{:S(2)}) collective-permute-start(bf16[1040,128]{1,0:T(8,128)(2,1)S(1)} %collective-permute-done.18), channel_id=1, source_target_pairs={{0,4},{5,1},{4,8},{9,5},{8,12},{13,9},{12,14},{15,13},{14,10},{11,... | collective-permute-start | bytes 798728 | tf_op jit(solution)/shard_map/ppermute | solution.py:222
  55.1 6.5 %collective-permute-start.19 = (bf16[1040,128]{1,0:T(8,128)(2,1)S(1)}, bf16[1040,128]{1,0:T(8,128)(2,1)S(1)}, u32[]{:S(2)}, u32[]{:S(2)}) collective-permute-start(bf16[1040,128]{1,0:T(8,128)(2,1)S(1)} %collective-permute-done.18), channel_id=1, source_target_pairs={{0,1},{1,0},{2,3},{3,2},{4,5},{5,4},{6,7},{7,6},{8,9},{9,8},{10,11... | collective-permute-start | bytes 798728 | tf_op jit(solution)/shard_map/ppermute | solution.py:223
  57.1 9.3 %collective-permute-start.21 = (bf16[1040,128]{1,0:T(8,128)(2,1)S(1)}, bf16[1040,128]{1,0:T(8,128)(2,1)S(1)}, u32[]{:S(2)}, u32[]{:S(2)}) collective-permute-start(bf16[1040,128]{1,0:T(8,128)(2,1)S(1)} %collective-permute-done.20), channel_id=1, source_target_pairs={{0,1},{1,0},{2,3},{3,2},{4,5},{5,4},{6,7},{7,6},{8,9},{9,8},{10,11... | collective-permute-start | bytes 798728 | tf_op jit(solution)/shard_map/ppermute | solution.py:220
  57.1 6.4 %collective-permute-start.24 = (bf16[1040,128]{1,0:T(8,128)(2,1)S(1)}, bf16[1040,128]{1,0:T(8,128)(2,1)S(1)}, u32[]{:S(2)}, u32[]{:S(2)}) collective-permute-start(bf16[1040,128]{1,0:T(8,128)(2,1)S(1)} %collective-permute-done.20), channel_id=1, source_target_pairs={{0,4},{5,1},{4,8},{9,5},{8,12},{13,9},{12,14},{15,13},{14,10},{11,... | collective-permute-start | bytes 798728 | tf_op jit(solution)/shard_map/ppermute | solution.py:219
  60.0 6.5 %collective-permute-start.23 = (bf16[1040,128]{1,0:T(8,128)(2,1)S(1)}, bf16[1040,128]{1,0:T(8,128)(2,1)S(1)}, u32[]{:S(2)}, u32[]{:S(2)}) collective-permute-start(bf16[1040,128]{1,0:T(8,128)(2,1)S(1)} %collective-permute-done.22), channel_id=1, source_target_pairs={{0,1},{1,0},{2,3},{3,2},{4,5},{5,4},{6,7},{7,6},{8,9},{9,8},{10,11... | collective-permute-start | bytes 798728 | tf_op jit(solution)/shard_map/ppermute | solution.py:223
  60.0 6.4 %collective-permute-start.26 = (bf16[1040,128]{1,0:T(8,128)(2,1)S(1)}, bf16[1040,128]{1,0:T(8,128)(2,1)S(1)}, u32[]{:S(2)}, u32[]{:S(2)}) collective-permute-start(bf16[1040,128]{1,0:T(8,128)(2,1)S(1)} %collective-permute-done.22), channel_id=1, source_target_pairs={{0,4},{5,1},{4,8},{9,5},{8,12},{13,9},{12,14},{15,13},{14,10},{11,... | collective-permute-start | bytes 798728 | tf_op jit(solution)/shard_map/ppermute | solution.py:222
  63.5 6.4 %collective-permute-start.25 = (bf16[1040,128]{1,0:T(8,128)(2,1)S(1)}, bf16[1040,128]{1,0:T(8,128)(2,1)S(1)}, u32[]{:S(2)}, u32[]{:S(2)}) collective-permute-start(bf16[1040,128]{1,0:T(8,128)(2,1)S(1)} %collective-permute-done.24), channel_id=1, source_target_pairs={{0,1},{1,0},{2,3},{3,2},{4,5},{5,4},{6,7},{7,6},{8,9},{9,8},{10,11... | collective-permute-start | bytes 798728 | tf_op jit(solution)/shard_map/ppermute | solution.py:220
  63.5 6.4 %collective-permute-start.28 = (bf16[1040,128]{1,0:T(8,128)(2,1)S(1)}, bf16[1040,128]{1,0:T(8,128)(2,1)S(1)}, u32[]{:S(2)}, u32[]{:S(2)}) collective-permute-start(bf16[1040,128]{1,0:T(8,128)(2,1)S(1)} %collective-permute-done.24), channel_id=1, source_target_pairs={{0,4},{5,1},{4,8},{9,5},{8,12},{13,9},{12,14},{15,13},{14,10},{11,... | collective-permute-start | bytes 798728 | tf_op jit(solution)/shard_map/ppermute | solution.py:219
  66.4 3.7 %collective-permute-start.27 = (bf16[1040,128]{1,0:T(8,128)(2,1)S(1)}, bf16[1040,128]{1,0:T(8,128)(2,1)S(1)}, u32[]{:S(2)}, u32[]{:S(2)}) collective-permute-start(bf16[1040,128]{1,0:T(8,128)(2,1)S(1)} %collective-permute-done.26), channel_id=1, source_target_pairs={{0,1},{1,0},{2,3},{3,2},{4,5},{5,4},{6,7},{7,6},{8,9},{9,8},{10,11... | collective-permute-start | bytes 798728 | tf_op jit(solution)/shard_map/ppermute | solution.py:223
  69.9 1.5 %collective-permute-start.29 = (bf16[1040,128]{1,0:T(8,128)(2,1)S(1)}, bf16[1040,128]{1,0:T(8,128)(2,1)S(1)}, u32[]{:S(2)}, u32[]{:S(2)}) collective-permute-start(bf16[1040,128]{1,0:T(8,128)(2,1)S(1)} %collective-permute-done.28), channel_id=1, source_target_pairs={{0,1},{1,0},{2,3},{3,2},{4,5},{5,4},{6,7},{7,6},{8,9},{9,8},{10,11... | collective-permute-start | bytes 798728 | tf_op jit(solution)/shard_map/ppermute | solution.py:220
  79.0 1.6 %collective-permute-start.30 = (bf16[1040,128]{1,0:T(8,128)(2,1)S(1)}, bf16[1040,128]{1,0:T(8,128)(2,1)S(1)}, u32[]{:S(2)}, u32[]{:S(2)}) collective-permute-start(bf16[1040,128]{1,0:T(8,128)(2,1)S(1)} %get-tuple-element.29), channel_id=1, source_target_pairs={{0,1},{1,0},{2,3},{3,2},{4,5},{5,4},{6,7},{7,6},{8,9},{9,8},{10,11... | collective-permute-start | bytes 798728 | tf_op jit(solution)/shard_map/ppermute | solution.py:215
  80.6 6.4 %collective-permute-start.31 = (bf16[1040,128]{1,0:T(8,128)(2,1)S(1)}, bf16[1040,128]{1,0:T(8,128)(2,1)S(1)}, u32[]{:S(2)}, u32[]{:S(2)}) collective-permute-start(bf16[1040,128]{1,0:T(8,128)(2,1)S(1)} %get-tuple-element.29), channel_id=1, source_target_pairs={{0,4},{5,1},{4,8},{9,5},{8,12},{13,9},{12,14},{15,13},{14,10},{11,... | collective-permute-start | bytes 798728 | tf_op jit(solution)/shard_map/ppermute | solution.py:219
  82.1 7.7 %collective-permute-start.33 = (bf16[1040,128]{1,0:T(8,128)(2,1)S(1)}, bf16[1040,128]{1,0:T(8,128)(2,1)S(1)}, u32[]{:S(2)}, u32[]{:S(2)}) collective-permute-start(bf16[1040,128]{1,0:T(8,128)(2,1)S(1)} %collective-permute-done.30), channel_id=1, source_target_pairs={{0,4},{5,1},{4,8},{9,5},{8,12},{13,9},{12,14},{15,13},{14,10},{11,... | collective-permute-start | bytes 798728 | tf_op jit(solution)/shard_map/ppermute | solution.py:222
  87.0 9.3 %collective-permute-start.32 = (bf16[1040,128]{1,0:T(8,128)(2,1)S(1)}, bf16[1040,128]{1,0:T(8,128)(2,1)S(1)}, u32[]{:S(2)}, u32[]{:S(2)}) collective-permute-start(bf16[1040,128]{1,0:T(8,128)(2,1)S(1)} %collective-permute-done.31), channel_id=1, source_target_pairs={{0,1},{1,0},{2,3},{3,2},{4,5},{5,4},{6,7},{7,6},{8,9},{9,8},{10,11... | collective-permute-start | bytes 798728 | tf_op jit(solution)/shard_map/ppermute | solution.py:220
  87.0 6.4 %collective-permute-start.35 = (bf16[1040,128]{1,0:T(8,128)(2,1)S(1)}, bf16[1040,128]{1,0:T(8,128)(2,1)S(1)}, u32[]{:S(2)}, u32[]{:S(2)}) collective-permute-start(bf16[1040,128]{1,0:T(8,128)(2,1)S(1)} %collective-permute-done.31), channel_id=1, source_target_pairs={{0,4},{5,1},{4,8},{9,5},{8,12},{13,9},{12,14},{15,13},{14,10},{11,... | collective-permute-start | bytes 798728 | tf_op jit(solution)/shard_map/ppermute | solution.py:219
  89.8 6.4 %collective-permute-start.37 = (bf16[1040,128]{1,0:T(8,128)(2,1)S(1)}, bf16[1040,128]{1,0:T(8,128)(2,1)S(1)}, u32[]{:S(2)}, u32[]{:S(2)}) collective-permute-start(bf16[1040,128]{1,0:T(8,128)(2,1)S(1)} %collective-permute-done.33), channel_id=1, source_target_pairs={{0,4},{5,1},{4,8},{9,5},{8,12},{13,9},{12,14},{15,13},{14,10},{11,... | collective-permute-start | bytes 798728 | tf_op jit(solution)/shard_map/ppermute | solution.py:222
  91.4 6.5 %collective-permute-start.34 = (bf16[1040,128]{1,0:T(8,128)(2,1)S(1)}, bf16[1040,128]{1,0:T(8,128)(2,1)S(1)}, u32[]{:S(2)}, u32[]{:S(2)}) collective-permute-start(bf16[1040,128]{1,0:T(8,128)(2,1)S(1)} %collective-permute-done.33), channel_id=1, source_target_pairs={{0,1},{1,0},{2,3},{3,2},{4,5},{5,4},{6,7},{7,6},{8,9},{9,8},{10,11... | collective-permute-start | bytes 798728 | tf_op jit(solution)/shard_map/ppermute | solution.py:223
  93.4 9.3 %collective-permute-start.36 = (bf16[1040,128]{1,0:T(8,128)(2,1)S(1)}, bf16[1040,128]{1,0:T(8,128)(2,1)S(1)}, u32[]{:S(2)}, u32[]{:S(2)}) collective-permute-start(bf16[1040,128]{1,0:T(8,128)(2,1)S(1)} %collective-permute-done.35), channel_id=1, source_target_pairs={{0,1},{1,0},{2,3},{3,2},{4,5},{5,4},{6,7},{7,6},{8,9},{9,8},{10,11... | collective-permute-start | bytes 798728 | tf_op jit(solution)/shard_map/ppermute | solution.py:220
  93.4 6.4 %collective-permute-start.39 = (bf16[1040,128]{1,0:T(8,128)(2,1)S(1)}, bf16[1040,128]{1,0:T(8,128)(2,1)S(1)}, u32[]{:S(2)}, u32[]{:S(2)}) collective-permute-start(bf16[1040,128]{1,0:T(8,128)(2,1)S(1)} %collective-permute-done.35), channel_id=1, source_target_pairs={{0,4},{5,1},{4,8},{9,5},{8,12},{13,9},{12,14},{15,13},{14,10},{11,... | collective-permute-start | bytes 798728 | tf_op jit(solution)/shard_map/ppermute | solution.py:219
  96.3 6.5 %collective-permute-start.38 = (bf16[1040,128]{1,0:T(8,128)(2,1)S(1)}, bf16[1040,128]{1,0:T(8,128)(2,1)S(1)}, u32[]{:S(2)}, u32[]{:S(2)}) collective-permute-start(bf16[1040,128]{1,0:T(8,128)(2,1)S(1)} %collective-permute-done.37), channel_id=1, source_target_pairs={{0,1},{1,0},{2,3},{3,2},{4,5},{5,4},{6,7},{7,6},{8,9},{9,8},{10,11... | collective-permute-start | bytes 798728 | tf_op jit(solution)/shard_map/ppermute | solution.py:223
  96.3 6.4 %collective-permute-start.41 = (bf16[1040,128]{1,0:T(8,128)(2,1)S(1)}, bf16[1040,128]{1,0:T(8,128)(2,1)S(1)}, u32[]{:S(2)}, u32[]{:S(2)}) collective-permute-start(bf16[1040,128]{1,0:T(8,128)(2,1)S(1)} %collective-permute-done.37), channel_id=1, source_target_pairs={{0,4},{5,1},{4,8},{9,5},{8,12},{13,9},{12,14},{15,13},{14,10},{11,... | collective-permute-start | bytes 798728 | tf_op jit(solution)/shard_map/ppermute | solution.py:222
  99.8 6.4 %collective-permute-start.40 = (bf16[1040,128]{1,0:T(8,128)(2,1)S(1)}, bf16[1040,128]{1,0:T(8,128)(2,1)S(1)}, u32[]{:S(2)}, u32[]{:S(2)}) collective-permute-start(bf16[1040,128]{1,0:T(8,128)(2,1)S(1)} %collective-permute-done.39), channel_id=1, source_target_pairs={{0,1},{1,0},{2,3},{3,2},{4,5},{5,4},{6,7},{7,6},{8,9},{9,8},{10,11... | collective-permute-start | bytes 798728 | tf_op jit(solution)/shard_map/ppermute | solution.py:220
  99.8 6.4 %collective-permute-start.43 = (bf16[1040,128]{1,0:T(8,128)(2,1)S(1)}, bf16[1040,128]{1,0:T(8,128)(2,1)S(1)}, u32[]{:S(2)}, u32[]{:S(2)}) collective-permute-start(bf16[1040,128]{1,0:T(8,128)(2,1)S(1)} %collective-permute-done.39), channel_id=1, source_target_pairs={{0,4},{5,1},{4,8},{9,5},{8,12},{13,9},{12,14},{15,13},{14,10},{11,... | collective-permute-start | bytes 798728 | tf_op jit(solution)/shard_map/ppermute | solution.py:219
  102.7 3.7 %collective-permute-start.42 = (bf16[1040,128]{1,0:T(8,128)(2,1)S(1)}, bf16[1040,128]{1,0:T(8,128)(2,1)S(1)}, u32[]{:S(2)}, u32[]{:S(2)}) collective-permute-start(bf16[1040,128]{1,0:T(8,128)(2,1)S(1)} %collective-permute-done.41), channel_id=1, source_target_pairs={{0,1},{1,0},{2,3},{3,2},{4,5},{5,4},{6,7},{7,6},{8,9},{9,8},{10,11... | collective-permute-start | bytes 798728 | tf_op jit(solution)/shard_map/ppermute | solution.py:223
  106.2 1.5 %collective-permute-start.44 = (bf16[1040,128]{1,0:T(8,128)(2,1)S(1)}, bf16[1040,128]{1,0:T(8,128)(2,1)S(1)}, u32[]{:S(2)}, u32[]{:S(2)}) collective-permute-start(bf16[1040,128]{1,0:T(8,128)(2,1)S(1)} %collective-permute-done.43), channel_id=1, source_target_pairs={{0,1},{1,0},{2,3},{3,2},{4,5},{5,4},{6,7},{7,6},{8,9},{9,8},{10,11... | collective-permute-start | bytes 798728 | tf_op jit(solution)/shard_map/ppermute | solution.py:220
  117.3 3.6 %collective-permute-start.46 = (f32[8,128]{1,0:T(8,128)S(1)}, f32[8,128]{1,0:T(8,128)S(1)}, u32[]{:S(2)}, u32[]{:S(2)}) collective-permute-start(f32[8,128]{1,0:T(8,128)S(1)} %add.160), channel_id=1, source_target_pairs={{0,2},{1,3},{2,0},{3,1},{4,6},{5,7},{6,4},{7,5},{8,10},{9,11},{10,... | collective-permute-start | bytes 12296 | tf_op jit(solution)/shard_map/ppermute | solution.py:295
  120.9 3.6 %collective-permute-start.47 = (f32[8,128]{1,0:T(8,128)S(1)}, f32[8,128]{1,0:T(8,128)S(1)}, u32[]{:S(2)}, u32[]{:S(2)}) collective-permute-start(f32[8,128]{1,0:T(8,128)S(1)} %add.161), channel_id=1, source_target_pairs={{0,4},{1,5},{2,6},{3,7},{4,0},{5,1},{6,2},{7,3},{8,12},{9,13},{10,... | collective-permute-start | bytes 12296 | tf_op jit(solution)/shard_map/ppermute | solution.py:295
  124.5 4.5 %collective-permute-start.48 = (f32[8,128]{1,0:T(8,128)S(1)}, f32[8,128]{1,0:T(8,128)S(1)}, u32[]{:S(2)}, u32[]{:S(2)}) collective-permute-start(f32[8,128]{1,0:T(8,128)S(1)} %add.162), channel_id=1, source_target_pairs={{0,8},{1,9},{2,10},{3,11},{4,12},{5,13},{6,14},{7,15},{8,0},{9,1},... | collective-permute-start | bytes 12296 | tf_op jit(solution)/shard_map/ppermute | solution.py:295
  (6 other events, 30.1 us)

commit v3 on v2

--- a/solution.py
+++ b/solution.py
@@ -11,6 +11,7 @@
 f32 = jnp.float32
 bf16 = jnp.bfloat16
 STAT_ROWS = 16
+LOADS = 4
 
 
 def row(value):
@@ -41,53 +42,98 @@
     piece_ref[rows:, :] = split_rows([lane_sums(wide * wide)])
 
 
-def load_kernel(env_ref, right_ref, env_out, right_out, sems):
-    parts = 8
-    step = env_ref.shape[0] // parts
-    copies = [
-        pltpu.make_async_copy(
-            env_ref.at[pl.ds(j * step, step)], env_out.at[pl.ds(j * step, step)], sems.at[j]
-        )
-        for j in range(parts)
-    ]
-    copies.append(pltpu.make_async_copy(right_ref, right_out, sems.at[parts]))
+def prepare_kernel(sizes, phases, phase_ref, offset_ref, env_ref, *rest):
+    count_ref, list_ref, env_out, sems = rest
+    tile_dev, shifts, group, tile_rows, total = sizes
+    records = tile_dev * shifts
+    step = env_ref.shape[0] // LOADS
+    copies = []
+    for j in range(LOADS):
+        rows = pl.ds(j * step, step)
+        copies.append(pltpu.make_async_copy(env_ref.at[rows], env_out.at[rows], sems.at[j]))
     for copy in copies:
         copy.start()
+    for p in range(phases):
+        count_ref[p] = 0
+
+    def one_tile(tile, carry):
+        for shift in range(shifts):
+            r = tile * shifts + shift
+            p = phase_ref[r]
+            n = count_ref[p]
+            list_ref[0, p * records + n] = offset_ref[r]
+            list_ref[1, p * records + n] = r * group * tile_rows
+            list_ref[2, p * records + n] = (shift * tile_dev + tile) * tile_rows
+            count_ref[p] = n + 1
+        return carry
+
+    lax.fori_loop(0, tile_dev, one_tile, 0)
     for copy in copies:
         copy.wait()
 
 
-def apply_kernel(stage, sizes, tile_ref, stat_ref, buf_ref, env_ref, right_ref, w_ref, *rest):
+def contract_left(phase, unroll, sizes, count_ref, list_ref, buf_ref, env_ref, left_ref):
     tile_dev, shifts, group, tile_rows, total = sizes
-    prior = rest[: stage - 1]
-    rest = rest[stage - 1 :]
+    base = phase * tile_dev * shifts
+    width = group * tile_rows
+    count = count_ref[phase]
+
+    def one(n):
+        offset = pl.multiple_of(list_ref[0, n], 16)
+        start = pl.multiple_of(list_ref[1, n], 128)
+        target = pl.multiple_of(list_ref[2, n], 128)
+        picked = buf_ref[pl.ds(offset, tile_rows), :]
+        for t in range(group):
+            left_ref[pl.ds(target, tile_rows), t * 128 : (t + 1) * 128] = jnp.dot(
+                env_ref[pl.ds(start + t * tile_rows, tile_rows), :],
+                picked,
+                preferred_element_type=f32,
+            ).astype(bf16)
+
+    def many(j, carry):
+        for q in range(unroll):
+            one(base + j * unroll + q)
+        return carry
+
+    def few(j, carry):
+        for q in range(4):
+            one(base + jnp.minimum(whole * unroll + j * 4 + q, count - 1))
+        return carry
+
+    whole = count // unroll
+    lax.fori_loop(0, whole, many, 0)
+    lax.fori_loop(0, (count - whole * unroll + 3) // 4, few, 0)
+
+
+def left_kernel(phase, unroll, sizes, count_ref, list_ref, buf_ref, env_ref, *rest):
+    contract_left(phase, unroll, sizes, count_ref, list_ref, buf_ref, env_ref, rest[-1])
+
+
+def apply_kernel(stage, sizes, slots, stat_ref, right_ref, w_ref, *rest):
+    tile_dev, shifts, group, tile_rows, total = sizes
+    rows = tile_dev * tile_rows
+    phases = max(p for p, _ in slots) + 1
+    bufs, rest = rest[:phases], rest[phases:]
+    prior, rest = rest[: stage - 1], rest[stage - 1 :]
     if stage > 1:
         coef_in, rest = rest[0], rest[1:]
-    image_ref, coef_ref, send_ref, left_ref = rest
+    left_ref, image_ref, coef_ref, send_ref, all_stats = rest
+
     width = group * tile_rows
-
-    def one_tile(i, carry):
-        for k in range(shifts):
-            offset = pl.multiple_of(tile_ref[i * shifts + k], 16)
-            picked = buf_ref[pl.ds(offset, tile_rows), :]
-            start = pl.multiple_of((i * shifts + k) * width, width)
-            product = jnp.dot(
-                env_ref[pl.ds(start, width), :], picked, preferred_element_type=f32
-            ).astype(bf16)
-            for t in range(group):
-                left_ref[
-                    pl.ds(pl.multiple_of(i * tile_rows, tile_rows), tile_rows),
-                    (k * group + t) * 128 : (k * group + t + 1) * 128,
-                ] = product[t * tile_rows : (t + 1) * tile_rows]
-        return carry
-
-    lax.fori_loop(0, tile_dev, one_tile, 0)
-    applied = jnp.dot(left_ref[...], right_ref[...], preferred_element_type=f32)
-
+    applied = jnp.zeros((rows, 128), f32)
+    for k in range(shifts):
+        applied = applied + jnp.dot(
+            left_ref[k * rows : (k + 1) * rows, :],
+            right_ref[k * width : (k + 1) * width, :],
+            preferred_element_type=f32,
+        )
+
+    for n, (p, offset) in enumerate(slots):
+        all_stats[n * STAT_ROWS : (n + 1) * STAT_ROWS, :] = bufs[p][offset : offset + STAT_ROWS, :]
     gathered = jnp.zeros((STAT_ROWS, 128), f32)
     for d in range(stat_ref.shape[0]):
         offset = pl.multiple_of(stat_ref[d], 16)
-        gathered = gathered + buf_ref[pl.ds(offset, STAT_ROWS), :].astype(f32)
+        gathered = gathered + all_stats[pl.ds(offset, STAT_ROWS), :].astype(f32)
 
     def mean_of(j):
         lanes = gathered[3 * j : 3 * j + 1] + gathered[3 * j + 1 : 3 * j + 2]
@@ -195,33 +241,65 @@
         core = own % 2
         here = ring_place(own // 2, chips)
 
-        def slot_of(device):
+        half = chips // 2
+        groups = [[(0, 0, 0), (0, 0, 1)]]
+        for step in range(1, half):
+            groups += [[(step, shard, 0), (step, shard, 1)] for shard in (0, 1)]
+        groups += [[(half, 0, 0), (half, 0, 1)]]
+        slots = [
+            (p, j * piece_rows + rows) for p, group in enumerate(groups) for j in range(len(group))
+        ]
+        firsts = [sum(len(group) for group in groups[:p]) for p in range(1, len(groups))]
+        codes = [(4 * step + 2 * shard + swap) for group in groups for step, shard, swap in group]
+
+        def code_of(device):
             ahead = (here - ring_place(device // 2, chips)) % chips
             steps = jnp.where(core == 0, ahead, (chips - ahead) % chips)
             other = (device + core) % 2
-            half = chips // 2
-            last = 2 + 4 * (half - 1)
-            direct = 2 + 4 * (steps - 1) + 2 * other
-            passed = 2 + 4 * (chips - steps - 1) + 3 - 2 * other
-            slot = jnp.where(steps < half, direct, passed)
-            slot = jnp.where(steps == half, last + other, slot)
-            return jnp.where(steps == 0, other, slot)
-
-        tile_offset = slot_of(source) * piece_rows + local * tile_rows
-        stat_offset = slot_of(devices) * piece_rows + rows
-
-        def exchange(piece):
-            first, second = lax.optimization_barrier(
-                (piece, lax.ppermute(piece, "sector", sibling))
-            )
-            parts = [first, second]
-            for step in range(1, chips // 2 + 1):
-                first = lax.ppermute(first, "sector", onward)
-                parts += [first, lax.ppermute(first, "sector", sibling)]
-                if 2 * step < chips:
-                    second = lax.ppermute(second, "sector", onward)
-                    parts += [second, lax.ppermute(second, "sector", sibling)]
-            return jnp.concatenate(parts, axis=0)
+            direct = 4 * steps + 2 * other
+            swapped = 4 * (chips - steps) + 2 * (1 - other) + 1
+            code = jnp.where(steps < half, direct, swapped)
+            code = jnp.where(steps == half, 4 * half + other, code)
+            return jnp.where(steps == 0, other, code)
+
+        def slot_of(device):
+            same = code_of(device)[:, None] == jnp.array(codes, jnp.int32)[None, :]
+            return jnp.sum(same * jnp.arange(len(codes), dtype=jnp.int32), axis=1)
+
+        record_slot = slot_of(source)
+        phase = sum((record_slot >= slot).astype(jnp.int32) for slot in firsts)
+        first_slot = sum((phase == p + 1) * slot for p, slot in enumerate(firsts))
+        offset = (record_slot - first_slot) * piece_rows + local * tile_rows
+        stat_offset = slot_of(devices) * STAT_ROWS
+
+        def swap_cores(x):
+            return lax.ppermute(x, "sector", sibling)
+
+        def step_on(x):
+            return lax.ppermute(x, "sector", onward)
+
+        def exchange(piece, contract, prepare, late=False):
+            first, second = lax.optimization_barrier((piece, swap_cores(piece)))
+            pairs = [(first, second)]
+            for step in range(1, half):
+                first = step_on(first)
+                pairs.append((first, swap_cores(first)))
+                second = step_on(second)
+                pairs.append((second, swap_cores(second)))
+            near = prepare(pairs[0][1])
+            first = step_on(first)
+            buffers = [jnp.concatenate(pair, axis=0) for pair in pairs]
+            left = []
+            order = list(range(len(buffers)))
+            if late:
+                order = order[1:3] + order[:1] + order[3:]
+            for p in order:
+                left = [contract(p, buffers[p], near, left)]
+                if p == len(buffers) - 2:
+                    first, left[0] = lax.optimization_barrier((first, left[0]))
+            buffers.append(jnp.concatenate([first, swap_cores(first)], axis=0))
+            left = [contract(len(pairs), buffers[-1], near, left)]
+            return buffers, near, left[0]
 
     else:
         capacity = max(1, 2 * records // peers)
@@ -235,15 +313,19 @@
         chosen = wanted[:, :, None] * (order[:, :, None] == slots).astype(jnp.int32)
         send_index = jnp.sum(chosen * (every % tile_dev)[:, :, None], axis=1).reshape(-1)
         place = jnp.where(is_self, local, tile_dev + source * capacity + rank)
-        tile_offset = place * tile_rows
+        phase = jnp.zeros_like(source)
+        offset = place * tile_rows
+        stat_offset = devices * STAT_ROWS
         stat_base = (tile_dev + peers * capacity) * tile_rows
-        stat_offset = stat_base + devices * STAT_ROWS
-
-        def exchange(piece):
+        slots = [(0, stat_base + d * STAT_ROWS) for d in range(peers)]
+
+        def exchange(piece, contract, prepare, late=False):
             tiles = piece[:rows].reshape(tile_dev, tile_rows, columns)
             incoming = lax.all_to_all(tiles[send_index], "sector", 0, 0, tiled=True)
             stats = lax.all_gather(piece[rows:], "sector", axis=0, tiled=True)
-            return jnp.concatenate([piece[:rows], incoming.reshape(-1, columns), stats], axis=0)
+            buffer = jnp.concatenate([piece[:rows], incoming.reshape(-1, columns), stats], axis=0)
+            near = prepare(piece)
+            return [buffer], near, contract(0, buffer, near, [])
 
     vmem = pl.BlockSpec(memory_space=pltpu.VMEM)
     smem = pl.BlockSpec(memory_space=pltpu.SMEM)
@@ -256,38 +338,68 @@
         out_specs=vmem,
         compiler_params=pltpu.CompilerParams(vmem_limit_bytes=4 * 2**20),
     )(wavefunction)
+    phases = max(p for p, _ in slots) + 1
     env_flat = env_left.reshape(tile_dev * terms * tile_rows, tile_rows)
     right_flat = right_environment_terms.reshape(terms * columns, columns)
-    env_near, right_near = pl.pallas_call(
-        load_kernel,
-        out_shape=(pltpu.VMEM(env_flat.shape, bf16), pltpu.VMEM(right_flat.shape, bf16)),
-        in_specs=[hbm, hbm],
-        out_specs=(vmem, vmem),
-        scratch_shapes=[pltpu.SemaphoreType.DMA((9,))],
-        compiler_params=pltpu.CompilerParams(vmem_limit_bytes=2 * 2**20),
-    )(env_flat, right_flat)
-
-    def apply_operator(stage, buffer, prior, coefs):
+    left_type = pltpu.VMEM((shifts * rows, (terms // shifts) * columns), bf16)
+
+    def prepare(marker):
+        tied = lax.optimization_barrier((phase, offset, env_flat, marker))
+        counts, lists, env_near = pl.pallas_call(
+            functools.partial(prepare_kernel, sizes, phases),
+            out_shape=(
+                jax.ShapeDtypeStruct((phases,), jnp.int32),
+                jax.ShapeDtypeStruct((3, phases * records), jnp.int32),
+                pltpu.VMEM(env_flat.shape, bf16),
+            ),
+            in_specs=[smem, smem, hbm],
+            out_specs=(smem, smem, vmem),
+            scratch_shapes=[pltpu.SemaphoreType.DMA((LOADS,))],
+            compiler_params=pltpu.CompilerParams(vmem_limit_bytes=40 * 2**20),
+        )(*tied[:3])
+        return env_near, right_flat, counts, lists
+
+    def contract(phase, buffer, near, held):
+        env_near, right_near, counts, lists = near
+        return pl.pallas_call(
+            functools.partial(left_kernel, phase, 8 if phase == 0 else 10, sizes),
+            out_shape=left_type,
+            in_specs=[smem, smem] + [vmem] * (2 + len(held)),
+            out_specs=vmem,
+            input_output_aliases={4: 0} if held else {},
+            compiler_params=pltpu.CompilerParams(vmem_limit_bytes=4 * 2**20),
+            cost_estimate=pl.CostEstimate(flops=2**30, bytes_accessed=2**20, transcendentals=0),
+        )(counts, lists, buffer, env_near, *held)
+
+    def apply_operator(stage, buffers, near, held, prior, coefs):
         image = jax.ShapeDtypeStruct((rows, columns), f32)
         small = jax.ShapeDtypeStruct((8, 128), f32)
         send = small if stage == 3 else jax.ShapeDtypeStruct((piece_rows, columns), bf16)
-        operands = [buffer, env_near, right_near, wavefunction, *prior, *coefs]
+        env_near, right_near, counts, lists = near
+        operands = [right_near, wavefunction, *buffers, *prior, *coefs, held]
         return pl.pallas_call(
-            functools.partial(apply_kernel, stage, sizes),
+            functools.partial(apply_kernel, stage, sizes, slots),
             out_shape=(image, small, send),
-            in_specs=[smem, smem] + [vmem] * len(operands),
+            in_specs=[smem] + [vmem] * len(operands),
             out_specs=(vmem, vmem, vmem),
-            scratch_shapes=[pltpu.VMEM((rows, terms * columns), bf16)],
-            compiler_params=pltpu.CompilerParams(vmem_limit_bytes=20 * 2**20),
+            scratch_shapes=[pltpu.VMEM((peers * STAT_ROWS, 128), bf16)],
+            compiler_params=pltpu.CompilerParams(vmem_limit_bytes=12 * 2**20),
             cost_estimate=pl.CostEstimate(
                 flops=4 * rows * terms * tile_rows * columns, bytes_accessed=2**24, transcendentals=0
             ),
-        )(tile_offset, stat_offset, *operands)
-
-    image_one, coefs_one, piece = apply_operator(1, exchange(piece), [], [])
-    image_two, coefs_two, piece = apply_operator(2, exchange(piece), [image_one], [coefs_one])
+        )(stat_offset, *operands)
+
+    buffers, near, held = exchange(piece, contract, prepare, True)
+    image_one, coefs_one, piece = apply_operator(1, buffers, near, held, [], [])
+
+    def prepared(marker):
+        return near
+
+    buffers, _, held = exchange(piece, contract, prepared)
+    image_two, coefs_two, piece = apply_operator(2, buffers, near, held, [image_one], [coefs_one])
+    buffers, _, held = exchange(piece, contract, prepared)
     image_three, coefs_three, stats = apply_operator(
-        3, exchange(piece), [image_one, image_two], [coefs_two]
+        3, buffers, near, held, [image_one, image_two], [coefs_two]
     )
     distance = 1
     while distance < peers:

time: 130 us -> 125 us (0.962)
  Pallas kernels: 24.8 us -> 49 us
  waiting for transfers between devices: 54.8 us -> 35.8 us
  starting transfers between devices: 40.6 us -> 33.6 us
  local copies, waits for them, and re-layouts: 8.2 us -> 3.12 us
  other arithmetic: 0.1 us -> 1.71 us
    pallas_call x4 -> x28, Pallas kernels: 24 us -> 48.2 us  [the longest x24 31.6 us: contract(): pl.pallas_call(functools.partial(left_kernel, phase, 8 if phase == 0 else...]
    ppermute x45, waiting for transfers between devices: 47.1 us -> 28.4 us  [the longest x21 25.7 us: step_on(): return lax.ppermute(x, 'sector', onward)]
    ppermute x45, starting transfers between devices: 35.3 us -> 27.7 us  [the longest x21 25 us: step_on(): return lax.ppermute(x, 'sector', onward)]
    unnamed x55 -> x34, local copies, waits for them, and re-layouts: 7.86 us -> 2.01 us
    reduce_sum x0 -> x2, other arithmetic: none -> 1.59 us  [slot_of(): return jnp.sum(same * jnp.arange(len(codes), dtype=jnp.int32), axis=1)]
  transfers between devices with their start and end apart: 49 -> 49, of which waited for: 29 -> 22; matrix products, arithmetic and copies ran while one was open for 1% -> 3% of each run, Pallas kernels for 1% -> 28%
where the time goes in v3:
time: 125 us
  Pallas kernels  49 us (39%)
  waiting for transfers between devices  35.8 us (29%)
  starting transfers between devices  33.6 us (27%)
  local copies, waits for them, and re-layouts  3.12 us (2%)
  other arithmetic  1.71 us (1%)
  between operations  1.41 us (1%)
    pallas_call x24, Pallas kernels, contract(): pl.pallas_call(functools.partial(left_kernel, phase, 8 if phase == 0 else...  31.6 us
    ppermute x21, waiting for transfers between devices, step_on(): return lax.ppermute(x, 'sector', onward)  25.7 us
    ppermute x21, starting transfers between devices, step_on(): return lax.ppermute(x, 'sector', onward)  25 us
    pallas_call x3, Pallas kernels, apply_operator(): pl.pallas_call(functools.partial(apply_kernel, stage, sizes, slots), out_...  11.2 us
    ppermute x4, waiting for transfers between devices, per_device(): stats = stats + lax.ppermute(stats, 'sector', pairs)  7.33 us
    ppermute x4, starting transfers between devices, per_device(): stats = stats + lax.ppermute(stats, 'sector', pairs)  5.88 us
    pallas_call x1, Pallas kernels, prepare(): pl.pallas_call(functools.partial(prepare_kernel, sizes, phases), out_shap...  5.4 us
    ppermute x24, waiting for transfers between devices, swap_cores(): return lax.ppermute(x, 'sector', sibling)  2.73 us
  transfers between devices with their start and end apart: 49, of which 22 were waited for; matrix products, arithmetic and copies ran while one was open for 3% of the time, Pallas kernels for 28%

profile of v3, /device:TPU:0, one launch (start us, length us, event | category | flops | bytes accessed | tf_op | source)
XLA Modules:
  0.0 124.6 jit_solution(9546392768713537573)
XLA Ops:
  4.3 2.7 %collective-permute-start.1 = (bf16[1040,128]{1,0:T(8,128)(2,1)S(1)}, bf16[1040,128]{1,0:T(8,128)(2,1)S(1)}, u32[]{:S(2)}, u32[]{:S(2)}) collective-permute-start(bf16[1040,128]{1,0:T(8,128)(2,1)S(1)} %shard_map.77), channel_id=1, source_target_pairs={{0,4},{5,1},{4,8},{9,5},{8,12},{13,9},{12,14},{15,13},{14,10},{11,... | collective-permute-start | bytes 798728 | tf_op jit(solution)/shard_map/ppermute | solution.py:279
  6.9 1.6 %collective-permute-start.3 = (bf16[1040,128]{1,0:T(8,128)(2,1)S(1)}, bf16[1040,128]{1,0:T(8,128)(2,1)S(1)}, u32[]{:S(2)}, u32[]{:S(2)}) collective-permute-start(bf16[1040,128]{1,0:T(8,128)(2,1)S(1)} %collective-permute-done), channel_id=1, source_target_pairs={{0,4},{5,1},{4,8},{9,5},{8,12},{13,9},{12,14},{15,13},{14,10},{11,... | collective-permute-start | bytes 798728 | tf_op jit(solution)/shard_map/ppermute | solution.py:279
  8.5 5.4 %shard_map.78 = (s32[8]{0:T(128)S(1)}, s32[3,640]{1,0:T(4,128)S(1)}, bf16[40960,128]{1,0:T(8,128)(2,1)S(1)}) custom-call(s32[80]{0:T(128)S(1)} %get-tuple-element.31.phase_ref, s32[80]{0:T(128)S(1)} %get-tuple-element.32.offset_ref, bf16[40960,128]{1,0:T(8,128)(2,1)} %bitcast.5), custom_call_target="tpu_custom_call" | custom-call | tf_op jit(solution)/shard_map/pallas_call | solution.py:348
  14.0 1.6 %collective-permute-start.5 = (bf16[1040,128]{1,0:T(8,128)(2,1)S(1)}, bf16[1040,128]{1,0:T(8,128)(2,1)S(1)}, u32[]{:S(2)}, u32[]{:S(2)}) collective-permute-start(bf16[1040,128]{1,0:T(8,128)(2,1)S(1)} %collective-permute-done.1), channel_id=1, source_target_pairs={{0,4},{5,1},{4,8},{9,5},{8,12},{13,9},{12,14},{15,13},{14,10},{11,... | collective-permute-start | bytes 798728 | tf_op jit(solution)/shard_map/ppermute | solution.py:279
  15.6 1.5 %collective-permute-start.7 = (bf16[1040,128]{1,0:T(8,128)(2,1)S(1)}, bf16[1040,128]{1,0:T(8,128)(2,1)S(1)}, u32[]{:S(2)}, u32[]{:S(2)}) collective-permute-start(bf16[1040,128]{1,0:T(8,128)(2,1)S(1)} %collective-permute-done.3), channel_id=1, source_target_pairs={{0,4},{5,1},{4,8},{9,5},{8,12},{13,9},{12,14},{15,13},{14,10},{11,... | collective-permute-start | bytes 798728 | tf_op jit(solution)/shard_map/ppermute | solution.py:279
  17.2 3.3 %collective-permute-done.5 = bf16[1040,128]{1,0:T(8,128)(2,1)S(1)} collective-permute-done((bf16[1040,128]{1,0:T(8,128)(2,1)S(1)}, bf16[1040,128]{1,0:T(8,128)(2,1)S(1)}, u32[]{:S(2)}, u32[]{:S(2)}) %collective-permute-start.5) | collective-permute-done | bytes 266272 | tf_op jit(solution)/shard_map/ppermute | solution.py:279
  20.5 1.6 %collective-permute-start.9 = (bf16[1040,128]{1,0:T(8,128)(2,1)S(1)}, bf16[1040,128]{1,0:T(8,128)(2,1)S(1)}, u32[]{:S(2)}, u32[]{:S(2)}) collective-permute-start(bf16[1040,128]{1,0:T(8,128)(2,1)S(1)} %collective-permute-done.5), channel_id=1, source_target_pairs={{0,4},{5,1},{4,8},{9,5},{8,12},{13,9},{12,14},{15,13},{14,10},{11,... | collective-permute-start | bytes 798728 | tf_op jit(solution)/shard_map/ppermute | solution.py:279
  24.7 2.0 %collective-permute-start.11 = (bf16[1040,128]{1,0:T(8,128)(2,1)S(1)}, bf16[1040,128]{1,0:T(8,128)(2,1)S(1)}, u32[]{:S(2)}, u32[]{:S(2)}) collective-permute-start(bf16[1040,128]{1,0:T(8,128)(2,1)S(1)} %collective-permute-done.7), channel_id=1, source_target_pairs={{0,4},{5,1},{4,8},{9,5},{8,12},{13,9},{12,14},{15,13},{14,10},{11,... | collective-permute-start | bytes 798728 | tf_op jit(solution)/shard_map/ppermute | solution.py:279
  26.7 1.9 %shard_map.81.rest_0_ = bf16[10240,512]{1,0:T(8,128)(2,1)S(1)} custom-call(s32[8]{0:T(128)S(1)} %get-tuple-element.34.count_ref, s32[3,640]{1,0:T(4,128)S(1)} %get-tuple-element.35.list_ref, bf16[2080,128]{1,0:T(8,128)(2,1)S(1)} %constant_dynamic-update-slice_fusion.buf_ref.rest_0_, ...), custom_call_target="tpu_custom_call", output_to_operand_aliasing={{}: (4, {})} | custom-call | flops 1073741824 | bytes 1048576 | tf_op jit(solution)/shard_map/pallas_call | solution.py:364
  31.2 1.8 %shard_map.83.rest_0_ = bf16[10240,512]{1,0:T(8,128)(2,1)S(1)} custom-call(s32[8]{0:T(128)S(1)} %get-tuple-element.34.count_ref, s32[3,640]{1,0:T(4,128)S(1)} %get-tuple-element.35.list_ref, bf16[2080,128]{1,0:T(8,128)(2,1)S(1)} %constant_dynamic-update-slice_fusion.8.buf_ref.rest_4_, ...), custom_call_target="tpu_custom_call", output_to_operand_aliasing={{}: (4, {})} | custom-call | flops 1073741824 | bytes 1048576 | tf_op jit(solution)/shard_map/pallas_call | solution.py:364
  33.8 2.6 %collective-permute-done.13 = bf16[1040,128]{1,0:T(8,128)(2,1)S(1)} collective-permute-done((bf16[1040,128]{1,0:T(8,128)(2,1)S(1)}, bf16[1040,128]{1,0:T(8,128)(2,1)S(1)}, u32[]{:S(2)}, u32[]{:S(2)}) %collective-permute-start.13) | collective-permute-done | bytes 266272 | tf_op jit(solution)/shard_map/ppermute | solution.py:279
  36.5 1.5 %shard_map.85.rest_0_ = bf16[10240,512]{1,0:T(8,128)(2,1)S(1)} custom-call(s32[8]{0:T(128)S(1)} %get-tuple-element.34.count_ref, s32[3,640]{1,0:T(4,128)S(1)} %get-tuple-element.35.list_ref, bf16[2080,128]{1,0:T(8,128)(2,1)S(1)} %constant_dynamic-update-slice_fusion.12.buf_ref.rest_6_, ...), custom_call_target="tpu_custom_call", output_to_operand_aliasing={{}: (4, {})} | custom-call | flops 1073741824 | bytes 1048576 | tf_op jit(solution)/shard_map/pallas_call | solution.py:364
  39.5 3.4 %shard_map.87 = (f32[1024,128]{1,0:T(8,128)S(1)}, f32[8,128]{1,0:T(8,128)S(1)}, bf16[1040,128]{1,0:T(8,128)(2,1)S(1)}) custom-call(s32[16]{0:T(128)S(1)} %broadcast_multiply_fusion.stat_ref, bf16[5120,128]{1,0:T(8,128)(2,1)S(1)} %bitcast.2, bf16[1024,128]{1,0:T(8,128)(2,1)S(1)} %copy-done.4, ...), custom_call_target="tpu_custom_call" | custom-call | flops 2684354560 | bytes 16777216 | tf_op jit(solution)/shard_map/pallas_call | solution.py:380
  43.2 1.3 %collective-permute-done.15 = bf16[1040,128]{1,0:T(8,128)(2,1)S(1)} collective-permute-done((bf16[1040,128]{1,0:T(8,128)(2,1)S(1)}, bf16[1040,128]{1,0:T(8,128)(2,1)S(1)}, u32[]{:S(2)}, u32[]{:S(2)}) %collective-permute-start.15) | collective-permute-done | bytes 266272 | tf_op jit(solution)/shard_map/ppermute | solution.py:276
  44.7 1.5 %collective-permute-start.18 = (bf16[1040,128]{1,0:T(8,128)(2,1)S(1)}, bf16[1040,128]{1,0:T(8,128)(2,1)S(1)}, u32[]{:S(2)}, u32[]{:S(2)}) collective-permute-start(bf16[1040,128]{1,0:T(8,128)(2,1)S(1)} %collective-permute-done.15), channel_id=1, source_target_pairs={{0,4},{5,1},{4,8},{9,5},{8,12},{13,9},{12,14},{15,13},{14,10},{11,... | collective-permute-start | bytes 798728 | tf_op jit(solution)/shard_map/ppermute | solution.py:279
  46.3 1.9 %shard_map.88.rest_0_ = bf16[10240,512]{1,0:T(8,128)(2,1)S(1)} custom-call(s32[8]{0:T(128)S(1)} %get-tuple-element.34.count_ref, s32[3,640]{1,0:T(4,128)S(1)} %get-tuple-element.35.list_ref, bf16[2080,128]{1,0:T(8,128)(2,1)S(1)} %constant_dynamic-update-slice_fusion.16.buf_ref.rest_0_, bf16[40960,128]{1,0:T(8,128)(2,1)S(1)} %get-tuple-element.36.env_ref), custom_call_target="tpu_custom_call" | custom-call | flops 1073741824 | bytes 1048576 | tf_op jit(solution)/shard_map/pallas_call | solution.py:364
  48.2 2.8 %collective-permute-done.16 = bf16[1040,128]{1,0:T(8,128)(2,1)S(1)} collective-permute-done((bf16[1040,128]{1,0:T(8,128)(2,1)S(1)}, bf16[1040,128]{1,0:T(8,128)(2,1)S(1)}, u32[]{:S(2)}, u32[]{:S(2)}) %collective-permute-start.16) | collective-permute-done | bytes 266272 | tf_op jit(solution)/shard_map/ppermute | solution.py:279
  51.1 2.7 %collective-permute-done.18 = bf16[1040,128]{1,0:T(8,128)(2,1)S(1)} collective-permute-done((bf16[1040,128]{1,0:T(8,128)(2,1)S(1)}, bf16[1040,128]{1,0:T(8,128)(2,1)S(1)}, u32[]{:S(2)}, u32[]{:S(2)}) %collective-permute-start.18) | collective-permute-done | bytes 266272 | tf_op jit(solution)/shard_map/ppermute | solution.py:279
  54.1 1.4 %shard_map.89.rest_0_ = bf16[10240,512]{1,0:T(8,128)(2,1)S(1)} custom-call(s32[8]{0:T(128)S(1)} %get-tuple-element.34.count_ref, s32[3,640]{1,0:T(4,128)S(1)} %get-tuple-element.35.list_ref, bf16[2080,128]{1,0:T(8,128)(2,1)S(1)} %constant_dynamic-update-slice_fusion.18.buf_ref.rest_1_, ...), custom_call_target="tpu_custom_call", output_to_operand_aliasing={{}: (4, {})} | custom-call | flops 1073741824 | bytes 1048576 | tf_op jit(solution)/shard_map/pallas_call | solution.py:364
  55.5 1.9 %collective-permute-done.20 = bf16[1040,128]{1,0:T(8,128)(2,1)S(1)} collective-permute-done((bf16[1040,128]{1,0:T(8,128)(2,1)S(1)}, bf16[1040,128]{1,0:T(8,128)(2,1)S(1)}, u32[]{:S(2)}, u32[]{:S(2)}) %collective-permute-start.20) | collective-permute-done | bytes 266272 | tf_op jit(solution)/shard_map/ppermute | solution.py:279
  57.9 2.3 %collective-permute-done.22 = bf16[1040,128]{1,0:T(8,128)(2,1)S(1)} collective-permute-done((bf16[1040,128]{1,0:T(8,128)(2,1)S(1)}, bf16[1040,128]{1,0:T(8,128)(2,1)S(1)}, u32[]{:S(2)}, u32[]{:S(2)}) %collective-permute-start.22) | collective-permute-done | bytes 266272 | tf_op jit(solution)/shard_map/ppermute | solution.py:279
  60.4 1.3 %shard_map.90.rest_0_ = bf16[10240,512]{1,0:T(8,128)(2,1)S(1)} custom-call(s32[8]{0:T(128)S(1)} %get-tuple-element.34.count_ref, s32[3,640]{1,0:T(4,128)S(1)} %get-tuple-element.35.list_ref, bf16[2080,128]{1,0:T(8,128)(2,1)S(1)} %constant_dynamic-update-slice_fusion.20.buf_ref.rest_2_, ...), custom_call_target="tpu_custom_call", output_to_operand_aliasing={{}: (4, {})} | custom-call | flops 1073741824 | bytes 1048576 | tf_op jit(solution)/shard_map/pallas_call | solution.py:364
  65.2 1.4 %collective-permute-done.26 = bf16[1040,128]{1,0:T(8,128)(2,1)S(1)} collective-permute-done((bf16[1040,128]{1,0:T(8,128)(2,1)S(1)}, bf16[1040,128]{1,0:T(8,128)(2,1)S(1)}, u32[]{:S(2)}, u32[]{:S(2)}) %collective-permute-start.26) | collective-permute-done | bytes 266272 | tf_op jit(solution)/shard_map/ppermute | solution.py:279
  66.7 1.8 %shard_map.92.rest_0_ = bf16[10240,512]{1,0:T(8,128)(2,1)S(1)} custom-call(s32[8]{0:T(128)S(1)} %get-tuple-element.34.count_ref, s32[3,640]{1,0:T(4,128)S(1)} %get-tuple-element.35.list_ref, bf16[2080,128]{1,0:T(8,128)(2,1)S(1)} %constant_dynamic-update-slice_fusion.24.buf_ref.rest_4_, ...), custom_call_target="tpu_custom_call", output_to_operand_aliasing={{}: (4, {})} | custom-call | flops 1073741824 | bytes 1048576 | tf_op jit(solution)/shard_map/pallas_call | solution.py:364
  70.2 1.6 %shard_map.94.rest_0_ = bf16[10240,512]{1,0:T(8,128)(2,1)S(1)} custom-call(s32[8]{0:T(128)S(1)} %get-tuple-element.34.count_ref, s32[3,640]{1,0:T(4,128)S(1)} %get-tuple-element.35.list_ref, bf16[2080,128]{1,0:T(8,128)(2,1)S(1)} %constant_dynamic-update-slice_fusion.28.buf_ref.rest_6_, ...), custom_call_target="tpu_custom_call", output_to_operand_aliasing={{}: (4, {})} | custom-call | flops 1073741824 | bytes 1048576 | tf_op jit(solution)/shard_map/pallas_call | solution.py:364
  72.6 3.4 %shard_map.96 = (f32[1024,128]{1,0:T(8,128)S(1)}, f32[8,128]{1,0:T(8,128)S(1)}, bf16[1040,128]{1,0:T(8,128)(2,1)S(1)}) custom-call(s32[16]{0:T(128)S(1)} %broadcast_multiply_fusion.stat_ref, bf16[5120,128]{1,0:T(8,128)(2,1)S(1)} %bitcast.3, bf16[1024,128]{1,0:T(8,128)(2,1)S(1)} %copy-done.4, ...), custom_call_target="tpu_custom_call" | custom-call | flops 2684354560 | bytes 16777216 | tf_op jit(solution)/shard_map/pallas_call | solution.py:380
  76.3 1.3 %collective-permute-done.30 = bf16[1040,128]{1,0:T(8,128)(2,1)S(1)} collective-permute-done((bf16[1040,128]{1,0:T(8,128)(2,1)S(1)}, bf16[1040,128]{1,0:T(8,128)(2,1)S(1)}, u32[]{:S(2)}, u32[]{:S(2)}) %collective-permute-start.30) | collective-permute-done | bytes 266272 | tf_op jit(solution)/shard_map/ppermute | solution.py:276
  77.7 1.5 %collective-permute-start.31 = (bf16[1040,128]{1,0:T(8,128)(2,1)S(1)}, bf16[1040,128]{1,0:T(8,128)(2,1)S(1)}, u32[]{:S(2)}, u32[]{:S(2)}) collective-permute-start(bf16[1040,128]{1,0:T(8,128)(2,1)S(1)} %get-tuple-element.47), channel_id=1, source_target_pairs={{0,4},{5,1},{4,8},{9,5},{8,12},{13,9},{12,14},{15,13},{14,10},{11,... | collective-permute-start | bytes 798728 | tf_op jit(solution)/shard_map/ppermute | solution.py:279
  79.2 1.7 %collective-permute-start.33 = (bf16[1040,128]{1,0:T(8,128)(2,1)S(1)}, bf16[1040,128]{1,0:T(8,128)(2,1)S(1)}, u32[]{:S(2)}, u32[]{:S(2)}) collective-permute-start(bf16[1040,128]{1,0:T(8,128)(2,1)S(1)} %collective-permute-done.30), channel_id=1, source_target_pairs={{0,4},{5,1},{4,8},{9,5},{8,12},{13,9},{12,14},{15,13},{14,10},{11,... | collective-permute-start | bytes 798728 | tf_op jit(solution)/shard_map/ppermute | solution.py:279
  80.9 1.9 %shard_map.97.rest_0_ = bf16[10240,512]{1,0:T(8,128)(2,1)S(1)} custom-call(s32[8]{0:T(128)S(1)} %get-tuple-element.34.count_ref, s32[3,640]{1,0:T(4,128)S(1)} %get-tuple-element.35.list_ref, bf16[2080,128]{1,0:T(8,128)(2,1)S(1)} %constant_dynamic-update-slice_fusion.32.buf_ref.rest_0_, bf16[40960,128]{1,0:T(8,128)(2,1)S(1)} %get-tuple-element.36.env_ref), custom_call_target="tpu_custom_call" | custom-call | flops 1073741824 | bytes 1048576 | tf_op jit(solution)/shard_map/pallas_call | solution.py:364
  82.8 1.3 %collective-permute-done.31 = bf16[1040,128]{1,0:T(8,128)(2,1)S(1)} collective-permute-done((bf16[1040,128]{1,0:T(8,128)(2,1)S(1)}, bf16[1040,128]{1,0:T(8,128)(2,1)S(1)}, u32[]{:S(2)}, u32[]{:S(2)}) %collective-permute-start.31) | collective-permute-done | bytes 266272 | tf_op jit(solution)/shard_map/ppermute | solution.py:279
  84.1 1.5 %collective-permute-start.35 = (bf16[1040,128]{1,0:T(8,128)(2,1)S(1)}, bf16[1040,128]{1,0:T(8,128)(2,1)S(1)}, u32[]{:S(2)}, u32[]{:S(2)}) collective-permute-start(bf16[1040,128]{1,0:T(8,128)(2,1)S(1)} %collective-permute-done.31), channel_id=1, source_target_pairs={{0,4},{5,1},{4,8},{9,5},{8,12},{13,9},{12,14},{15,13},{14,10},{11,... | collective-permute-start | bytes 798728 | tf_op jit(solution)/shard_map/ppermute | solution.py:279
  85.6 1.4 %collective-permute-done.33 = bf16[1040,128]{1,0:T(8,128)(2,1)S(1)} collective-permute-done((bf16[1040,128]{1,0:T(8,128)(2,1)S(1)}, bf16[1040,128]{1,0:T(8,128)(2,1)S(1)}, u32[]{:S(2)}, u32[]{:S(2)}) %collective-permute-start.33) | collective-permute-done | bytes 266272 | tf_op jit(solution)/shard_map/ppermute | solution.py:279
  86.9 1.5 %collective-permute-start.37 = (bf16[1040,128]{1,0:T(8,128)(2,1)S(1)}, bf16[1040,128]{1,0:T(8,128)(2,1)S(1)}, u32[]{:S(2)}, u32[]{:S(2)}) collective-permute-start(bf16[1040,128]{1,0:T(8,128)(2,1)S(1)} %collective-permute-done.33), channel_id=1, source_target_pairs={{0,4},{5,1},{4,8},{9,5},{8,12},{13,9},{12,14},{15,13},{14,10},{11,... | collective-permute-start | bytes 798728 | tf_op jit(solution)/shard_map/ppermute | solution.py:279
  90.5 1.5 %collective-permute-start.39 = (bf16[1040,128]{1,0:T(8,128)(2,1)S(1)}, bf16[1040,128]{1,0:T(8,128)(2,1)S(1)}, u32[]{:S(2)}, u32[]{:S(2)}) collective-permute-start(bf16[1040,128]{1,0:T(8,128)(2,1)S(1)} %collective-permute-done.35), channel_id=1, source_target_pairs={{0,4},{5,1},{4,8},{9,5},{8,12},{13,9},{12,14},{15,13},{14,10},{11,... | collective-permute-start | bytes 798728 | tf_op jit(solution)/shard_map/ppermute | solution.py:279
  92.0 1.4 %collective-permute-done.37 = bf16[1040,128]{1,0:T(8,128)(2,1)S(1)} collective-permute-done((bf16[1040,128]{1,0:T(8,128)(2,1)S(1)}, bf16[1040,128]{1,0:T(8,128)(2,1)S(1)}, u32[]{:S(2)}, u32[]{:S(2)}) %collective-permute-start.37) | collective-permute-done | bytes 266272 | tf_op jit(solution)/shard_map/ppermute | solution.py:279
  93.3 1.5 %collective-permute-start.41 = (bf16[1040,128]{1,0:T(8,128)(2,1)S(1)}, bf16[1040,128]{1,0:T(8,128)(2,1)S(1)}, u32[]{:S(2)}, u32[]{:S(2)}) collective-permute-start(bf16[1040,128]{1,0:T(8,128)(2,1)S(1)} %collective-permute-done.37), channel_id=1, source_target_pairs={{0,4},{5,1},{4,8},{9,5},{8,12},{13,9},{12,14},{15,13},{14,10},{11,... | collective-permute-start | bytes 798728 | tf_op jit(solution)/shard_map/ppermute | solution.py:279
  94.9 1.2 %shard_map.99.rest_0_ = bf16[10240,512]{1,0:T(8,128)(2,1)S(1)} custom-call(s32[8]{0:T(128)S(1)} %get-tuple-element.34.count_ref, s32[3,640]{1,0:T(4,128)S(1)} %get-tuple-element.35.list_ref, bf16[2080,128]{1,0:T(8,128)(2,1)S(1)} %constant_dynamic-update-slice_fusion.36.buf_ref.rest_2_, ...), custom_call_target="tpu_custom_call", output_to_operand_aliasing={{}: (4, {})} | custom-call | flops 1073741824 | bytes 1048576 | tf_op jit(solution)/shard_map/pallas_call | solution.py:364
  97.5 1.7 %collective-permute-start.43 = (bf16[1040,128]{1,0:T(8,128)(2,1)S(1)}, bf16[1040,128]{1,0:T(8,128)(2,1)S(1)}, u32[]{:S(2)}, u32[]{:S(2)}) collective-permute-start(bf16[1040,128]{1,0:T(8,128)(2,1)S(1)} %collective-permute-done.39), channel_id=1, source_target_pairs={{0,4},{5,1},{4,8},{9,5},{8,12},{13,9},{12,14},{15,13},{14,10},{11,... | collective-permute-start | bytes 798728 | tf_op jit(solution)/shard_map/ppermute | solution.py:279
  99.8 2.0 %shard_map.101.rest_0_ = bf16[10240,512]{1,0:T(8,128)(2,1)S(1)} custom-call(s32[8]{0:T(128)S(1)} %get-tuple-element.34.count_ref, s32[3,640]{1,0:T(4,128)S(1)} %get-tuple-element.35.list_ref, bf16[2080,128]{1,0:T(8,128)(2,1)S(1)} %constant_dynamic-update-slice_fusion.40.buf_ref.rest_4_, ...), custom_call_target="tpu_custom_call", output_to_operand_aliasing={{}: (4, {})} | custom-call | flops 1073741824 | bytes 1048576 | tf_op jit(solution)/shard_map/pallas_call | solution.py:364
  102.7 1.3 %collective-permute-done.43 = bf16[1040,128]{1,0:T(8,128)(2,1)S(1)} collective-permute-done((bf16[1040,128]{1,0:T(8,128)(2,1)S(1)}, bf16[1040,128]{1,0:T(8,128)(2,1)S(1)}, u32[]{:S(2)}, u32[]{:S(2)}) %collective-permute-start.43) | collective-permute-done | bytes 266272 | tf_op jit(solution)/shard_map/ppermute | solution.py:279
  104.0 1.6 %shard_map.103.rest_0_ = bf16[10240,512]{1,0:T(8,128)(2,1)S(1)} custom-call(s32[8]{0:T(128)S(1)} %get-tuple-element.34.count_ref, s32[3,640]{1,0:T(4,128)S(1)} %get-tuple-element.35.list_ref, bf16[2080,128]{1,0:T(8,128)(2,1)S(1)} %constant_dynamic-update-slice_fusion.44.buf_ref.rest_6_, ...), custom_call_target="tpu_custom_call", output_to_operand_aliasing={{}: (4, {})} | custom-call | flops 1073741824 | bytes 1048576 | tf_op jit(solution)/shard_map/pallas_call | solution.py:364
  106.4 4.3 %shard_map.105 = (f32[1024,128]{1,0:T(8,128)}, f32[8,128]{1,0:T(8,128)S(1)}, f32[8,128]{1,0:T(8,128)S(1)}) custom-call(s32[16]{0:T(128)S(1)} %broadcast_multiply_fusion.stat_ref, bf16[5120,128]{1,0:T(8,128)(2,1)S(1)} %bitcast.4, bf16[1024,128]{1,0:T(8,128)(2,1)S(1)} %copy-done.4, bf16[2080,128]{1,0:T(8,128)(2,1)S(1)} %constant_dynamic-update-slice_fusion.32.buf_ref.rest_0_, ...), custom_call_target="tpu_custom_call" | custom-call | flops 2684354560 | bytes 16777216 | tf_op jit(solution)/shard_map/pallas_call | solution.py:380
  112.7 2.8 %collective-permute-done.46 = f32[8,128]{1,0:T(8,128)S(1)} collective-permute-done((f32[8,128]{1,0:T(8,128)S(1)}, f32[8,128]{1,0:T(8,128)S(1)}, u32[]{:S(2)}, u32[]{:S(2)}) %collective-permute-start.46) | collective-permute-done | bytes 4128 | tf_op jit(solution)/shard_map/ppermute | solution.py:407
  115.5 2.4 %collective-permute-start.47 = (f32[8,128]{1,0:T(8,128)S(1)}, f32[8,128]{1,0:T(8,128)S(1)}, u32[]{:S(2)}, u32[]{:S(2)}) collective-permute-start(f32[8,128]{1,0:T(8,128)S(1)} %add.278), channel_id=1, source_target_pairs={{0,4},{1,5},{2,6},{3,7},{4,0},{5,1},{6,2},{7,3},{8,12},{9,13},{10,... | collective-permute-start | bytes 12296 | tf_op jit(solution)/shard_map/ppermute | solution.py:407
  117.9 1.6 %collective-permute-done.47 = f32[8,128]{1,0:T(8,128)S(1)} collective-permute-done((f32[8,128]{1,0:T(8,128)S(1)}, f32[8,128]{1,0:T(8,128)S(1)}, u32[]{:S(2)}, u32[]{:S(2)}) %collective-permute-start.47) | collective-permute-done | bytes 4128 | tf_op jit(solution)/shard_map/ppermute | solution.py:407
  119.5 2.5 %collective-permute-start.48 = (f32[8,128]{1,0:T(8,128)S(1)}, f32[8,128]{1,0:T(8,128)S(1)}, u32[]{:S(2)}, u32[]{:S(2)}) collective-permute-start(f32[8,128]{1,0:T(8,128)S(1)} %add.279), channel_id=1, source_target_pairs={{0,8},{1,9},{2,10},{3,11},{4,12},{5,13},{6,14},{7,15},{8,0},{9,1},... | collective-permute-start | bytes 12296 | tf_op jit(solution)/shard_map/ppermute | solution.py:407
  122.0 2.0 %collective-permute-done.48 = f32[8,128]{1,0:T(8,128)S(1)} collective-permute-done((f32[8,128]{1,0:T(8,128)S(1)}, f32[8,128]{1,0:T(8,128)S(1)}, u32[]{:S(2)}, u32[]{:S(2)}) %collective-permute-start.48) | collective-permute-done | bytes 4128 | tf_op jit(solution)/shard_map/ppermute | solution.py:407
  (151 shorter events, 27.4 us)
Async XLA Ops:
  1.8 2.5 %collective-permute-start = (bf16[1040,128]{1,0:T(8,128)(2,1)S(1)}, bf16[1040,128]{1,0:T(8,128)(2,1)S(1)}, u32[]{:S(2)}, u32[]{:S(2)}) collective-permute-start(bf16[1040,128]{1,0:T(8,128)(2,1)S(1)} %shard_map.77), channel_id=1, source_target_pairs={{0,1},{1,0},{2,3},{3,2},{4,5},{5,4},{6,7},{7,6},{8,9},{9,8},{10,11... | collective-permute-start | bytes 798728 | tf_op jit(solution)/shard_map/ppermute | solution.py:276
  4.3 9.7 %collective-permute-start.1 = (bf16[1040,128]{1,0:T(8,128)(2,1)S(1)}, bf16[1040,128]{1,0:T(8,128)(2,1)S(1)}, u32[]{:S(2)}, u32[]{:S(2)}) collective-permute-start(bf16[1040,128]{1,0:T(8,128)(2,1)S(1)} %shard_map.77), channel_id=1, source_target_pairs={{0,4},{5,1},{4,8},{9,5},{8,12},{13,9},{12,14},{15,13},{14,10},{11,... | collective-permute-start | bytes 798728 | tf_op jit(solution)/shard_map/ppermute | solution.py:279
  6.9 8.7 %collective-permute-start.3 = (bf16[1040,128]{1,0:T(8,128)(2,1)S(1)}, bf16[1040,128]{1,0:T(8,128)(2,1)S(1)}, u32[]{:S(2)}, u32[]{:S(2)}) collective-permute-start(bf16[1040,128]{1,0:T(8,128)(2,1)S(1)} %collective-permute-done), channel_id=1, source_target_pairs={{0,4},{5,1},{4,8},{9,5},{8,12},{13,9},{12,14},{15,13},{14,10},{11,... | collective-permute-start | bytes 798728 | tf_op jit(solution)/shard_map/ppermute | solution.py:279
  14.0 6.5 %collective-permute-start.5 = (bf16[1040,128]{1,0:T(8,128)(2,1)S(1)}, bf16[1040,128]{1,0:T(8,128)(2,1)S(1)}, u32[]{:S(2)}, u32[]{:S(2)}) collective-permute-start(bf16[1040,128]{1,0:T(8,128)(2,1)S(1)} %collective-permute-done.1), channel_id=1, source_target_pairs={{0,4},{5,1},{4,8},{9,5},{8,12},{13,9},{12,14},{15,13},{14,10},{11,... | collective-permute-start | bytes 798728 | tf_op jit(solution)/shard_map/ppermute | solution.py:279
  15.6 6.5 %collective-permute-start.2 = (bf16[1040,128]{1,0:T(8,128)(2,1)S(1)}, bf16[1040,128]{1,0:T(8,128)(2,1)S(1)}, u32[]{:S(2)}, u32[]{:S(2)}) collective-permute-start(bf16[1040,128]{1,0:T(8,128)(2,1)S(1)} %collective-permute-done.1), channel_id=1, source_target_pairs={{0,1},{1,0},{2,3},{3,2},{4,5},{5,4},{6,7},{7,6},{8,9},{9,8},{10,11... | collective-permute-start | bytes 798728 | tf_op jit(solution)/shard_map/ppermute | solution.py:276
  15.6 9.0 %collective-permute-start.7 = (bf16[1040,128]{1,0:T(8,128)(2,1)S(1)}, bf16[1040,128]{1,0:T(8,128)(2,1)S(1)}, u32[]{:S(2)}, u32[]{:S(2)}) collective-permute-start(bf16[1040,128]{1,0:T(8,128)(2,1)S(1)} %collective-permute-done.3), channel_id=1, source_target_pairs={{0,4},{5,1},{4,8},{9,5},{8,12},{13,9},{12,14},{15,13},{14,10},{11,... | collective-permute-start | bytes 798728 | tf_op jit(solution)/shard_map/ppermute | solution.py:279
  17.1 4.9 %collective-permute-start.4 = (bf16[1040,128]{1,0:T(8,128)(2,1)S(1)}, bf16[1040,128]{1,0:T(8,128)(2,1)S(1)}, u32[]{:S(2)}, u32[]{:S(2)}) collective-permute-start(bf16[1040,128]{1,0:T(8,128)(2,1)S(1)} %collective-permute-done.3), channel_id=1, source_target_pairs={{0,1},{1,0},{2,3},{3,2},{4,5},{5,4},{6,7},{7,6},{8,9},{9,8},{10,11... | collective-permute-start | bytes 798728 | tf_op jit(solution)/shard_map/ppermute | solution.py:276
  20.5 9.5 %collective-permute-start.9 = (bf16[1040,128]{1,0:T(8,128)(2,1)S(1)}, bf16[1040,128]{1,0:T(8,128)(2,1)S(1)}, u32[]{:S(2)}, u32[]{:S(2)}) collective-permute-start(bf16[1040,128]{1,0:T(8,128)(2,1)S(1)} %collective-permute-done.5), channel_id=1, source_target_pairs={{0,4},{5,1},{4,8},{9,5},{8,12},{13,9},{12,14},{15,13},{14,10},{11,... | collective-permute-start | bytes 798728 | tf_op jit(solution)/shard_map/ppermute | solution.py:279
  22.1 6.6 %collective-permute-start.6 = (bf16[1040,128]{1,0:T(8,128)(2,1)S(1)}, bf16[1040,128]{1,0:T(8,128)(2,1)S(1)}, u32[]{:S(2)}, u32[]{:S(2)}) collective-permute-start(bf16[1040,128]{1,0:T(8,128)(2,1)S(1)} %collective-permute-done.5), channel_id=1, source_target_pairs={{0,1},{1,0},{2,3},{3,2},{4,5},{5,4},{6,7},{7,6},{8,9},{9,8},{10,11... | collective-permute-start | bytes 798728 | tf_op jit(solution)/shard_map/ppermute | solution.py:276
  24.7 6.5 %collective-permute-start.11 = (bf16[1040,128]{1,0:T(8,128)(2,1)S(1)}, bf16[1040,128]{1,0:T(8,128)(2,1)S(1)}, u32[]{:S(2)}, u32[]{:S(2)}) collective-permute-start(bf16[1040,128]{1,0:T(8,128)(2,1)S(1)} %collective-permute-done.7), channel_id=1, source_target_pairs={{0,4},{5,1},{4,8},{9,5},{8,12},{13,9},{12,14},{15,13},{14,10},{11,... | collective-permute-start | bytes 798728 | tf_op jit(solution)/shard_map/ppermute | solution.py:279
  26.7 4.5 %collective-permute-start.8 = (bf16[1040,128]{1,0:T(8,128)(2,1)S(1)}, bf16[1040,128]{1,0:T(8,128)(2,1)S(1)}, u32[]{:S(2)}, u32[]{:S(2)}) collective-permute-start(bf16[1040,128]{1,0:T(8,128)(2,1)S(1)} %collective-permute-done.7), channel_id=1, source_target_pairs={{0,1},{1,0},{2,3},{3,2},{4,5},{5,4},{6,7},{7,6},{8,9},{9,8},{10,11... | collective-permute-start | bytes 798728 | tf_op jit(solution)/shard_map/ppermute | solution.py:276
  30.0 6.5 %collective-permute-start.13 = (bf16[1040,128]{1,0:T(8,128)(2,1)S(1)}, bf16[1040,128]{1,0:T(8,128)(2,1)S(1)}, u32[]{:S(2)}, u32[]{:S(2)}) collective-permute-start(bf16[1040,128]{1,0:T(8,128)(2,1)S(1)} %collective-permute-done.9), channel_id=1, source_target_pairs={{0,4},{5,1},{4,8},{9,5},{8,12},{13,9},{12,14},{15,13},{14,10},{11,... | collective-permute-start | bytes 798728 | tf_op jit(solution)/shard_map/ppermute | solution.py:279
  30.1 3.0 %collective-permute-start.10 = (bf16[1040,128]{1,0:T(8,128)(2,1)S(1)}, bf16[1040,128]{1,0:T(8,128)(2,1)S(1)}, u32[]{:S(2)}, u32[]{:S(2)}) collective-permute-start(bf16[1040,128]{1,0:T(8,128)(2,1)S(1)} %collective-permute-done.9), channel_id=1, source_target_pairs={{0,1},{1,0},{2,3},{3,2},{4,5},{5,4},{6,7},{7,6},{8,9},{9,8},{10,11... | collective-permute-start | bytes 798728 | tf_op jit(solution)/shard_map/ppermute | solution.py:276
  31.1 5.3 %collective-permute-start.12 = (bf16[1040,128]{1,0:T(8,128)(2,1)S(1)}, bf16[1040,128]{1,0:T(8,128)(2,1)S(1)}, u32[]{:S(2)}, u32[]{:S(2)}) collective-permute-start(bf16[1040,128]{1,0:T(8,128)(2,1)S(1)} %collective-permute-done.11), channel_id=1, source_target_pairs={{0,1},{1,0},{2,3},{3,2},{4,5},{5,4},{6,7},{7,6},{8,9},{9,8},{10,11... | collective-permute-start | bytes 798728 | tf_op jit(solution)/shard_map/ppermute | solution.py:276
  36.5 1.6 %collective-permute-start.14 = (bf16[1040,128]{1,0:T(8,128)(2,1)S(1)}, bf16[1040,128]{1,0:T(8,128)(2,1)S(1)}, u32[]{:S(2)}, u32[]{:S(2)}) collective-permute-start(bf16[1040,128]{1,0:T(8,128)(2,1)S(1)} %collective-permute-done.13), channel_id=1, source_target_pairs={{0,1},{1,0},{2,3},{3,2},{4,5},{5,4},{6,7},{7,6},{8,9},{9,8},{10,11... | collective-permute-start | bytes 798728 | tf_op jit(solution)/shard_map/ppermute | solution.py:276
  42.9 1.6 %collective-permute-start.15 = (bf16[1040,128]{1,0:T(8,128)(2,1)S(1)}, bf16[1040,128]{1,0:T(8,128)(2,1)S(1)}, u32[]{:S(2)}, u32[]{:S(2)}) collective-permute-start(bf16[1040,128]{1,0:T(8,128)(2,1)S(1)} %get-tuple-element.40), channel_id=1, source_target_pairs={{0,1},{1,0},{2,3},{3,2},{4,5},{5,4},{6,7},{7,6},{8,9},{9,8},{10,11... | collective-permute-start | bytes 798728 | tf_op jit(solution)/shard_map/ppermute | solution.py:276
  44.5 6.4 %collective-permute-start.16 = (bf16[1040,128]{1,0:T(8,128)(2,1)S(1)}, bf16[1040,128]{1,0:T(8,128)(2,1)S(1)}, u32[]{:S(2)}, u32[]{:S(2)}) collective-permute-start(bf16[1040,128]{1,0:T(8,128)(2,1)S(1)} %get-tuple-element.40), channel_id=1, source_target_pairs={{0,4},{5,1},{4,8},{9,5},{8,12},{13,9},{12,14},{15,13},{14,10},{11,... | collective-permute-start | bytes 798728 | tf_op jit(solution)/shard_map/ppermute | solution.py:279
  44.7 9.1 %collective-permute-start.18 = (bf16[1040,128]{1,0:T(8,128)(2,1)S(1)}, bf16[1040,128]{1,0:T(8,128)(2,1)S(1)}, u32[]{:S(2)}, u32[]{:S(2)}) collective-permute-start(bf16[1040,128]{1,0:T(8,128)(2,1)S(1)} %collective-permute-done.15), channel_id=1, source_target_pairs={{0,4},{5,1},{4,8},{9,5},{8,12},{13,9},{12,14},{15,13},{14,10},{11,... | collective-permute-start | bytes 798728 | tf_op jit(solution)/shard_map/ppermute | solution.py:279
  50.9 6.4 %collective-permute-start.20 = (bf16[1040,128]{1,0:T(8,128)(2,1)S(1)}, bf16[1040,128]{1,0:T(8,128)(2,1)S(1)}, u32[]{:S(2)}, u32[]{:S(2)}) collective-permute-start(bf16[1040,128]{1,0:T(8,128)(2,1)S(1)} %collective-permute-done.16), channel_id=1, source_target_pairs={{0,4},{5,1},{4,8},{9,5},{8,12},{13,9},{12,14},{15,13},{14,10},{11,... | collective-permute-start | bytes 798728 | tf_op jit(solution)/shard_map/ppermute | solution.py:279
  51.1 2.9 %collective-permute-start.17 = (bf16[1040,128]{1,0:T(8,128)(2,1)S(1)}, bf16[1040,128]{1,0:T(8,128)(2,1)S(1)}, u32[]{:S(2)}, u32[]{:S(2)}) collective-permute-start(bf16[1040,128]{1,0:T(8,128)(2,1)S(1)} %collective-permute-done.16), channel_id=1, source_target_pairs={{0,1},{1,0},{2,3},{3,2},{4,5},{5,4},{6,7},{7,6},{8,9},{9,8},{10,11... | collective-permute-start | bytes 798728 | tf_op jit(solution)/shard_map/ppermute | solution.py:276
  53.8 6.4 %collective-permute-start.22 = (bf16[1040,128]{1,0:T(8,128)(2,1)S(1)}, bf16[1040,128]{1,0:T(8,128)(2,1)S(1)}, u32[]{:S(2)}, u32[]{:S(2)}) collective-permute-start(bf16[1040,128]{1,0:T(8,128)(2,1)S(1)} %collective-permute-done.18), channel_id=1, source_target_pairs={{0,4},{5,1},{4,8},{9,5},{8,12},{13,9},{12,14},{15,13},{14,10},{11,... | collective-permute-start | bytes 798728 | tf_op jit(solution)/shard_map/ppermute | solution.py:279
  53.9 6.4 %collective-permute-start.19 = (bf16[1040,128]{1,0:T(8,128)(2,1)S(1)}, bf16[1040,128]{1,0:T(8,128)(2,1)S(1)}, u32[]{:S(2)}, u32[]{:S(2)}) collective-permute-start(bf16[1040,128]{1,0:T(8,128)(2,1)S(1)} %collective-permute-done.18), channel_id=1, source_target_pairs={{0,1},{1,0},{2,3},{3,2},{4,5},{5,4},{6,7},{7,6},{8,9},{9,8},{10,11... | collective-permute-start | bytes 798728 | tf_op jit(solution)/shard_map/ppermute | solution.py:276
  57.4 6.4 %collective-permute-start.24 = (bf16[1040,128]{1,0:T(8,128)(2,1)S(1)}, bf16[1040,128]{1,0:T(8,128)(2,1)S(1)}, u32[]{:S(2)}, u32[]{:S(2)}) collective-permute-start(bf16[1040,128]{1,0:T(8,128)(2,1)S(1)} %collective-permute-done.20), channel_id=1, source_target_pairs={{0,4},{5,1},{4,8},{9,5},{8,12},{13,9},{12,14},{15,13},{14,10},{11,... | collective-permute-start | bytes 798728 | tf_op jit(solution)/shard_map/ppermute | solution.py:279
  57.5 4.2 %collective-permute-start.21 = (bf16[1040,128]{1,0:T(8,128)(2,1)S(1)}, bf16[1040,128]{1,0:T(8,128)(2,1)S(1)}, u32[]{:S(2)}, u32[]{:S(2)}) collective-permute-start(bf16[1040,128]{1,0:T(8,128)(2,1)S(1)} %collective-permute-done.20), channel_id=1, source_target_pairs={{0,1},{1,0},{2,3},{3,2},{4,5},{5,4},{6,7},{7,6},{8,9},{9,8},{10,11... | collective-permute-start | bytes 798728 | tf_op jit(solution)/shard_map/ppermute | solution.py:276
  60.2 6.4 %collective-permute-start.26 = (bf16[1040,128]{1,0:T(8,128)(2,1)S(1)}, bf16[1040,128]{1,0:T(8,128)(2,1)S(1)}, u32[]{:S(2)}, u32[]{:S(2)}) collective-permute-start(bf16[1040,128]{1,0:T(8,128)(2,1)S(1)} %collective-permute-done.22), channel_id=1, source_target_pairs={{0,4},{5,1},{4,8},{9,5},{8,12},{13,9},{12,14},{15,13},{14,10},{11,... | collective-permute-start | bytes 798728 | tf_op jit(solution)/shard_map/ppermute | solution.py:279
  60.4 6.3 %collective-permute-start.23 = (bf16[1040,128]{1,0:T(8,128)(2,1)S(1)}, bf16[1040,128]{1,0:T(8,128)(2,1)S(1)}, u32[]{:S(2)}, u32[]{:S(2)}) collective-permute-start(bf16[1040,128]{1,0:T(8,128)(2,1)S(1)} %collective-permute-done.22), channel_id=1, source_target_pairs={{0,1},{1,0},{2,3},{3,2},{4,5},{5,4},{6,7},{7,6},{8,9},{9,8},{10,11... | collective-permute-start | bytes 798728 | tf_op jit(solution)/shard_map/ppermute | solution.py:276
  63.8 6.4 %collective-permute-start.28 = (bf16[1040,128]{1,0:T(8,128)(2,1)S(1)}, bf16[1040,128]{1,0:T(8,128)(2,1)S(1)}, u32[]{:S(2)}, u32[]{:S(2)}) collective-permute-start(bf16[1040,128]{1,0:T(8,128)(2,1)S(1)} %collective-permute-done.24), channel_id=1, source_target_pairs={{0,4},{5,1},{4,8},{9,5},{8,12},{13,9},{12,14},{15,13},{14,10},{11,... | collective-permute-start | bytes 798728 | tf_op jit(solution)/shard_map/ppermute | solution.py:279
  64.6 3.9 %collective-permute-start.25 = (bf16[1040,128]{1,0:T(8,128)(2,1)S(1)}, bf16[1040,128]{1,0:T(8,128)(2,1)S(1)}, u32[]{:S(2)}, u32[]{:S(2)}) collective-permute-start(bf16[1040,128]{1,0:T(8,128)(2,1)S(1)} %collective-permute-done.24), channel_id=1, source_target_pairs={{0,1},{1,0},{2,3},{3,2},{4,5},{5,4},{6,7},{7,6},{8,9},{9,8},{10,11... | collective-permute-start | bytes 798728 | tf_op jit(solution)/shard_map/ppermute | solution.py:276
  66.6 3.6 %collective-permute-start.27 = (bf16[1040,128]{1,0:T(8,128)(2,1)S(1)}, bf16[1040,128]{1,0:T(8,128)(2,1)S(1)}, u32[]{:S(2)}, u32[]{:S(2)}) collective-permute-start(bf16[1040,128]{1,0:T(8,128)(2,1)S(1)} %collective-permute-done.26), channel_id=1, source_target_pairs={{0,1},{1,0},{2,3},{3,2},{4,5},{5,4},{6,7},{7,6},{8,9},{9,8},{10,11... | collective-permute-start | bytes 798728 | tf_op jit(solution)/shard_map/ppermute | solution.py:276
  70.2 1.6 %collective-permute-start.29 = (bf16[1040,128]{1,0:T(8,128)(2,1)S(1)}, bf16[1040,128]{1,0:T(8,128)(2,1)S(1)}, u32[]{:S(2)}, u32[]{:S(2)}) collective-permute-start(bf16[1040,128]{1,0:T(8,128)(2,1)S(1)} %collective-permute-done.28), channel_id=1, source_target_pairs={{0,1},{1,0},{2,3},{3,2},{4,5},{5,4},{6,7},{7,6},{8,9},{9,8},{10,11... | collective-permute-start | bytes 798728 | tf_op jit(solution)/shard_map/ppermute | solution.py:276
  76.1 1.6 %collective-permute-start.30 = (bf16[1040,128]{1,0:T(8,128)(2,1)S(1)}, bf16[1040,128]{1,0:T(8,128)(2,1)S(1)}, u32[]{:S(2)}, u32[]{:S(2)}) collective-permute-start(bf16[1040,128]{1,0:T(8,128)(2,1)S(1)} %get-tuple-element.47), channel_id=1, source_target_pairs={{0,1},{1,0},{2,3},{3,2},{4,5},{5,4},{6,7},{7,6},{8,9},{9,8},{10,11... | collective-permute-start | bytes 798728 | tf_op jit(solution)/shard_map/ppermute | solution.py:276
  77.7 6.4 %collective-permute-start.31 = (bf16[1040,128]{1,0:T(8,128)(2,1)S(1)}, bf16[1040,128]{1,0:T(8,128)(2,1)S(1)}, u32[]{:S(2)}, u32[]{:S(2)}) collective-permute-start(bf16[1040,128]{1,0:T(8,128)(2,1)S(1)} %get-tuple-element.47), channel_id=1, source_target_pairs={{0,4},{5,1},{4,8},{9,5},{8,12},{13,9},{12,14},{15,13},{14,10},{11,... | collective-permute-start | bytes 798728 | tf_op jit(solution)/shard_map/ppermute | solution.py:279
  79.2 7.8 %collective-permute-start.33 = (bf16[1040,128]{1,0:T(8,128)(2,1)S(1)}, bf16[1040,128]{1,0:T(8,128)(2,1)S(1)}, u32[]{:S(2)}, u32[]{:S(2)}) collective-permute-start(bf16[1040,128]{1,0:T(8,128)(2,1)S(1)} %collective-permute-done.30), channel_id=1, source_target_pairs={{0,4},{5,1},{4,8},{9,5},{8,12},{13,9},{12,14},{15,13},{14,10},{11,... | collective-permute-start | bytes 798728 | tf_op jit(solution)/shard_map/ppermute | solution.py:279
  84.1 6.4 %collective-permute-start.35 = (bf16[1040,128]{1,0:T(8,128)(2,1)S(1)}, bf16[1040,128]{1,0:T(8,128)(2,1)S(1)}, u32[]{:S(2)}, u32[]{:S(2)}) collective-permute-start(bf16[1040,128]{1,0:T(8,128)(2,1)S(1)} %collective-permute-done.31), channel_id=1, source_target_pairs={{0,4},{5,1},{4,8},{9,5},{8,12},{13,9},{12,14},{15,13},{14,10},{11,... | collective-permute-start | bytes 798728 | tf_op jit(solution)/shard_map/ppermute | solution.py:279
  85.6 2.9 %collective-permute-start.32 = (bf16[1040,128]{1,0:T(8,128)(2,1)S(1)}, bf16[1040,128]{1,0:T(8,128)(2,1)S(1)}, u32[]{:S(2)}, u32[]{:S(2)}) collective-permute-start(bf16[1040,128]{1,0:T(8,128)(2,1)S(1)} %collective-permute-done.31), channel_id=1, source_target_pairs={{0,1},{1,0},{2,3},{3,2},{4,5},{5,4},{6,7},{7,6},{8,9},{9,8},{10,11... | collective-permute-start | bytes 798728 | tf_op jit(solution)/shard_map/ppermute | solution.py:276
  86.9 6.4 %collective-permute-start.37 = (bf16[1040,128]{1,0:T(8,128)(2,1)S(1)}, bf16[1040,128]{1,0:T(8,128)(2,1)S(1)}, u32[]{:S(2)}, u32[]{:S(2)}) collective-permute-start(bf16[1040,128]{1,0:T(8,128)(2,1)S(1)} %collective-permute-done.33), channel_id=1, source_target_pairs={{0,4},{5,1},{4,8},{9,5},{8,12},{13,9},{12,14},{15,13},{14,10},{11,... | collective-permute-start | bytes 798728 | tf_op jit(solution)/shard_map/ppermute | solution.py:279
  88.4 6.4 %collective-permute-start.34 = (bf16[1040,128]{1,0:T(8,128)(2,1)S(1)}, bf16[1040,128]{1,0:T(8,128)(2,1)S(1)}, u32[]{:S(2)}, u32[]{:S(2)}) collective-permute-start(bf16[1040,128]{1,0:T(8,128)(2,1)S(1)} %collective-permute-done.33), channel_id=1, source_target_pairs={{0,1},{1,0},{2,3},{3,2},{4,5},{5,4},{6,7},{7,6},{8,9},{9,8},{10,11... | collective-permute-start | bytes 798728 | tf_op jit(solution)/shard_map/ppermute | solution.py:276
  90.5 7.0 %collective-permute-start.39 = (bf16[1040,128]{1,0:T(8,128)(2,1)S(1)}, bf16[1040,128]{1,0:T(8,128)(2,1)S(1)}, u32[]{:S(2)}, u32[]{:S(2)}) collective-permute-start(bf16[1040,128]{1,0:T(8,128)(2,1)S(1)} %collective-permute-done.35), channel_id=1, source_target_pairs={{0,4},{5,1},{4,8},{9,5},{8,12},{13,9},{12,14},{15,13},{14,10},{11,... | collective-permute-start | bytes 798728 | tf_op jit(solution)/shard_map/ppermute | solution.py:279
  92.0 4.2 %collective-permute-start.36 = (bf16[1040,128]{1,0:T(8,128)(2,1)S(1)}, bf16[1040,128]{1,0:T(8,128)(2,1)S(1)}, u32[]{:S(2)}, u32[]{:S(2)}) collective-permute-start(bf16[1040,128]{1,0:T(8,128)(2,1)S(1)} %collective-permute-done.35), channel_id=1, source_target_pairs={{0,1},{1,0},{2,3},{3,2},{4,5},{5,4},{6,7},{7,6},{8,9},{9,8},{10,11... | collective-permute-start | bytes 798728 | tf_op jit(solution)/shard_map/ppermute | solution.py:276
  93.3 6.4 %collective-permute-start.41 = (bf16[1040,128]{1,0:T(8,128)(2,1)S(1)}, bf16[1040,128]{1,0:T(8,128)(2,1)S(1)}, u32[]{:S(2)}, u32[]{:S(2)}) collective-permute-start(bf16[1040,128]{1,0:T(8,128)(2,1)S(1)} %collective-permute-done.37), channel_id=1, source_target_pairs={{0,4},{5,1},{4,8},{9,5},{8,12},{13,9},{12,14},{15,13},{14,10},{11,... | collective-permute-start | bytes 798728 | tf_op jit(solution)/shard_map/ppermute | solution.py:279
  94.8 5.0 %collective-permute-start.38 = (bf16[1040,128]{1,0:T(8,128)(2,1)S(1)}, bf16[1040,128]{1,0:T(8,128)(2,1)S(1)}, u32[]{:S(2)}, u32[]{:S(2)}) collective-permute-start(bf16[1040,128]{1,0:T(8,128)(2,1)S(1)} %collective-permute-done.37), channel_id=1, source_target_pairs={{0,1},{1,0},{2,3},{3,2},{4,5},{5,4},{6,7},{7,6},{8,9},{9,8},{10,11... | collective-permute-start | bytes 798728 | tf_op jit(solution)/shard_map/ppermute | solution.py:276
  97.5 6.5 %collective-permute-start.43 = (bf16[1040,128]{1,0:T(8,128)(2,1)S(1)}, bf16[1040,128]{1,0:T(8,128)(2,1)S(1)}, u32[]{:S(2)}, u32[]{:S(2)}) collective-permute-start(bf16[1040,128]{1,0:T(8,128)(2,1)S(1)} %collective-permute-done.39), channel_id=1, source_target_pairs={{0,4},{5,1},{4,8},{9,5},{8,12},{13,9},{12,14},{15,13},{14,10},{11,... | collective-permute-start | bytes 798728 | tf_op jit(solution)/shard_map/ppermute | solution.py:279
  99.2 2.6 %collective-permute-start.40 = (bf16[1040,128]{1,0:T(8,128)(2,1)S(1)}, bf16[1040,128]{1,0:T(8,128)(2,1)S(1)}, u32[]{:S(2)}, u32[]{:S(2)}) collective-permute-start(bf16[1040,128]{1,0:T(8,128)(2,1)S(1)} %collective-permute-done.39), channel_id=1, source_target_pairs={{0,1},{1,0},{2,3},{3,2},{4,5},{5,4},{6,7},{7,6},{8,9},{9,8},{10,11... | collective-permute-start | bytes 798728 | tf_op jit(solution)/shard_map/ppermute | solution.py:276
  99.8 4.2 %collective-permute-start.42 = (bf16[1040,128]{1,0:T(8,128)(2,1)S(1)}, bf16[1040,128]{1,0:T(8,128)(2,1)S(1)}, u32[]{:S(2)}, u32[]{:S(2)}) collective-permute-start(bf16[1040,128]{1,0:T(8,128)(2,1)S(1)} %collective-permute-done.41), channel_id=1, source_target_pairs={{0,1},{1,0},{2,3},{3,2},{4,5},{5,4},{6,7},{7,6},{8,9},{9,8},{10,11... | collective-permute-start | bytes 798728 | tf_op jit(solution)/shard_map/ppermute | solution.py:276
  104.0 1.6 %collective-permute-start.44 = (bf16[1040,128]{1,0:T(8,128)(2,1)S(1)}, bf16[1040,128]{1,0:T(8,128)(2,1)S(1)}, u32[]{:S(2)}, u32[]{:S(2)}) collective-permute-start(bf16[1040,128]{1,0:T(8,128)(2,1)S(1)} %collective-permute-done.43), channel_id=1, source_target_pairs={{0,1},{1,0},{2,3},{3,2},{4,5},{5,4},{6,7},{7,6},{8,9},{9,8},{10,11... | collective-permute-start | bytes 798728 | tf_op jit(solution)/shard_map/ppermute | solution.py:276
  111.9 3.6 %collective-permute-start.46 = (f32[8,128]{1,0:T(8,128)S(1)}, f32[8,128]{1,0:T(8,128)S(1)}, u32[]{:S(2)}, u32[]{:S(2)}) collective-permute-start(f32[8,128]{1,0:T(8,128)S(1)} %add.277), channel_id=1, source_target_pairs={{0,2},{1,3},{2,0},{3,1},{4,6},{5,7},{6,4},{7,5},{8,10},{9,11},{10,... | collective-permute-start | bytes 12296 | tf_op jit(solution)/shard_map/ppermute | solution.py:407
  115.5 3.9 %collective-permute-start.47 = (f32[8,128]{1,0:T(8,128)S(1)}, f32[8,128]{1,0:T(8,128)S(1)}, u32[]{:S(2)}, u32[]{:S(2)}) collective-permute-start(f32[8,128]{1,0:T(8,128)S(1)} %add.278), channel_id=1, source_target_pairs={{0,4},{1,5},{2,6},{3,7},{4,0},{5,1},{6,2},{7,3},{8,12},{9,13},{10,... | collective-permute-start | bytes 12296 | tf_op jit(solution)/shard_map/ppermute | solution.py:407
  119.5 4.5 %collective-permute-start.48 = (f32[8,128]{1,0:T(8,128)S(1)}, f32[8,128]{1,0:T(8,128)S(1)}, u32[]{:S(2)}, u32[]{:S(2)}) collective-permute-start(f32[8,128]{1,0:T(8,128)S(1)} %add.279), channel_id=1, source_target_pairs={{0,8},{1,9},{2,10},{3,11},{4,12},{5,13},{6,14},{7,15},{8,0},{9,1},... | collective-permute-start | bytes 12296 | tf_op jit(solution)/shard_map/ppermute | solution.py:407
  (6 other events, 26.3 us)

commit v4 on v3

--- a/solution.py
+++ b/solution.py
@@ -42,8 +42,8 @@
     piece_ref[rows:, :] = split_rows([lane_sums(wide * wide)])
 
 
-def prepare_kernel(sizes, phases, phase_ref, offset_ref, env_ref, *rest):
-    count_ref, list_ref, env_out, sems = rest
+def prepare_kernel(sizes, phases, phase_ref, offset_ref, place_ref, env_ref, *rest):
+    count_ref, list_ref, stat_ref, env_out, sems = rest
     tile_dev, shifts, group, tile_rows, total = sizes
     records = tile_dev * shifts
     step = env_ref.shape[0] // LOADS
@@ -67,7 +67,12 @@
             count_ref[p] = n + 1
         return carry
 
+    def one_place(d, carry):
+        stat_ref[d] = place_ref[d]
+        return carry
+
     lax.fori_loop(0, tile_dev, one_tile, 0)
+    lax.fori_loop(0, place_ref.shape[0], one_place, 0)
     for copy in copies:
         copy.wait()
 
@@ -344,23 +349,24 @@
     left_type = pltpu.VMEM((shifts * rows, (terms // shifts) * columns), bf16)
 
     def prepare(marker):
-        tied = lax.optimization_barrier((phase, offset, env_flat, marker))
-        counts, lists, env_near = pl.pallas_call(
+        tied = lax.optimization_barrier((phase, offset, stat_offset, env_flat, marker))
+        counts, lists, places, env_near = pl.pallas_call(
             functools.partial(prepare_kernel, sizes, phases),
             out_shape=(
-                jax.ShapeDtypeStruct((phases,), jnp.int32),
-                jax.ShapeDtypeStruct((3, phases * records), jnp.int32),
+                pltpu.SMEM((phases,), jnp.int32),
+                pltpu.SMEM((3, phases * records), jnp.int32),
+                pltpu.SMEM((peers,), jnp.int32),
                 pltpu.VMEM(env_flat.shape, bf16),
             ),
-            in_specs=[smem, smem, hbm],
-            out_specs=(smem, smem, vmem),
+            in_specs=[smem, smem, smem, hbm],
+            out_specs=(smem, smem, smem, vmem),
             scratch_shapes=[pltpu.SemaphoreType.DMA((LOADS,))],
             compiler_params=pltpu.CompilerParams(vmem_limit_bytes=40 * 2**20),
-        )(*tied[:3])
-        return env_near, right_flat, counts, lists
+        )(*tied[:4])
+        return env_near, right_flat, counts, lists, places
 
     def contract(phase, buffer, near, held):
-        env_near, right_near, counts, lists = near
+        env_near, right_near, counts, lists, places = near
         return pl.pallas_call(
             functools.partial(left_kernel, phase, 8 if phase == 0 else 10, sizes),
             out_shape=left_type,
@@ -372,10 +378,10 @@
         )(counts, lists, buffer, env_near, *held)
 
     def apply_operator(stage, buffers, near, held, prior, coefs):
-        image = jax.ShapeDtypeStruct((rows, columns), f32)
+        image = pltpu.VMEM((rows, columns), f32)
         small = jax.ShapeDtypeStruct((8, 128), f32)
         send = small if stage == 3 else jax.ShapeDtypeStruct((piece_rows, columns), bf16)
-        env_near, right_near, counts, lists = near
+        env_near, right_near, counts, lists, places = near
         operands = [right_near, wavefunction, *buffers, *prior, *coefs, held]
         return pl.pallas_call(
             functools.partial(apply_kernel, stage, sizes, slots),
@@ -387,7 +393,7 @@
             cost_estimate=pl.CostEstimate(
                 flops=4 * rows * terms * tile_rows * columns, bytes_accessed=2**24, transcendentals=0
             ),
-        )(stat_offset, *operands)
+        )(places, *operands)
 
     buffers, near, held = exchange(piece, contract, prepare, True)
     image_one, coefs_one, piece = apply_operator(1, buffers, near, held, [], [])

time: 125 us -> 118 us (0.944)
  Pallas kernels: 49 us -> 29 us
  starting transfers between devices: 33.6 us -> 43.9 us
  waiting for transfers between devices: 35.8 us -> 37.2 us
    pallas_call x24, Pallas kernels: 31.6 us -> 14.7 us  [contract(): pl.pallas_call(functools.partial(left_kernel, phase, 8 if phase == 0 else...]
    ppermute x21, starting transfers between devices: 25 us -> 36.6 us  [step_on(): return lax.ppermute(x, 'sector', onward)]
    pallas_call x3, Pallas kernels: 11.2 us -> 8.77 us  [apply_operator(): pl.pallas_call(functools.partial(apply_kernel, stage, sizes, slots), out_...]
    ppermute x24, waiting for transfers between devices: 2.73 us -> 4.86 us  [swap_cores(): return lax.ppermute(x, 'sector', sibling)]
    ppermute x24, starting transfers between devices: 2.73 us -> 0.84 us  [swap_cores(): return lax.ppermute(x, 'sector', sibling)]
    unnamed x34 -> x35, local copies, waits for them, and re-layouts: 2.01 us -> 3 us
  transfers between devices with their start and end apart: 49 -> 49, of which waited for: 22 -> 27; matrix products, arithmetic and copies ran while one was open for 3% -> 3% of each run, Pallas kernels for 28% -> 15%
where the time goes in v4:
time: 118 us; the launch traced here: 117 us
  starting transfers between devices  43.9 us (37%)
  waiting for transfers between devices  37.2 us (32%)
  Pallas kernels  29 us (25%)
  local copies, waits for them, and re-layouts  4.11 us (3%)
  other arithmetic  1.71 us (1%)
  between operations  1.38 us (1%)
    ppermute x21, starting transfers between devices, step_on(): return lax.ppermute(x, 'sector', onward)  36.6 us
    ppermute x21, waiting for transfers between devices, step_on(): return lax.ppermute(x, 'sector', onward)  26.1 us
    pallas_call x24, Pallas kernels, contract(): pl.pallas_call(functools.partial(left_kernel, phase, 8 if phase == 0 else...  14.7 us
    pallas_call x3, Pallas kernels, apply_operator(): pl.pallas_call(functools.partial(apply_kernel, stage, sizes, slots), out_...  8.77 us
    ppermute x4, starting transfers between devices, per_device(): stats = stats + lax.ppermute(stats, 'sector', pairs)  6.46 us
    ppermute x4, waiting for transfers between devices, per_device(): stats = stats + lax.ppermute(stats, 'sector', pairs)  6.25 us
    ppermute x24, waiting for transfers between devices, swap_cores(): return lax.ppermute(x, 'sector', sibling)  4.86 us
    pallas_call x1, Pallas kernels, prepare(): pl.pallas_call(functools.partial(prepare_kernel, sizes, phases), out_shap...  4.65 us
  transfers between devices with their start and end apart: 49, of which 27 were waited for; matrix products, arithmetic and copies ran while one was open for 3% of the time, Pallas kernels for 15%

profile of v4, /device:TPU:0, one launch (start us, length us, event | category | flops | bytes accessed | tf_op | source)
XLA Modules:
  0.0 117.3 jit_solution(6517851423250024502)
XLA Ops:
  4.3 2.7 %collective-permute-start.1 = (bf16[1040,128]{1,0:T(8,128)(2,1)S(1)}, bf16[1040,128]{1,0:T(8,128)(2,1)S(1)}, u32[]{:S(2)}, u32[]{:S(2)}) collective-permute-start(bf16[1040,128]{1,0:T(8,128)(2,1)S(1)} %shard_map.77), channel_id=1, source_target_pairs={{0,4},{5,1},{4,8},{9,5},{8,12},{13,9},{12,14},{15,13},{14,10},{11,... | collective-permute-start | bytes 798728 | tf_op jit(solution)/shard_map/ppermute | solution.py:284
  6.9 1.6 %collective-permute-start.3 = (bf16[1040,128]{1,0:T(8,128)(2,1)S(1)}, bf16[1040,128]{1,0:T(8,128)(2,1)S(1)}, u32[]{:S(2)}, u32[]{:S(2)}) collective-permute-start(bf16[1040,128]{1,0:T(8,128)(2,1)S(1)} %collective-permute-done), channel_id=1, source_target_pairs={{0,4},{5,1},{4,8},{9,5},{8,12},{13,9},{12,14},{15,13},{14,10},{11,... | collective-permute-start | bytes 798728 | tf_op jit(solution)/shard_map/ppermute | solution.py:284
  8.5 4.7 %shard_map.78 = (s32[8]{0:T(128)S(4)}, s32[3,640]{1,0:T(4,128)S(4)}, s32[16]{0:T(128)S(4)}, bf16[40960,128]{1,0:T(8,128)(2,1)S(1)}) custom-call(s32[80]{0:T(128)S(1)} %get-tuple-element.32.phase_ref, s32[80]{0:T(128)S(1)} %get-tuple-element.33.offset_ref, s32[16]{0:T(128)S(1)} %broadcast_multiply_fusion.place_ref, bf16[40960,128]{1,0:T(8,128)(2,1)} %bitcast.5), custom_call_target="tpu_custom_call" | custom-call | tf_op jit(solution)/shard_map/pallas_call | solution.py:353
  13.3 1.6 %collective-permute-start.5 = (bf16[1040,128]{1,0:T(8,128)(2,1)S(1)}, bf16[1040,128]{1,0:T(8,128)(2,1)S(1)}, u32[]{:S(2)}, u32[]{:S(2)}) collective-permute-start(bf16[1040,128]{1,0:T(8,128)(2,1)S(1)} %collective-permute-done.1), channel_id=1, source_target_pairs={{0,4},{5,1},{4,8},{9,5},{8,12},{13,9},{12,14},{15,13},{14,10},{11,... | collective-permute-start | bytes 798728 | tf_op jit(solution)/shard_map/ppermute | solution.py:284
  14.9 1.5 %collective-permute-start.7 = (bf16[1040,128]{1,0:T(8,128)(2,1)S(1)}, bf16[1040,128]{1,0:T(8,128)(2,1)S(1)}, u32[]{:S(2)}, u32[]{:S(2)}) collective-permute-start(bf16[1040,128]{1,0:T(8,128)(2,1)S(1)} %collective-permute-done.3), channel_id=1, source_target_pairs={{0,4},{5,1},{4,8},{9,5},{8,12},{13,9},{12,14},{15,13},{14,10},{11,... | collective-permute-start | bytes 798728 | tf_op jit(solution)/shard_map/ppermute | solution.py:284
  16.4 3.3 %collective-permute-done.5 = bf16[1040,128]{1,0:T(8,128)(2,1)S(1)} collective-permute-done((bf16[1040,128]{1,0:T(8,128)(2,1)S(1)}, bf16[1040,128]{1,0:T(8,128)(2,1)S(1)}, u32[]{:S(2)}, u32[]{:S(2)}) %collective-permute-start.5) | collective-permute-done | bytes 266272 | tf_op jit(solution)/shard_map/ppermute | solution.py:284
  19.7 1.6 %collective-permute-start.9 = (bf16[1040,128]{1,0:T(8,128)(2,1)S(1)}, bf16[1040,128]{1,0:T(8,128)(2,1)S(1)}, u32[]{:S(2)}, u32[]{:S(2)}) collective-permute-start(bf16[1040,128]{1,0:T(8,128)(2,1)S(1)} %collective-permute-done.5), channel_id=1, source_target_pairs={{0,4},{5,1},{4,8},{9,5},{8,12},{13,9},{12,14},{15,13},{14,10},{11,... | collective-permute-start | bytes 798728 | tf_op jit(solution)/shard_map/ppermute | solution.py:284
  23.0 1.5 %collective-permute-start.11 = (bf16[1040,128]{1,0:T(8,128)(2,1)S(1)}, bf16[1040,128]{1,0:T(8,128)(2,1)S(1)}, u32[]{:S(2)}, u32[]{:S(2)}) collective-permute-start(bf16[1040,128]{1,0:T(8,128)(2,1)S(1)} %collective-permute-done.7), channel_id=1, source_target_pairs={{0,4},{5,1},{4,8},{9,5},{8,12},{13,9},{12,14},{15,13},{14,10},{11,... | collective-permute-start | bytes 798728 | tf_op jit(solution)/shard_map/ppermute | solution.py:284
  24.6 1.2 %shard_map.81.rest_0_ = bf16[10240,512]{1,0:T(8,128)(2,1)S(1)} custom-call(s32[8]{0:T(128)S(4)} %get-tuple-element.38.count_ref, s32[3,640]{1,0:T(4,128)S(4)} %get-tuple-element.39.list_ref, bf16[2080,128]{1,0:T(8,128)(2,1)S(1)} %constant_dynamic-update-slice_fusion.buf_ref.rest_0_, ...), custom_call_target="tpu_custom_call", output_to_operand_aliasing={{}: (4, {})} | custom-call | flops 1073741824 | bytes 1048576 | tf_op jit(solution)/shard_map/pallas_call | solution.py:370
  26.1 1.6 %collective-permute-start.13 = (bf16[1040,128]{1,0:T(8,128)(2,1)S(1)}, bf16[1040,128]{1,0:T(8,128)(2,1)S(1)}, u32[]{:S(2)}, u32[]{:S(2)}) collective-permute-start(bf16[1040,128]{1,0:T(8,128)(2,1)S(1)} %collective-permute-done.9), channel_id=1, source_target_pairs={{0,4},{5,1},{4,8},{9,5},{8,12},{13,9},{12,14},{15,13},{14,10},{11,... | collective-permute-start | bytes 798728 | tf_op jit(solution)/shard_map/ppermute | solution.py:284
  27.7 1.8 %collective-permute-done.11 = bf16[1040,128]{1,0:T(8,128)(2,1)S(1)} collective-permute-done((bf16[1040,128]{1,0:T(8,128)(2,1)S(1)}, bf16[1040,128]{1,0:T(8,128)(2,1)S(1)}, u32[]{:S(2)}, u32[]{:S(2)}) %collective-permute-start.11) | collective-permute-done | bytes 266272 | tf_op jit(solution)/shard_map/ppermute | solution.py:284
  30.2 2.3 %collective-permute-done.13 = bf16[1040,128]{1,0:T(8,128)(2,1)S(1)} collective-permute-done((bf16[1040,128]{1,0:T(8,128)(2,1)S(1)}, bf16[1040,128]{1,0:T(8,128)(2,1)S(1)}, u32[]{:S(2)}, u32[]{:S(2)}) %collective-permute-start.13) | collective-permute-done | bytes 266272 | tf_op jit(solution)/shard_map/ppermute | solution.py:284
  35.5 2.9 %shard_map.87 = (f32[1024,128]{1,0:T(8,128)S(1)}, f32[8,128]{1,0:T(8,128)S(1)}, bf16[1040,128]{1,0:T(8,128)(2,1)S(1)}) custom-call(s32[16]{0:T(128)S(4)} %get-tuple-element.36.stat_ref, bf16[5120,128]{1,0:T(8,128)(2,1)S(1)} %bitcast.2, bf16[1024,128]{1,0:T(8,128)(2,1)S(1)} %copy-done.4, ...), custom_call_target="tpu_custom_call" | custom-call | flops 2684354560 | bytes 16777216 | tf_op jit(solution)/shard_map/pallas_call | solution.py:386
  38.6 1.4 %collective-permute-done.15 = bf16[1040,128]{1,0:T(8,128)(2,1)S(1)} collective-permute-done((bf16[1040,128]{1,0:T(8,128)(2,1)S(1)}, bf16[1040,128]{1,0:T(8,128)(2,1)S(1)}, u32[]{:S(2)}, u32[]{:S(2)}) %collective-permute-start.15) | collective-permute-done | bytes 266272 | tf_op jit(solution)/shard_map/ppermute | solution.py:281
  40.0 1.6 %collective-permute-start.16 = (bf16[1040,128]{1,0:T(8,128)(2,1)S(1)}, bf16[1040,128]{1,0:T(8,128)(2,1)S(1)}, u32[]{:S(2)}, u32[]{:S(2)}) collective-permute-start(bf16[1040,128]{1,0:T(8,128)(2,1)S(1)} %get-tuple-element.44), channel_id=1, source_target_pairs={{0,4},{5,1},{4,8},{9,5},{8,12},{13,9},{12,14},{15,13},{14,10},{11,... | collective-permute-start | bytes 798728 | tf_op jit(solution)/shard_map/ppermute | solution.py:284
  41.6 1.5 %collective-permute-start.18 = (bf16[1040,128]{1,0:T(8,128)(2,1)S(1)}, bf16[1040,128]{1,0:T(8,128)(2,1)S(1)}, u32[]{:S(2)}, u32[]{:S(2)}) collective-permute-start(bf16[1040,128]{1,0:T(8,128)(2,1)S(1)} %collective-permute-done.15), channel_id=1, source_target_pairs={{0,4},{5,1},{4,8},{9,5},{8,12},{13,9},{12,14},{15,13},{14,10},{11,... | collective-permute-start | bytes 798728 | tf_op jit(solution)/shard_map/ppermute | solution.py:284
  43.2 1.2 %shard_map.88.rest_0_ = bf16[10240,512]{1,0:T(8,128)(2,1)S(1)} custom-call(s32[8]{0:T(128)S(4)} %get-tuple-element.38.count_ref, s32[3,640]{1,0:T(4,128)S(4)} %get-tuple-element.39.list_ref, bf16[2080,128]{1,0:T(8,128)(2,1)S(1)} %constant_dynamic-update-slice_fusion.16.buf_ref.rest_0_, bf16[40960,128]{1,0:T(8,128)(2,1)S(1)} %get-tuple-element.40.env_ref), custom_call_target="tpu_custom_call" | custom-call | flops 1073741824 | bytes 1048576 | tf_op jit(solution)/shard_map/pallas_call | solution.py:370
  44.4 2.0 %collective-permute-done.16 = bf16[1040,128]{1,0:T(8,128)(2,1)S(1)} collective-permute-done((bf16[1040,128]{1,0:T(8,128)(2,1)S(1)}, bf16[1040,128]{1,0:T(8,128)(2,1)S(1)}, u32[]{:S(2)}, u32[]{:S(2)}) %collective-permute-start.16) | collective-permute-done | bytes 266272 | tf_op jit(solution)/shard_map/ppermute | solution.py:284
  46.4 1.6 %collective-permute-start.20 = (bf16[1040,128]{1,0:T(8,128)(2,1)S(1)}, bf16[1040,128]{1,0:T(8,128)(2,1)S(1)}, u32[]{:S(2)}, u32[]{:S(2)}) collective-permute-start(bf16[1040,128]{1,0:T(8,128)(2,1)S(1)} %collective-permute-done.16), channel_id=1, source_target_pairs={{0,4},{5,1},{4,8},{9,5},{8,12},{13,9},{12,14},{15,13},{14,10},{11,... | collective-permute-start | bytes 798728 | tf_op jit(solution)/shard_map/ppermute | solution.py:284
  48.0 1.3 %collective-permute-done.18 = bf16[1040,128]{1,0:T(8,128)(2,1)S(1)} collective-permute-done((bf16[1040,128]{1,0:T(8,128)(2,1)S(1)}, bf16[1040,128]{1,0:T(8,128)(2,1)S(1)}, u32[]{:S(2)}, u32[]{:S(2)}) %collective-permute-start.18) | collective-permute-done | bytes 266272 | tf_op jit(solution)/shard_map/ppermute | solution.py:284
  49.3 1.6 %collective-permute-start.22 = (bf16[1040,128]{1,0:T(8,128)(2,1)S(1)}, bf16[1040,128]{1,0:T(8,128)(2,1)S(1)}, u32[]{:S(2)}, u32[]{:S(2)}) collective-permute-start(bf16[1040,128]{1,0:T(8,128)(2,1)S(1)} %collective-permute-done.18), channel_id=1, source_target_pairs={{0,4},{5,1},{4,8},{9,5},{8,12},{13,9},{12,14},{15,13},{14,10},{11,... | collective-permute-start | bytes 798728 | tf_op jit(solution)/shard_map/ppermute | solution.py:284
  50.9 1.2 %shard_map.89.rest_0_ = bf16[10240,512]{1,0:T(8,128)(2,1)S(1)} custom-call(s32[8]{0:T(128)S(4)} %get-tuple-element.38.count_ref, s32[3,640]{1,0:T(4,128)S(4)} %get-tuple-element.39.list_ref, bf16[2080,128]{1,0:T(8,128)(2,1)S(1)} %constant_dynamic-update-slice_fusion.18.buf_ref.rest_1_, ...), custom_call_target="tpu_custom_call", output_to_operand_aliasing={{}: (4, {})} | custom-call | flops 1073741824 | bytes 1048576 | tf_op jit(solution)/shard_map/pallas_call | solution.py:370
  52.8 1.6 %collective-permute-start.24 = (bf16[1040,128]{1,0:T(8,128)(2,1)S(1)}, bf16[1040,128]{1,0:T(8,128)(2,1)S(1)}, u32[]{:S(2)}, u32[]{:S(2)}) collective-permute-start(bf16[1040,128]{1,0:T(8,128)(2,1)S(1)} %collective-permute-done.20), channel_id=1, source_target_pairs={{0,4},{5,1},{4,8},{9,5},{8,12},{13,9},{12,14},{15,13},{14,10},{11,... | collective-permute-start | bytes 798728 | tf_op jit(solution)/shard_map/ppermute | solution.py:284
  54.4 1.3 %collective-permute-done.22 = bf16[1040,128]{1,0:T(8,128)(2,1)S(1)} collective-permute-done((bf16[1040,128]{1,0:T(8,128)(2,1)S(1)}, bf16[1040,128]{1,0:T(8,128)(2,1)S(1)}, u32[]{:S(2)}, u32[]{:S(2)}) %collective-permute-start.22) | collective-permute-done | bytes 266272 | tf_op jit(solution)/shard_map/ppermute | solution.py:284
  55.7 1.6 %collective-permute-start.26 = (bf16[1040,128]{1,0:T(8,128)(2,1)S(1)}, bf16[1040,128]{1,0:T(8,128)(2,1)S(1)}, u32[]{:S(2)}, u32[]{:S(2)}) collective-permute-start(bf16[1040,128]{1,0:T(8,128)(2,1)S(1)} %collective-permute-done.22), channel_id=1, source_target_pairs={{0,4},{5,1},{4,8},{9,5},{8,12},{13,9},{12,14},{15,13},{14,10},{11,... | collective-permute-start | bytes 798728 | tf_op jit(solution)/shard_map/ppermute | solution.py:284
  58.0 1.2 %collective-permute-done.24 = bf16[1040,128]{1,0:T(8,128)(2,1)S(1)} collective-permute-done((bf16[1040,128]{1,0:T(8,128)(2,1)S(1)}, bf16[1040,128]{1,0:T(8,128)(2,1)S(1)}, u32[]{:S(2)}, u32[]{:S(2)}) %collective-permute-start.24) | collective-permute-done | bytes 266272 | tf_op jit(solution)/shard_map/ppermute | solution.py:284
  59.2 1.6 %collective-permute-start.28 = (bf16[1040,128]{1,0:T(8,128)(2,1)S(1)}, bf16[1040,128]{1,0:T(8,128)(2,1)S(1)}, u32[]{:S(2)}, u32[]{:S(2)}) collective-permute-start(bf16[1040,128]{1,0:T(8,128)(2,1)S(1)} %collective-permute-done.24), channel_id=1, source_target_pairs={{0,4},{5,1},{4,8},{9,5},{8,12},{13,9},{12,14},{15,13},{14,10},{11,... | collective-permute-start | bytes 798728 | tf_op jit(solution)/shard_map/ppermute | solution.py:284
  60.8 1.3 %collective-permute-done.26 = bf16[1040,128]{1,0:T(8,128)(2,1)S(1)} collective-permute-done((bf16[1040,128]{1,0:T(8,128)(2,1)S(1)}, bf16[1040,128]{1,0:T(8,128)(2,1)S(1)}, u32[]{:S(2)}, u32[]{:S(2)}) %collective-permute-start.26) | collective-permute-done | bytes 266272 | tf_op jit(solution)/shard_map/ppermute | solution.py:284
  62.8 2.8 %collective-permute-done.28 = bf16[1040,128]{1,0:T(8,128)(2,1)S(1)} collective-permute-done((bf16[1040,128]{1,0:T(8,128)(2,1)S(1)}, bf16[1040,128]{1,0:T(8,128)(2,1)S(1)}, u32[]{:S(2)}, u32[]{:S(2)}) %collective-permute-start.28) | collective-permute-done | bytes 266272 | tf_op jit(solution)/shard_map/ppermute | solution.py:284
  67.8 2.9 %shard_map.96 = (f32[1024,128]{1,0:T(8,128)S(1)}, f32[8,128]{1,0:T(8,128)S(1)}, bf16[1040,128]{1,0:T(8,128)(2,1)S(1)}) custom-call(s32[16]{0:T(128)S(4)} %get-tuple-element.36.stat_ref, bf16[5120,128]{1,0:T(8,128)(2,1)S(1)} %bitcast.3, bf16[1024,128]{1,0:T(8,128)(2,1)S(1)} %copy-done.4, ...), custom_call_target="tpu_custom_call" | custom-call | flops 2684354560 | bytes 16777216 | tf_op jit(solution)/shard_map/pallas_call | solution.py:386
  70.8 1.5 %collective-permute-done.30 = bf16[1040,128]{1,0:T(8,128)(2,1)S(1)} collective-permute-done((bf16[1040,128]{1,0:T(8,128)(2,1)S(1)}, bf16[1040,128]{1,0:T(8,128)(2,1)S(1)}, u32[]{:S(2)}, u32[]{:S(2)}) %collective-permute-start.30) | collective-permute-done | bytes 266272 | tf_op jit(solution)/shard_map/ppermute | solution.py:281
  72.3 2.1 %collective-permute-start.31 = (bf16[1040,128]{1,0:T(8,128)(2,1)S(1)}, bf16[1040,128]{1,0:T(8,128)(2,1)S(1)}, u32[]{:S(2)}, u32[]{:S(2)}) collective-permute-start(bf16[1040,128]{1,0:T(8,128)(2,1)S(1)} %get-tuple-element.51), channel_id=1, source_target_pairs={{0,4},{5,1},{4,8},{9,5},{8,12},{13,9},{12,14},{15,13},{14,10},{11,... | collective-permute-start | bytes 798728 | tf_op jit(solution)/shard_map/ppermute | solution.py:284
  75.5 1.2 %shard_map.97.rest_0_ = bf16[10240,512]{1,0:T(8,128)(2,1)S(1)} custom-call(s32[8]{0:T(128)S(4)} %get-tuple-element.38.count_ref, s32[3,640]{1,0:T(4,128)S(4)} %get-tuple-element.39.list_ref, bf16[2080,128]{1,0:T(8,128)(2,1)S(1)} %constant_dynamic-update-slice_fusion.32.buf_ref.rest_0_, bf16[40960,128]{1,0:T(8,128)(2,1)S(1)} %get-tuple-element.40.env_ref), custom_call_target="tpu_custom_call" | custom-call | flops 1073741824 | bytes 1048576 | tf_op jit(solution)/shard_map/pallas_call | solution.py:370
  76.7 2.0 %collective-permute-done.31 = bf16[1040,128]{1,0:T(8,128)(2,1)S(1)} collective-permute-done((bf16[1040,128]{1,0:T(8,128)(2,1)S(1)}, bf16[1040,128]{1,0:T(8,128)(2,1)S(1)}, u32[]{:S(2)}, u32[]{:S(2)}) %collective-permute-start.31) | collective-permute-done | bytes 266272 | tf_op jit(solution)/shard_map/ppermute | solution.py:284
  78.7 2.1 %collective-permute-start.35 = (bf16[1040,128]{1,0:T(8,128)(2,1)S(1)}, bf16[1040,128]{1,0:T(8,128)(2,1)S(1)}, u32[]{:S(2)}, u32[]{:S(2)}) collective-permute-start(bf16[1040,128]{1,0:T(8,128)(2,1)S(1)} %collective-permute-done.31), channel_id=1, source_target_pairs={{0,4},{5,1},{4,8},{9,5},{8,12},{13,9},{12,14},{15,13},{14,10},{11,... | collective-permute-start | bytes 798728 | tf_op jit(solution)/shard_map/ppermute | solution.py:284
  81.6 2.1 %collective-permute-start.37 = (bf16[1040,128]{1,0:T(8,128)(2,1)S(1)}, bf16[1040,128]{1,0:T(8,128)(2,1)S(1)}, u32[]{:S(2)}, u32[]{:S(2)}) collective-permute-start(bf16[1040,128]{1,0:T(8,128)(2,1)S(1)} %collective-permute-done.33), channel_id=1, source_target_pairs={{0,4},{5,1},{4,8},{9,5},{8,12},{13,9},{12,14},{15,13},{14,10},{11,... | collective-permute-start | bytes 798728 | tf_op jit(solution)/shard_map/ppermute | solution.py:284
  85.1 2.1 %collective-permute-start.39 = (bf16[1040,128]{1,0:T(8,128)(2,1)S(1)}, bf16[1040,128]{1,0:T(8,128)(2,1)S(1)}, u32[]{:S(2)}, u32[]{:S(2)}) collective-permute-start(bf16[1040,128]{1,0:T(8,128)(2,1)S(1)} %collective-permute-done.35), channel_id=1, source_target_pairs={{0,4},{5,1},{4,8},{9,5},{8,12},{13,9},{12,14},{15,13},{14,10},{11,... | collective-permute-start | bytes 798728 | tf_op jit(solution)/shard_map/ppermute | solution.py:284
  88.0 2.1 %collective-permute-start.41 = (bf16[1040,128]{1,0:T(8,128)(2,1)S(1)}, bf16[1040,128]{1,0:T(8,128)(2,1)S(1)}, u32[]{:S(2)}, u32[]{:S(2)}) collective-permute-start(bf16[1040,128]{1,0:T(8,128)(2,1)S(1)} %collective-permute-done.37), channel_id=1, source_target_pairs={{0,4},{5,1},{4,8},{9,5},{8,12},{13,9},{12,14},{15,13},{14,10},{11,... | collective-permute-start | bytes 798728 | tf_op jit(solution)/shard_map/ppermute | solution.py:284
  91.5 2.1 %collective-permute-start.43 = (bf16[1040,128]{1,0:T(8,128)(2,1)S(1)}, bf16[1040,128]{1,0:T(8,128)(2,1)S(1)}, u32[]{:S(2)}, u32[]{:S(2)}) collective-permute-start(bf16[1040,128]{1,0:T(8,128)(2,1)S(1)} %collective-permute-done.39), channel_id=1, source_target_pairs={{0,4},{5,1},{4,8},{9,5},{8,12},{13,9},{12,14},{15,13},{14,10},{11,... | collective-permute-start | bytes 798728 | tf_op jit(solution)/shard_map/ppermute | solution.py:284
  95.4 2.6 %collective-permute-done.43 = bf16[1040,128]{1,0:T(8,128)(2,1)S(1)} collective-permute-done((bf16[1040,128]{1,0:T(8,128)(2,1)S(1)}, bf16[1040,128]{1,0:T(8,128)(2,1)S(1)}, u32[]{:S(2)}, u32[]{:S(2)}) %collective-permute-start.43) | collective-permute-done | bytes 266272 | tf_op jit(solution)/shard_map/ppermute | solution.py:284
  100.1 3.0 %shard_map.105 = (f32[1024,128]{1,0:T(8,128)S(1)}, f32[8,128]{1,0:T(8,128)S(1)}, f32[8,128]{1,0:T(8,128)S(1)}) custom-call(s32[16]{0:T(128)S(4)} %get-tuple-element.36.stat_ref, bf16[5120,128]{1,0:T(8,128)(2,1)S(1)} %bitcast.4, bf16[1024,128]{1,0:T(8,128)(2,1)S(1)} %copy-done.4, bf16[2080,128]{1,0:T(8,128)(2,1)S(1)} %constant_dynamic-update-slice_fusion.32.buf_ref.rest_0_, ...), custom_call_target="tpu_custom_call" | custom-call | flops 2684354560 | bytes 16777216 | tf_op jit(solution)/shard_map/pallas_call | solution.py:386
  103.2 1.2 collective-permute-done.45
  104.3 1.9 %collective-permute-start.46 = (f32[8,128]{1,0:T(8,128)S(1)}, f32[8,128]{1,0:T(8,128)S(1)}, u32[]{:S(2)}, u32[]{:S(2)}) collective-permute-start(f32[8,128]{1,0:T(8,128)S(1)} %add.277), channel_id=1, source_target_pairs={{0,2},{1,3},{2,0},{3,1},{4,6},{5,7},{6,4},{7,5},{8,10},{9,11},{10,... | collective-permute-start | bytes 12296 | tf_op jit(solution)/shard_map/ppermute | solution.py:413
  106.2 1.7 %collective-permute-done.46 = f32[8,128]{1,0:T(8,128)S(1)} collective-permute-done((f32[8,128]{1,0:T(8,128)S(1)}, f32[8,128]{1,0:T(8,128)S(1)}, u32[]{:S(2)}, u32[]{:S(2)}) %collective-permute-start.46) | collective-permute-done | bytes 4128 | tf_op jit(solution)/shard_map/ppermute | solution.py:413
  107.9 2.6 %collective-permute-start.47 = (f32[8,128]{1,0:T(8,128)S(1)}, f32[8,128]{1,0:T(8,128)S(1)}, u32[]{:S(2)}, u32[]{:S(2)}) collective-permute-start(f32[8,128]{1,0:T(8,128)S(1)} %add.278), channel_id=1, source_target_pairs={{0,4},{1,5},{2,6},{3,7},{4,0},{5,1},{6,2},{7,3},{8,12},{9,13},{10,... | collective-permute-start | bytes 12296 | tf_op jit(solution)/shard_map/ppermute | solution.py:413
  110.5 1.6 %collective-permute-done.47 = f32[8,128]{1,0:T(8,128)S(1)} collective-permute-done((f32[8,128]{1,0:T(8,128)S(1)}, f32[8,128]{1,0:T(8,128)S(1)}, u32[]{:S(2)}, u32[]{:S(2)}) %collective-permute-start.47) | collective-permute-done | bytes 4128 | tf_op jit(solution)/shard_map/ppermute | solution.py:413
  112.1 1.9 %collective-permute-start.48 = (f32[8,128]{1,0:T(8,128)S(1)}, f32[8,128]{1,0:T(8,128)S(1)}, u32[]{:S(2)}, u32[]{:S(2)}) collective-permute-start(f32[8,128]{1,0:T(8,128)S(1)} %add.279), channel_id=1, source_target_pairs={{0,8},{1,9},{2,10},{3,11},{4,12},{5,13},{6,14},{7,15},{8,0},{9,1},... | collective-permute-start | bytes 12296 | tf_op jit(solution)/shard_map/ppermute | solution.py:413
  114.8 1.8 %collective-permute-done.48 = f32[8,128]{1,0:T(8,128)S(1)} collective-permute-done((f32[8,128]{1,0:T(8,128)S(1)}, f32[8,128]{1,0:T(8,128)S(1)}, u32[]{:S(2)}, u32[]{:S(2)}) %collective-permute-start.48) | collective-permute-done | bytes 4128 | tf_op jit(solution)/shard_map/ppermute | solution.py:413
  (152 shorter events, 24.6 us)
Async XLA Ops:
  1.8 2.5 %collective-permute-start = (bf16[1040,128]{1,0:T(8,128)(2,1)S(1)}, bf16[1040,128]{1,0:T(8,128)(2,1)S(1)}, u32[]{:S(2)}, u32[]{:S(2)}) collective-permute-start(bf16[1040,128]{1,0:T(8,128)(2,1)S(1)} %shard_map.77), channel_id=1, source_target_pairs={{0,1},{1,0},{2,3},{3,2},{4,5},{5,4},{6,7},{7,6},{8,9},{9,8},{10,11... | collective-permute-start | bytes 798728 | tf_op jit(solution)/shard_map/ppermute | solution.py:281
  4.3 9.0 %collective-permute-start.1 = (bf16[1040,128]{1,0:T(8,128)(2,1)S(1)}, bf16[1040,128]{1,0:T(8,128)(2,1)S(1)}, u32[]{:S(2)}, u32[]{:S(2)}) collective-permute-start(bf16[1040,128]{1,0:T(8,128)(2,1)S(1)} %shard_map.77), channel_id=1, source_target_pairs={{0,4},{5,1},{4,8},{9,5},{8,12},{13,9},{12,14},{15,13},{14,10},{11,... | collective-permute-start | bytes 798728 | tf_op jit(solution)/shard_map/ppermute | solution.py:284
  6.9 7.9 %collective-permute-start.3 = (bf16[1040,128]{1,0:T(8,128)(2,1)S(1)}, bf16[1040,128]{1,0:T(8,128)(2,1)S(1)}, u32[]{:S(2)}, u32[]{:S(2)}) collective-permute-start(bf16[1040,128]{1,0:T(8,128)(2,1)S(1)} %collective-permute-done), channel_id=1, source_target_pairs={{0,4},{5,1},{4,8},{9,5},{8,12},{13,9},{12,14},{15,13},{14,10},{11,... | collective-permute-start | bytes 798728 | tf_op jit(solution)/shard_map/ppermute | solution.py:284
  13.3 6.5 %collective-permute-start.5 = (bf16[1040,128]{1,0:T(8,128)(2,1)S(1)}, bf16[1040,128]{1,0:T(8,128)(2,1)S(1)}, u32[]{:S(2)}, u32[]{:S(2)}) collective-permute-start(bf16[1040,128]{1,0:T(8,128)(2,1)S(1)} %collective-permute-done.1), channel_id=1, source_target_pairs={{0,4},{5,1},{4,8},{9,5},{8,12},{13,9},{12,14},{15,13},{14,10},{11,... | collective-permute-start | bytes 798728 | tf_op jit(solution)/shard_map/ppermute | solution.py:284
  14.9 6.5 %collective-permute-start.2 = (bf16[1040,128]{1,0:T(8,128)(2,1)S(1)}, bf16[1040,128]{1,0:T(8,128)(2,1)S(1)}, u32[]{:S(2)}, u32[]{:S(2)}) collective-permute-start(bf16[1040,128]{1,0:T(8,128)(2,1)S(1)} %collective-permute-done.1), channel_id=1, source_target_pairs={{0,1},{1,0},{2,3},{3,2},{4,5},{5,4},{6,7},{7,6},{8,9},{9,8},{10,11... | collective-permute-start | bytes 798728 | tf_op jit(solution)/shard_map/ppermute | solution.py:281
  14.9 8.1 %collective-permute-start.7 = (bf16[1040,128]{1,0:T(8,128)(2,1)S(1)}, bf16[1040,128]{1,0:T(8,128)(2,1)S(1)}, u32[]{:S(2)}, u32[]{:S(2)}) collective-permute-start(bf16[1040,128]{1,0:T(8,128)(2,1)S(1)} %collective-permute-done.3), channel_id=1, source_target_pairs={{0,4},{5,1},{4,8},{9,5},{8,12},{13,9},{12,14},{15,13},{14,10},{11,... | collective-permute-start | bytes 798728 | tf_op jit(solution)/shard_map/ppermute | solution.py:284
  16.4 4.9 %collective-permute-start.4 = (bf16[1040,128]{1,0:T(8,128)(2,1)S(1)}, bf16[1040,128]{1,0:T(8,128)(2,1)S(1)}, u32[]{:S(2)}, u32[]{:S(2)}) collective-permute-start(bf16[1040,128]{1,0:T(8,128)(2,1)S(1)} %collective-permute-done.3), channel_id=1, source_target_pairs={{0,1},{1,0},{2,3},{3,2},{4,5},{5,4},{6,7},{7,6},{8,9},{9,8},{10,11... | collective-permute-start | bytes 798728 | tf_op jit(solution)/shard_map/ppermute | solution.py:281
  19.7 6.4 %collective-permute-start.9 = (bf16[1040,128]{1,0:T(8,128)(2,1)S(1)}, bf16[1040,128]{1,0:T(8,128)(2,1)S(1)}, u32[]{:S(2)}, u32[]{:S(2)}) collective-permute-start(bf16[1040,128]{1,0:T(8,128)(2,1)S(1)} %collective-permute-done.5), channel_id=1, source_target_pairs={{0,4},{5,1},{4,8},{9,5},{8,12},{13,9},{12,14},{15,13},{14,10},{11,... | collective-permute-start | bytes 798728 | tf_op jit(solution)/shard_map/ppermute | solution.py:284
  21.3 4.5 %collective-permute-start.6 = (bf16[1040,128]{1,0:T(8,128)(2,1)S(1)}, bf16[1040,128]{1,0:T(8,128)(2,1)S(1)}, u32[]{:S(2)}, u32[]{:S(2)}) collective-permute-start(bf16[1040,128]{1,0:T(8,128)(2,1)S(1)} %collective-permute-done.5), channel_id=1, source_target_pairs={{0,1},{1,0},{2,3},{3,2},{4,5},{5,4},{6,7},{7,6},{8,9},{9,8},{10,11... | collective-permute-start | bytes 798728 | tf_op jit(solution)/shard_map/ppermute | solution.py:281
  23.0 6.5 %collective-permute-start.11 = (bf16[1040,128]{1,0:T(8,128)(2,1)S(1)}, bf16[1040,128]{1,0:T(8,128)(2,1)S(1)}, u32[]{:S(2)}, u32[]{:S(2)}) collective-permute-start(bf16[1040,128]{1,0:T(8,128)(2,1)S(1)} %collective-permute-done.7), channel_id=1, source_target_pairs={{0,4},{5,1},{4,8},{9,5},{8,12},{13,9},{12,14},{15,13},{14,10},{11,... | collective-permute-start | bytes 798728 | tf_op jit(solution)/shard_map/ppermute | solution.py:284
  24.6 5.0 %collective-permute-start.8 = (bf16[1040,128]{1,0:T(8,128)(2,1)S(1)}, bf16[1040,128]{1,0:T(8,128)(2,1)S(1)}, u32[]{:S(2)}, u32[]{:S(2)}) collective-permute-start(bf16[1040,128]{1,0:T(8,128)(2,1)S(1)} %collective-permute-done.7), channel_id=1, source_target_pairs={{0,1},{1,0},{2,3},{3,2},{4,5},{5,4},{6,7},{7,6},{8,9},{9,8},{10,11... | collective-permute-start | bytes 798728 | tf_op jit(solution)/shard_map/ppermute | solution.py:281
  26.1 6.4 %collective-permute-start.13 = (bf16[1040,128]{1,0:T(8,128)(2,1)S(1)}, bf16[1040,128]{1,0:T(8,128)(2,1)S(1)}, u32[]{:S(2)}, u32[]{:S(2)}) collective-permute-start(bf16[1040,128]{1,0:T(8,128)(2,1)S(1)} %collective-permute-done.9), channel_id=1, source_target_pairs={{0,4},{5,1},{4,8},{9,5},{8,12},{13,9},{12,14},{15,13},{14,10},{11,... | collective-permute-start | bytes 798728 | tf_op jit(solution)/shard_map/ppermute | solution.py:284
  27.7 2.4 %collective-permute-start.10 = (bf16[1040,128]{1,0:T(8,128)(2,1)S(1)}, bf16[1040,128]{1,0:T(8,128)(2,1)S(1)}, u32[]{:S(2)}, u32[]{:S(2)}) collective-permute-start(bf16[1040,128]{1,0:T(8,128)(2,1)S(1)} %collective-permute-done.9), channel_id=1, source_target_pairs={{0,1},{1,0},{2,3},{3,2},{4,5},{5,4},{6,7},{7,6},{8,9},{9,8},{10,11... | collective-permute-start | bytes 798728 | tf_op jit(solution)/shard_map/ppermute | solution.py:281
  29.5 3.1 %collective-permute-start.12 = (bf16[1040,128]{1,0:T(8,128)(2,1)S(1)}, bf16[1040,128]{1,0:T(8,128)(2,1)S(1)}, u32[]{:S(2)}, u32[]{:S(2)}) collective-permute-start(bf16[1040,128]{1,0:T(8,128)(2,1)S(1)} %collective-permute-done.11), channel_id=1, source_target_pairs={{0,1},{1,0},{2,3},{3,2},{4,5},{5,4},{6,7},{7,6},{8,9},{9,8},{10,11... | collective-permute-start | bytes 798728 | tf_op jit(solution)/shard_map/ppermute | solution.py:281
  32.6 1.5 %collective-permute-start.14 = (bf16[1040,128]{1,0:T(8,128)(2,1)S(1)}, bf16[1040,128]{1,0:T(8,128)(2,1)S(1)}, u32[]{:S(2)}, u32[]{:S(2)}) collective-permute-start(bf16[1040,128]{1,0:T(8,128)(2,1)S(1)} %collective-permute-done.13), channel_id=1, source_target_pairs={{0,1},{1,0},{2,3},{3,2},{4,5},{5,4},{6,7},{7,6},{8,9},{9,8},{10,11... | collective-permute-start | bytes 798728 | tf_op jit(solution)/shard_map/ppermute | solution.py:281
  38.4 1.6 %collective-permute-start.15 = (bf16[1040,128]{1,0:T(8,128)(2,1)S(1)}, bf16[1040,128]{1,0:T(8,128)(2,1)S(1)}, u32[]{:S(2)}, u32[]{:S(2)}) collective-permute-start(bf16[1040,128]{1,0:T(8,128)(2,1)S(1)} %get-tuple-element.44), channel_id=1, source_target_pairs={{0,1},{1,0},{2,3},{3,2},{4,5},{5,4},{6,7},{7,6},{8,9},{9,8},{10,11... | collective-permute-start | bytes 798728 | tf_op jit(solution)/shard_map/ppermute | solution.py:281
  40.0 6.4 %collective-permute-start.16 = (bf16[1040,128]{1,0:T(8,128)(2,1)S(1)}, bf16[1040,128]{1,0:T(8,128)(2,1)S(1)}, u32[]{:S(2)}, u32[]{:S(2)}) collective-permute-start(bf16[1040,128]{1,0:T(8,128)(2,1)S(1)} %get-tuple-element.44), channel_id=1, source_target_pairs={{0,4},{5,1},{4,8},{9,5},{8,12},{13,9},{12,14},{15,13},{14,10},{11,... | collective-permute-start | bytes 798728 | tf_op jit(solution)/shard_map/ppermute | solution.py:284
  41.6 7.7 %collective-permute-start.18 = (bf16[1040,128]{1,0:T(8,128)(2,1)S(1)}, bf16[1040,128]{1,0:T(8,128)(2,1)S(1)}, u32[]{:S(2)}, u32[]{:S(2)}) collective-permute-start(bf16[1040,128]{1,0:T(8,128)(2,1)S(1)} %collective-permute-done.15), channel_id=1, source_target_pairs={{0,4},{5,1},{4,8},{9,5},{8,12},{13,9},{12,14},{15,13},{14,10},{11,... | collective-permute-start | bytes 798728 | tf_op jit(solution)/shard_map/ppermute | solution.py:284
  46.4 6.4 %collective-permute-start.20 = (bf16[1040,128]{1,0:T(8,128)(2,1)S(1)}, bf16[1040,128]{1,0:T(8,128)(2,1)S(1)}, u32[]{:S(2)}, u32[]{:S(2)}) collective-permute-start(bf16[1040,128]{1,0:T(8,128)(2,1)S(1)} %collective-permute-done.16), channel_id=1, source_target_pairs={{0,4},{5,1},{4,8},{9,5},{8,12},{13,9},{12,14},{15,13},{14,10},{11,... | collective-permute-start | bytes 798728 | tf_op jit(solution)/shard_map/ppermute | solution.py:284
  48.0 2.9 %collective-permute-start.17 = (bf16[1040,128]{1,0:T(8,128)(2,1)S(1)}, bf16[1040,128]{1,0:T(8,128)(2,1)S(1)}, u32[]{:S(2)}, u32[]{:S(2)}) collective-permute-start(bf16[1040,128]{1,0:T(8,128)(2,1)S(1)} %collective-permute-done.16), channel_id=1, source_target_pairs={{0,1},{1,0},{2,3},{3,2},{4,5},{5,4},{6,7},{7,6},{8,9},{9,8},{10,11... | collective-permute-start | bytes 798728 | tf_op jit(solution)/shard_map/ppermute | solution.py:281
  49.3 6.4 %collective-permute-start.22 = (bf16[1040,128]{1,0:T(8,128)(2,1)S(1)}, bf16[1040,128]{1,0:T(8,128)(2,1)S(1)}, u32[]{:S(2)}, u32[]{:S(2)}) collective-permute-start(bf16[1040,128]{1,0:T(8,128)(2,1)S(1)} %collective-permute-done.18), channel_id=1, source_target_pairs={{0,4},{5,1},{4,8},{9,5},{8,12},{13,9},{12,14},{15,13},{14,10},{11,... | collective-permute-start | bytes 798728 | tf_op jit(solution)/shard_map/ppermute | solution.py:284
  50.8 6.4 %collective-permute-start.19 = (bf16[1040,128]{1,0:T(8,128)(2,1)S(1)}, bf16[1040,128]{1,0:T(8,128)(2,1)S(1)}, u32[]{:S(2)}, u32[]{:S(2)}) collective-permute-start(bf16[1040,128]{1,0:T(8,128)(2,1)S(1)} %collective-permute-done.18), channel_id=1, source_target_pairs={{0,1},{1,0},{2,3},{3,2},{4,5},{5,4},{6,7},{7,6},{8,9},{9,8},{10,11... | collective-permute-start | bytes 798728 | tf_op jit(solution)/shard_map/ppermute | solution.py:281
  52.8 6.4 %collective-permute-start.24 = (bf16[1040,128]{1,0:T(8,128)(2,1)S(1)}, bf16[1040,128]{1,0:T(8,128)(2,1)S(1)}, u32[]{:S(2)}, u32[]{:S(2)}) collective-permute-start(bf16[1040,128]{1,0:T(8,128)(2,1)S(1)} %collective-permute-done.20), channel_id=1, source_target_pairs={{0,4},{5,1},{4,8},{9,5},{8,12},{13,9},{12,14},{15,13},{14,10},{11,... | collective-permute-start | bytes 798728 | tf_op jit(solution)/shard_map/ppermute | solution.py:284
  54.4 3.5 %collective-permute-start.21 = (bf16[1040,128]{1,0:T(8,128)(2,1)S(1)}, bf16[1040,128]{1,0:T(8,128)(2,1)S(1)}, u32[]{:S(2)}, u32[]{:S(2)}) collective-permute-start(bf16[1040,128]{1,0:T(8,128)(2,1)S(1)} %collective-permute-done.20), channel_id=1, source_target_pairs={{0,1},{1,0},{2,3},{3,2},{4,5},{5,4},{6,7},{7,6},{8,9},{9,8},{10,11... | collective-permute-start | bytes 798728 | tf_op jit(solution)/shard_map/ppermute | solution.py:281
  55.7 6.4 %collective-permute-start.26 = (bf16[1040,128]{1,0:T(8,128)(2,1)S(1)}, bf16[1040,128]{1,0:T(8,128)(2,1)S(1)}, u32[]{:S(2)}, u32[]{:S(2)}) collective-permute-start(bf16[1040,128]{1,0:T(8,128)(2,1)S(1)} %collective-permute-done.22), channel_id=1, source_target_pairs={{0,4},{5,1},{4,8},{9,5},{8,12},{13,9},{12,14},{15,13},{14,10},{11,... | collective-permute-start | bytes 798728 | tf_op jit(solution)/shard_map/ppermute | solution.py:284
  57.3 4.9 %collective-permute-start.23 = (bf16[1040,128]{1,0:T(8,128)(2,1)S(1)}, bf16[1040,128]{1,0:T(8,128)(2,1)S(1)}, u32[]{:S(2)}, u32[]{:S(2)}) collective-permute-start(bf16[1040,128]{1,0:T(8,128)(2,1)S(1)} %collective-permute-done.22), channel_id=1, source_target_pairs={{0,1},{1,0},{2,3},{3,2},{4,5},{5,4},{6,7},{7,6},{8,9},{9,8},{10,11... | collective-permute-start | bytes 798728 | tf_op jit(solution)/shard_map/ppermute | solution.py:281
  59.2 6.4 %collective-permute-start.28 = (bf16[1040,128]{1,0:T(8,128)(2,1)S(1)}, bf16[1040,128]{1,0:T(8,128)(2,1)S(1)}, u32[]{:S(2)}, u32[]{:S(2)}) collective-permute-start(bf16[1040,128]{1,0:T(8,128)(2,1)S(1)} %collective-permute-done.24), channel_id=1, source_target_pairs={{0,4},{5,1},{4,8},{9,5},{8,12},{13,9},{12,14},{15,13},{14,10},{11,... | collective-permute-start | bytes 798728 | tf_op jit(solution)/shard_map/ppermute | solution.py:284
  60.8 1.9 %collective-permute-start.25 = (bf16[1040,128]{1,0:T(8,128)(2,1)S(1)}, bf16[1040,128]{1,0:T(8,128)(2,1)S(1)}, u32[]{:S(2)}, u32[]{:S(2)}) collective-permute-start(bf16[1040,128]{1,0:T(8,128)(2,1)S(1)} %collective-permute-done.24), channel_id=1, source_target_pairs={{0,1},{1,0},{2,3},{3,2},{4,5},{5,4},{6,7},{7,6},{8,9},{9,8},{10,11... | collective-permute-start | bytes 798728 | tf_op jit(solution)/shard_map/ppermute | solution.py:281
  62.1 3.6 %collective-permute-start.27 = (bf16[1040,128]{1,0:T(8,128)(2,1)S(1)}, bf16[1040,128]{1,0:T(8,128)(2,1)S(1)}, u32[]{:S(2)}, u32[]{:S(2)}) collective-permute-start(bf16[1040,128]{1,0:T(8,128)(2,1)S(1)} %collective-permute-done.26), channel_id=1, source_target_pairs={{0,1},{1,0},{2,3},{3,2},{4,5},{5,4},{6,7},{7,6},{8,9},{9,8},{10,11... | collective-permute-start | bytes 798728 | tf_op jit(solution)/shard_map/ppermute | solution.py:281
  65.7 1.5 %collective-permute-start.29 = (bf16[1040,128]{1,0:T(8,128)(2,1)S(1)}, bf16[1040,128]{1,0:T(8,128)(2,1)S(1)}, u32[]{:S(2)}, u32[]{:S(2)}) collective-permute-start(bf16[1040,128]{1,0:T(8,128)(2,1)S(1)} %collective-permute-done.28), channel_id=1, source_target_pairs={{0,1},{1,0},{2,3},{3,2},{4,5},{5,4},{6,7},{7,6},{8,9},{9,8},{10,11... | collective-permute-start | bytes 798728 | tf_op jit(solution)/shard_map/ppermute | solution.py:281
  70.7 1.6 %collective-permute-start.30 = (bf16[1040,128]{1,0:T(8,128)(2,1)S(1)}, bf16[1040,128]{1,0:T(8,128)(2,1)S(1)}, u32[]{:S(2)}, u32[]{:S(2)}) collective-permute-start(bf16[1040,128]{1,0:T(8,128)(2,1)S(1)} %get-tuple-element.51), channel_id=1, source_target_pairs={{0,1},{1,0},{2,3},{3,2},{4,5},{5,4},{6,7},{7,6},{8,9},{9,8},{10,11... | collective-permute-start | bytes 798728 | tf_op jit(solution)/shard_map/ppermute | solution.py:281
  72.3 6.4 %collective-permute-start.31 = (bf16[1040,128]{1,0:T(8,128)(2,1)S(1)}, bf16[1040,128]{1,0:T(8,128)(2,1)S(1)}, u32[]{:S(2)}, u32[]{:S(2)}) collective-permute-start(bf16[1040,128]{1,0:T(8,128)(2,1)S(1)} %get-tuple-element.51), channel_id=1, source_target_pairs={{0,4},{5,1},{4,8},{9,5},{8,12},{13,9},{12,14},{15,13},{14,10},{11,... | collective-permute-start | bytes 798728 | tf_op jit(solution)/shard_map/ppermute | solution.py:284
  74.4 7.2 %collective-permute-start.33 = (bf16[1040,128]{1,0:T(8,128)(2,1)S(1)}, bf16[1040,128]{1,0:T(8,128)(2,1)S(1)}, u32[]{:S(2)}, u32[]{:S(2)}) collective-permute-start(bf16[1040,128]{1,0:T(8,128)(2,1)S(1)} %collective-permute-done.30), channel_id=1, source_target_pairs={{0,4},{5,1},{4,8},{9,5},{8,12},{13,9},{12,14},{15,13},{14,10},{11,... | collective-permute-start | bytes 798728 | tf_op jit(solution)/shard_map/ppermute | solution.py:284
  78.7 6.4 %collective-permute-start.35 = (bf16[1040,128]{1,0:T(8,128)(2,1)S(1)}, bf16[1040,128]{1,0:T(8,128)(2,1)S(1)}, u32[]{:S(2)}, u32[]{:S(2)}) collective-permute-start(bf16[1040,128]{1,0:T(8,128)(2,1)S(1)} %collective-permute-done.31), channel_id=1, source_target_pairs={{0,4},{5,1},{4,8},{9,5},{8,12},{13,9},{12,14},{15,13},{14,10},{11,... | collective-permute-start | bytes 798728 | tf_op jit(solution)/shard_map/ppermute | solution.py:284
  80.8 2.9 %collective-permute-start.32 = (bf16[1040,128]{1,0:T(8,128)(2,1)S(1)}, bf16[1040,128]{1,0:T(8,128)(2,1)S(1)}, u32[]{:S(2)}, u32[]{:S(2)}) collective-permute-start(bf16[1040,128]{1,0:T(8,128)(2,1)S(1)} %collective-permute-done.31), channel_id=1, source_target_pairs={{0,1},{1,0},{2,3},{3,2},{4,5},{5,4},{6,7},{7,6},{8,9},{9,8},{10,11... | collective-permute-start | bytes 798728 | tf_op jit(solution)/shard_map/ppermute | solution.py:281
  81.6 6.4 %collective-permute-start.37 = (bf16[1040,128]{1,0:T(8,128)(2,1)S(1)}, bf16[1040,128]{1,0:T(8,128)(2,1)S(1)}, u32[]{:S(2)}, u32[]{:S(2)}) collective-permute-start(bf16[1040,128]{1,0:T(8,128)(2,1)S(1)} %collective-permute-done.33), channel_id=1, source_target_pairs={{0,4},{5,1},{4,8},{9,5},{8,12},{13,9},{12,14},{15,13},{14,10},{11,... | collective-permute-start | bytes 798728 | tf_op jit(solution)/shard_map/ppermute | solution.py:284
  83.6 6.4 %collective-permute-start.34 = (bf16[1040,128]{1,0:T(8,128)(2,1)S(1)}, bf16[1040,128]{1,0:T(8,128)(2,1)S(1)}, u32[]{:S(2)}, u32[]{:S(2)}) collective-permute-start(bf16[1040,128]{1,0:T(8,128)(2,1)S(1)} %collective-permute-done.33), channel_id=1, source_target_pairs={{0,1},{1,0},{2,3},{3,2},{4,5},{5,4},{6,7},{7,6},{8,9},{9,8},{10,11... | collective-permute-start | bytes 798728 | tf_op jit(solution)/shard_map/ppermute | solution.py:281
  85.1 6.4 %collective-permute-start.39 = (bf16[1040,128]{1,0:T(8,128)(2,1)S(1)}, bf16[1040,128]{1,0:T(8,128)(2,1)S(1)}, u32[]{:S(2)}, u32[]{:S(2)}) collective-permute-start(bf16[1040,128]{1,0:T(8,128)(2,1)S(1)} %collective-permute-done.35), channel_id=1, source_target_pairs={{0,4},{5,1},{4,8},{9,5},{8,12},{13,9},{12,14},{15,13},{14,10},{11,... | collective-permute-start | bytes 798728 | tf_op jit(solution)/shard_map/ppermute | solution.py:284
  87.2 3.5 %collective-permute-start.36 = (bf16[1040,128]{1,0:T(8,128)(2,1)S(1)}, bf16[1040,128]{1,0:T(8,128)(2,1)S(1)}, u32[]{:S(2)}, u32[]{:S(2)}) collective-permute-start(bf16[1040,128]{1,0:T(8,128)(2,1)S(1)} %collective-permute-done.35), channel_id=1, source_target_pairs={{0,1},{1,0},{2,3},{3,2},{4,5},{5,4},{6,7},{7,6},{8,9},{9,8},{10,11... | collective-permute-start | bytes 798728 | tf_op jit(solution)/shard_map/ppermute | solution.py:281
  88.0 6.4 %collective-permute-start.41 = (bf16[1040,128]{1,0:T(8,128)(2,1)S(1)}, bf16[1040,128]{1,0:T(8,128)(2,1)S(1)}, u32[]{:S(2)}, u32[]{:S(2)}) collective-permute-start(bf16[1040,128]{1,0:T(8,128)(2,1)S(1)} %collective-permute-done.37), channel_id=1, source_target_pairs={{0,4},{5,1},{4,8},{9,5},{8,12},{13,9},{12,14},{15,13},{14,10},{11,... | collective-permute-start | bytes 798728 | tf_op jit(solution)/shard_map/ppermute | solution.py:284
  90.1 4.4 %collective-permute-start.38 = (bf16[1040,128]{1,0:T(8,128)(2,1)S(1)}, bf16[1040,128]{1,0:T(8,128)(2,1)S(1)}, u32[]{:S(2)}, u32[]{:S(2)}) collective-permute-start(bf16[1040,128]{1,0:T(8,128)(2,1)S(1)} %collective-permute-done.37), channel_id=1, source_target_pairs={{0,1},{1,0},{2,3},{3,2},{4,5},{5,4},{6,7},{7,6},{8,9},{9,8},{10,11... | collective-permute-start | bytes 798728 | tf_op jit(solution)/shard_map/ppermute | solution.py:281
  91.5 6.4 %collective-permute-start.43 = (bf16[1040,128]{1,0:T(8,128)(2,1)S(1)}, bf16[1040,128]{1,0:T(8,128)(2,1)S(1)}, u32[]{:S(2)}, u32[]{:S(2)}) collective-permute-start(bf16[1040,128]{1,0:T(8,128)(2,1)S(1)} %collective-permute-done.39), channel_id=1, source_target_pairs={{0,4},{5,1},{4,8},{9,5},{8,12},{13,9},{12,14},{15,13},{14,10},{11,... | collective-permute-start | bytes 798728 | tf_op jit(solution)/shard_map/ppermute | solution.py:284
  93.6 1.6 %collective-permute-start.40 = (bf16[1040,128]{1,0:T(8,128)(2,1)S(1)}, bf16[1040,128]{1,0:T(8,128)(2,1)S(1)}, u32[]{:S(2)}, u32[]{:S(2)}) collective-permute-start(bf16[1040,128]{1,0:T(8,128)(2,1)S(1)} %collective-permute-done.39), channel_id=1, source_target_pairs={{0,1},{1,0},{2,3},{3,2},{4,5},{5,4},{6,7},{7,6},{8,9},{9,8},{10,11... | collective-permute-start | bytes 798728 | tf_op jit(solution)/shard_map/ppermute | solution.py:281
  94.4 3.6 %collective-permute-start.42 = (bf16[1040,128]{1,0:T(8,128)(2,1)S(1)}, bf16[1040,128]{1,0:T(8,128)(2,1)S(1)}, u32[]{:S(2)}, u32[]{:S(2)}) collective-permute-start(bf16[1040,128]{1,0:T(8,128)(2,1)S(1)} %collective-permute-done.41), channel_id=1, source_target_pairs={{0,1},{1,0},{2,3},{3,2},{4,5},{5,4},{6,7},{7,6},{8,9},{9,8},{10,11... | collective-permute-start | bytes 798728 | tf_op jit(solution)/shard_map/ppermute | solution.py:281
  98.0 1.5 %collective-permute-start.44 = (bf16[1040,128]{1,0:T(8,128)(2,1)S(1)}, bf16[1040,128]{1,0:T(8,128)(2,1)S(1)}, u32[]{:S(2)}, u32[]{:S(2)}) collective-permute-start(bf16[1040,128]{1,0:T(8,128)(2,1)S(1)} %collective-permute-done.43), channel_id=1, source_target_pairs={{0,1},{1,0},{2,3},{3,2},{4,5},{5,4},{6,7},{7,6},{8,9},{9,8},{10,11... | collective-permute-start | bytes 798728 | tf_op jit(solution)/shard_map/ppermute | solution.py:281
  104.3 3.6 %collective-permute-start.46 = (f32[8,128]{1,0:T(8,128)S(1)}, f32[8,128]{1,0:T(8,128)S(1)}, u32[]{:S(2)}, u32[]{:S(2)}) collective-permute-start(f32[8,128]{1,0:T(8,128)S(1)} %add.277), channel_id=1, source_target_pairs={{0,2},{1,3},{2,0},{3,1},{4,6},{5,7},{6,4},{7,5},{8,10},{9,11},{10,... | collective-permute-start | bytes 12296 | tf_op jit(solution)/shard_map/ppermute | solution.py:413
  107.9 4.2 %collective-permute-start.47 = (f32[8,128]{1,0:T(8,128)S(1)}, f32[8,128]{1,0:T(8,128)S(1)}, u32[]{:S(2)}, u32[]{:S(2)}) collective-permute-start(f32[8,128]{1,0:T(8,128)S(1)} %add.278), channel_id=1, source_target_pairs={{0,4},{1,5},{2,6},{3,7},{4,0},{5,1},{6,2},{7,3},{8,12},{9,13},{10,... | collective-permute-start | bytes 12296 | tf_op jit(solution)/shard_map/ppermute | solution.py:413
  112.1 4.5 %collective-permute-start.48 = (f32[8,128]{1,0:T(8,128)S(1)}, f32[8,128]{1,0:T(8,128)S(1)}, u32[]{:S(2)}, u32[]{:S(2)}) collective-permute-start(f32[8,128]{1,0:T(8,128)S(1)} %add.279), channel_id=1, source_target_pairs={{0,8},{1,9},{2,10},{3,11},{4,12},{5,13},{6,14},{7,15},{8,0},{9,1},... | collective-permute-start | bytes 12296 | tf_op jit(solution)/shard_map/ppermute | solution.py:413
  (6 other events, 25.1 us)
